TPU v7x, 32 devices: a whole 2x2x4 slice. The times are simulated.
32 devices in a mesh: side: 2 (over y), grp: 4 (over z), cuts: 4 (over x, core).
Axes of the slice: x: 2, y: 2, z: 4, core: 2. Of those that a mesh axis runs over, the one named last changes fastest.
Arguments:
- query: bfloat16 [128, 6144], P(('side', 'grp', 'cuts')), may hold values from -21 to 21, as said below
- k_cache: bfloat16 [128, 256, 1024], P(('side', 'grp', 'cuts')), may hold values from -5 to 5
- v_cache: bfloat16 [128, 256, 1024], P(('side', 'grp', 'cuts')), may hold values from -6 to 6
- new_key: bfloat16 [128, 1024], P(('side', 'grp', 'cuts')), may hold values from -6 to 6
- new_value: bfloat16 [128, 1024], P(('side', 'grp', 'cuts')), may hold values from -6 to 6
- lengths: int32 [128], P(('side', 'grp', 'cuts')), may hold values from 2 to 256, as said below
- residual: bfloat16 [128, 6144], P(('side', 'grp', 'cuts')), may hold values from -6 to 6
- norm_gain: bfloat16 [6144], replicated, may hold values from 0.099609375 to 1.8984375
- router: bfloat16 [6144, 4], replicated, may hold values from -0.078125 to 0.078125
- routes: int32 [128, 2], P(('side', 'grp', 'cuts')), may hold values from 0 to 3, all different within a row; in each aligned block of 4 rows (0 to 3, 4 to 7, ...) at most 2 rows name the same one
- w_gate: bfloat16 [4, 6144, 8192], P('grp', None, ('side', 'cuts')), may hold values from -0.078125 to 0.078125
- w_up: bfloat16 [4, 6144, 8192], P('grp', None, ('side', 'cuts')), may hold values from -0.078125 to 0.078125
- w_down: bfloat16 [4, 8192, 6144], P('grp', ('side', 'cuts')), may hold values from -0.0625 to 0.0625
Outputs:
- layer_out: bfloat16 [128, 6144], P(('side', 'grp', 'cuts'))
Inputs may be any that keep to these rules, and one draw needn't show every extreme that they name: `query`: queries are the new token's queries; in some draws a few rows have queries aligned with some cached keys. `lengths`: some row in every draw has all 256 positions live. `routes`: the two experts of a row differ. Within the rows of one device (aligned blocks of 4 rows) no expert is named more than 2 times, a bound that some block of every draw reaches.
All inputs are finite; a program needn't handle non-finite values.
Results may differ from a plain program's by a relative error of at most 0.0095.
Values may be sent and summed in bfloat16 or wider, within the bound.
No kernel may reach another device: no remote copies, remote signals or barrier semaphores. Data moves between devices by JAX's collectives and lax.ppermute only.
A program may use at most 128 MiB of HBM per device.

v0:
```python
import math

import jax
import jax.numpy as jnp
from jax import lax
from jax.sharding import PartitionSpec as P

Q_HEADS = 48
KV_HEADS = 8
HEAD_DIM = 128


def attend(query, k_cache, v_cache, new_key, new_value, lengths):
    rows, span, _ = k_cache.shape
    group = Q_HEADS // KV_HEADS
    scale = 1.0 / math.sqrt(HEAD_DIM)
    queries = query.reshape(rows, KV_HEADS, group, HEAD_DIM)
    keys = k_cache.reshape(rows, span, KV_HEADS, HEAD_DIM)
    values = v_cache.reshape(rows, span, KV_HEADS, HEAD_DIM)
    fresh_key = new_key.reshape(rows, KV_HEADS, HEAD_DIM)
    fresh_value = new_value.astype(jnp.float32).reshape(rows, KV_HEADS, 1, HEAD_DIM)
    old = jnp.einsum("rkgd,rskd->rkgs", queries, keys, preferred_element_type=jnp.float32) * scale
    own = (
        jnp.einsum("rkgd,rkd->rkg", queries, fresh_key, preferred_element_type=jnp.float32) * scale
    )
    live = jnp.arange(span)[None, :] < lengths[:, None]
    old = jnp.where(live[:, None, None, :], old, -jnp.inf)
    top = jnp.maximum(jnp.max(old, axis=-1), own)
    e_old = jnp.exp(old - top[..., None])
    e_own = jnp.exp(own - top)
    total = jnp.sum(e_old, axis=-1) + e_own
    p_old = (e_old / total[..., None]).astype(jnp.bfloat16)
    p_own = (e_own / total).astype(jnp.bfloat16).astype(jnp.float32)
    out = jnp.einsum("rkgs,rskd->rkgd", p_old, values, preferred_element_type=jnp.float32)
    out = out + p_own[..., None] * fresh_value
    return out.reshape(rows, Q_HEADS * HEAD_DIM)


def slot_ranks(block):
    flat = block.reshape(-1)
    order = jnp.arange(flat.shape[0])
    same = (flat[:, None] == flat[None, :]) & (order[None, :] < order[:, None])
    return jnp.sum(same.astype(jnp.int32), axis=1).reshape(block.shape)


def activate(rows_in, gate_w, up_w):
    gate = jnp.dot(rows_in, gate_w, preferred_element_type=jnp.float32)
    upper = jnp.dot(rows_in, up_w, preferred_element_type=jnp.float32)
    return (jax.nn.silu(gate) * upper).astype(jnp.bfloat16)


def local(
    query,
    k_cache,
    v_cache,
    new_key,
    new_value,
    lengths,
    residual,
    norm_gain,
    router,
    routes,
    w_gate,
    w_up,
    w_down,
):
    rows = query.shape[0]
    width = query.shape[1]
    experts = lax.axis_size("grp")
    n_side = lax.axis_size("side")
    n_cuts = lax.axis_size("cuts")
    most = max(2, 2 * rows // experts)
    gate_w = w_gate[0]
    up_w = w_up[0]
    down_w = w_down[0]
    attended = attend(query, k_cache, v_cache, new_key, new_value, lengths)
    mixed = residual.astype(jnp.float32) + attended
    power = jnp.mean(mixed * mixed, axis=1, keepdims=True)
    normed = (mixed * lax.rsqrt(power + 1e-05) * norm_gain.astype(jnp.float32)).astype(jnp.bfloat16)
    logits = jnp.dot(normed, router, preferred_element_type=jnp.float32)
    chosen = routes[:, :, None] == jnp.arange(experts)[None, None, :]
    picked = jnp.sum(jnp.where(chosen, logits[:, None, :], 0.0), axis=-1)
    first = jax.nn.sigmoid(picked[:, 0] - picked[:, 1])
    second = jax.nn.sigmoid(picked[:, 1] - picked[:, 0])
    weights = jnp.stack([first, second], axis=1)
    ranks = slot_ranks(routes)
    slot_of = routes * most + ranks
    slot_range = jnp.arange(experts * most)
    placing = slot_of[:, :, None] == slot_range[None, None, :]
    one_hot = jnp.sum(placing.astype(jnp.float32), axis=1).astype(jnp.bfloat16)
    outgoing = jnp.einsum("rj,rx->jx", one_hot, normed, preferred_element_type=jnp.float32).astype(
        jnp.bfloat16
    )
    copies = jnp.broadcast_to(
        outgoing.reshape(1, experts, 1, most, width), (n_side, experts, n_cuts, most, width)
    )
    arrived = lax.all_to_all(
        copies.reshape(-1, width), ("side", "grp", "cuts"), split_axis=0, concat_axis=0, tiled=True
    )
    hidden = activate(arrived, gate_w, up_w)
    ff_dev = hidden.shape[1]
    hidden = (
        hidden.reshape(n_side, experts, n_cuts, most, ff_dev)
        .transpose(0, 2, 1, 3, 4)
        .reshape(-1, ff_dev)
    )
    mine = lax.psum_scatter(
        jnp.dot(hidden, down_w, preferred_element_type=jnp.float32).astype(jnp.bfloat16),
        ("side", "cuts"),
        scatter_dimension=0,
        tiled=True,
    ).astype(jnp.float32)
    returned = lax.all_to_all(
        mine.astype(jnp.bfloat16), "grp", split_axis=0, concat_axis=0, tiled=True
    ).astype(mine.dtype)
    mixing = jnp.sum(jnp.where(placing, weights[:, :, None], 0.0), axis=1)
    combined = jnp.dot(
        mixing, returned, precision=lax.Precision.HIGHEST, preferred_element_type=jnp.float32
    )
    return (mixed + combined).astype(jnp.bfloat16)


def solution(mesh):
    placed = (
        P(("side", "grp", "cuts"), None),
        P(("side", "grp", "cuts"), None, None),
        P(("side", "grp", "cuts"), None, None),
        P(("side", "grp", "cuts"), None),
        P(("side", "grp", "cuts"), None),
        P(("side", "grp", "cuts")),
        P(("side", "grp", "cuts"), None),
        P(),
        P(),
        P(("side", "grp", "cuts"), None),
        P("grp", None, ("side", "cuts")),
        P("grp", None, ("side", "cuts")),
        P("grp", ("side", "cuts"), None),
    )
    return jax.shard_map(
        local,
        mesh=mesh,
        in_specs=placed,
        out_specs=P(("side", "grp", "cuts"), None),
        check_vma=False,
    )
```

profile of v0, /device:TPU:0, one launch (start us, length us, event | category | flops | bytes accessed | tf_op | source)
XLA Modules:
  0.0 119.6 jit_solution(17428758680372141868)
XLA Ops:
  6.5 0.0 copy-start
  6.5 0.0 reduce-scatter.2.cloned.1.call-start
  6.5 0.9 iota_compare_fusion.3
  7.4 0.8 copy.27
  8.2 0.1 eq.20
  8.3 0.2 convert_reduce_fusion.1
  8.5 0.1 reshape.74
  8.5 0.1 copy.29
  8.6 0.7 reshape.81
  9.4 0.7 convert_bitcast_fusion
  10.1 0.7 convert_element_type.48
  10.8 0.9 reshape.69
  11.6 0.0 copy-start.3
  11.7 0.1 fusion.39
  11.8 0.0 copy-done
  11.8 0.7 fusion.38
  12.5 0.0 copy-start.1
  12.5 0.0 copy-start.4
  12.6 0.2 fusion.31
  12.8 0.0 copy-start.2
  12.8 0.4 copy-done.3
  13.2 0.4 fusion.28
  13.7 0.1 reshape.73
  13.7 0.0 copy-done.1
  13.8 0.2 multiply_reduce_fusion
  13.9 0.1 multiply_convert_fusion
  14.0 0.0 copy-done.4
  14.0 0.2 fusion.40
  14.2 0.0 copy-done.2
  14.2 0.2 select_reduce_fusion.1
  14.4 0.1 convert_reduce_fusion
  14.5 0.2 convolution_convert_fusion
  14.7 0.1 broadcast_in_dim.65
  14.8 0.4 broadcast_in_dim.66
  15.3 28.7 %all_to_all.24 = bf16[32,2,6144]{2,1,0:T(2,128)(2,1)} all-to-all(bf16[32,2,6144]{2,1,0:T(2,128)(2,1)S(1)} %bitcast.60), channel_id=1, replica_groups=mesh['side'=2,'grp'=4,'cuts'=4] {'side','grp','cuts'}, dimensions={0} | all-to-all | bytes 1572864 | tf_op jit(solution)/shard_map/all_to_all | solution.py:97
  44.0 2.3 %all_to_all.18 = bf16[64,6144]{1,0:T(8,128)(2,1)S(1)} reshape(bf16[32,2,6144]{2,1,0:T(2,128)(2,1)} %all_to_all.24) | data formatting | bytes 1572864 | tf_op jit(solution)/shard_map/all_to_all | solution.py:97
  46.3 6.9 %fusion.4 = f32[64,1024]{1,0:T(8,128)S(1)} fusion(bf16[64,6144]{1,0:T(8,128)(2,1)S(1)} %all_to_all.18, bf16[1,6144,1024]{2,1,0:T(8,128)(2,1)} %param.23), kind=kOutput, calls=%fused_computation.4 | convolution fusion | flops 805306368 | bytes 13631488 | tf_op jit(solution)/shard_map/dot_general | solution.py:47
  53.2 6.9 %fusion.25 = bf16[64,1024]{1,0:T(8,128)(2,1)S(1)} fusion(bf16[64,6144]{1,0:T(8,128)(2,1)S(1)} %all_to_all.18, bf16[1,6144,1024]{2,1,0:T(8,128)(2,1)} %param.24, f32[64,1024]{1,0:T(8,128)S(1)} %fusion.4), kind=kOutput, calls=%fused_computation.19 | convolution fusion | flops 805699584 | bytes 13762560 | tf_op jit(solution)/shard_map/dot_general | solution.py:48
  60.0 0.1 reshape.75
  60.1 0.1 copy.54
  60.2 0.1 reshape.76
  60.3 7.8 %fusion.6 = bf16[64,6144]{1,0:T(8,128)(2,1)} fusion(bf16[64,1024]{1,0:T(8,128)(2,1)S(1)} %reshape.76, bf16[1,1024,6144]{2,1,0:T(8,128)(2,1)} %param.25), kind=kOutput, calls=%fused_computation.6 | convolution fusion | flops 805699584 | bytes 13500416 | tf_op jit(solution)/shard_map/dot_general | solution.py:108
  68.0 0.0 reduce-scatter.2.cloned.1.call-update
  68.0 32.7 %reduce-scatter.2.cloned.1.call-done = bf16[8,6144]{1,0:T(8,128)(2,1)} async-done(((bf16[64,6144]{1,0:T(8,128)(2,1)}), bf16[8,6144]{1,0:T(8,128)(2,1)}) %reduce-scatter.2.cloned.1.call-update) | async-done | bytes 98320 | tf_op jit(solution)/shard_map/reduce_scatter | solution.py:107
  100.7 1.0 all_to_all.19
  101.7 10.2 %all_to_all.25 = bf16[4,2,6144]{2,1,0:T(2,128)(2,1)S(1)} all-to-all(bf16[4,2,6144]{2,1,0:T(2,128)(2,1)S(1)} %all_to_all.19), channel_id=1, replica_groups=mesh['side'=2,'grp'=4,'cuts'=4] {'grp'}, dimensions={0} | all-to-all | bytes 196608 | tf_op jit(solution)/shard_map/all_to_all | solution.py:113
  111.9 0.8 fusion.9
  (8 shorter events, 0.1 us)
Async XLA Ops:
  6.5 5.3 %copy-start = (bf16[4,256,1024]{2,1,0:T(8,128)(2,1)S(1)}, bf16[4,256,1024]{2,1,0:T(8,128)(2,1)}, u32[]{:S(2)}) copy-start(bf16[4,256,1024]{2,1,0:T(8,128)(2,1)} %param.14) | copy-start | bytes 6291460
  6.5 94.2 %reduce-scatter.2.cloned.1.call-start = ((), (), s32[]{:S(2)}) async-start(), calls=%async_computation.3 | async-start | bytes 884736 | tf_op jit(solution)/shard_map/reduce_scatter | solution.py:107
  11.6 1.6 %copy-start.3 = (bf16[4,256,1024]{2,1,0:T(8,128)(2,1)S(1)}, bf16[4,256,1024]{2,1,0:T(8,128)(2,1)}, u32[]{:S(2)}) copy-start(bf16[4,256,1024]{2,1,0:T(8,128)(2,1)} %param.15) | copy-start | bytes 6291460
  12.5 1.2 %copy-start.1 = (bf16[4,6144]{1,0:T(4,128)(2,1)S(1)}, bf16[4,6144]{1,0:T(4,128)(2,1)}, u32[]{:S(2)}) copy-start(bf16[4,6144]{1,0:T(4,128)(2,1)} %param.19) | copy-start | bytes 147460
  12.5 1.5 %copy-start.4 = (bf16[6144,4]{0,1:T(4,128)(2,1)S(1)}, bf16[6144,4]{0,1:T(4,128)(2,1)}, u32[]{:S(2)}) copy-start(bf16[6144,4]{0,1:T(4,128)(2,1)} %param.21) | copy-start | bytes 147460
  12.8 1.4 %copy-start.2 = (s32[4,2]{0,1:T(2,128)S(1)}, s32[4,2]{0,1:T(2,128)}, u32[]{:S(2)}) copy-start(s32[4,2]{0,1:T(2,128)} %param.22) | copy-start | bytes 100
Sparse Core Ops, SparseCore 0:
  68.2 32.4 reduce-scatter.1
where the time goes:
time: 120 us
  blocking collectives  39 us (32%)
  waiting for transfers between devices  32.7 us (27%)
  matrix products  24 us (20%)
  between operations  13.6 us (11%)
  local copies, waits for them, and re-layouts  7.14 us (6%)
  other arithmetic  3.25 us (3%)
    reduce_scatter x1, waiting for transfers between devices, local(): lax.psum_scatter(jnp.dot(hidden, down_w, preferred_element_type=jnp.float...  32.7 us
    all_to_all x1, blocking collectives, local(): lax.all_to_all(copies.reshape(-1, width), ('side', 'grp', 'cuts'), split_...  28.7 us
    all_to_all x1, blocking collectives, local(): lax.all_to_all(mine.astype(jnp.bfloat16), 'grp', split_axis=0, concat_axi...  10.2 us
    dot_general x1, matrix products, local(): jnp.dot(hidden, down_w, preferred_element_type=jnp.float32)  7.75 us
    dot_general x1, matrix products, activate(): upper = jnp.dot(rows_in, up_w, preferred_element_type=jnp.float32)  6.88 us
    dot_general x1, matrix products, activate(): gate = jnp.dot(rows_in, gate_w, preferred_element_type=jnp.float32)  6.87 us
  transfers between devices with their start and end apart: 1, of which 1 were waited for; matrix products, arithmetic and copies ran while one was open for 0% of the time, Pallas kernels for 0%

commit v1 on v0

--- a/solution.py
+++ b/solution.py
@@ -91,28 +91,17 @@
     outgoing = jnp.einsum("rj,rx->jx", one_hot, normed, preferred_element_type=jnp.float32).astype(
         jnp.bfloat16
     )
-    copies = jnp.broadcast_to(
-        outgoing.reshape(1, experts, 1, most, width), (n_side, experts, n_cuts, most, width)
+    by_expert = lax.all_to_all(outgoing, "grp", split_axis=0, concat_axis=0, tiled=True)
+    arrived = lax.all_gather(by_expert, ("side", "cuts"), axis=0, tiled=True)
+    hidden = activate(arrived, gate_w, up_w)
+    partial = jnp.dot(hidden, down_w, preferred_element_type=jnp.float32).astype(jnp.bfloat16)
+    pieces = lax.all_to_all(partial, ("side", "cuts"), split_axis=0, concat_axis=0, tiled=True)
+    mine = jnp.sum(
+        pieces.reshape(n_side * n_cuts, experts * most, width).astype(jnp.float32), axis=0
     )
-    arrived = lax.all_to_all(
-        copies.reshape(-1, width), ("side", "grp", "cuts"), split_axis=0, concat_axis=0, tiled=True
-    )
-    hidden = activate(arrived, gate_w, up_w)
-    ff_dev = hidden.shape[1]
-    hidden = (
-        hidden.reshape(n_side, experts, n_cuts, most, ff_dev)
-        .transpose(0, 2, 1, 3, 4)
-        .reshape(-1, ff_dev)
-    )
-    mine = lax.psum_scatter(
-        jnp.dot(hidden, down_w, preferred_element_type=jnp.float32).astype(jnp.bfloat16),
-        ("side", "cuts"),
-        scatter_dimension=0,
-        tiled=True,
-    ).astype(jnp.float32)
     returned = lax.all_to_all(
         mine.astype(jnp.bfloat16), "grp", split_axis=0, concat_axis=0, tiled=True
-    ).astype(mine.dtype)
+    ).astype(jnp.float32)
     mixing = jnp.sum(jnp.where(placing, weights[:, :, None], 0.0), axis=1)
     combined = jnp.dot(
         mixing, returned, precision=lax.Precision.HIGHEST, preferred_element_type=jnp.float32

time: 120 us -> 76.9 us (0.64)
  waiting for transfers between devices: 32.7 us -> 0 us
  between operations: 13.6 us -> 0.14 us
  blocking collectives: 39 us -> 46.6 us
  local copies, waits for them, and re-layouts: 7.14 us -> 3.37 us
    reduce_scatter x1 -> x0, waiting for transfers between devices: 32.7 us -> none  [local(): lax.psum_scatter(jnp.dot(hidden, down_w, preferred_element_type=jnp.float...]
    all_gather x0 -> x1, blocking collectives: none -> 10.4 us  [local(): arrived = lax.all_gather(by_expert, ('side', 'cuts'), axis=0, tiled=True)]
    dot_general x1 -> x0, matrix products: 6.88 us -> none  [activate(): upper = jnp.dot(rows_in, up_w, preferred_element_type=jnp.float32)]
    dot_general x1, matrix products: 7.75 us -> 13.5 us  [local(): jnp.dot(hidden, down_w, preferred_element_type=jnp.float32)]
    all_to_all x1 -> x2, local copies, waits for them, and re-layouts: 2.28 us -> 0.13 us  [local(): lax.all_to_all(outgoing, 'grp', split_axis=0, concat_axis=0, tiled=True)]
    all_to_all x1, blocking collectives: 10.2 us -> 8.21 us  [local(): lax.all_to_all(mine.astype(jnp.bfloat16), 'grp', split_axis=0, concat_axi...]
    all_to_all x1 -> x2, blocking collectives: 28.7 us -> 28 us  [the longest x1 16 us: local(): lax.all_to_all(partial, ('side', 'cuts'), split_axis=0, concat_axis=0, ti...]
  transfers between devices with their start and end apart: 1 -> 0, of which waited for: 1 -> 0; matrix products, arithmetic and copies ran while one was open for 0% -> 0% of each run, Pallas kernels for 0% -> 0%
where the time goes in v1:
time: 76.9 us; the launch traced here: 76.4 us
  blocking collectives  46.6 us (61%)
  matrix products  22.9 us (30%)
  local copies, waits for them, and re-layouts  3.37 us (4%)
  other arithmetic  3.36 us (4%)
    all_to_all x1, blocking collectives, local(): lax.all_to_all(partial, ('side', 'cuts'), split_axis=0, concat_axis=0, ti...  16 us
    dot_general x1, matrix products, local(): jnp.dot(hidden, down_w, preferred_element_type=jnp.float32)  13.5 us
    all_to_all x1, blocking collectives, local(): lax.all_to_all(outgoing, 'grp', split_axis=0, concat_axis=0, tiled=True)  12 us
    all_gather x1, blocking collectives, local(): arrived = lax.all_gather(by_expert, ('side', 'cuts'), axis=0, tiled=True)  10.4 us
    all_to_all x1, blocking collectives, local(): lax.all_to_all(mine.astype(jnp.bfloat16), 'grp', split_axis=0, concat_axi...  8.21 us
    dot_general x1, matrix products, activate(): gate = jnp.dot(rows_in, gate_w, preferred_element_type=jnp.float32)  6.86 us

profile of v1, /device:TPU:0, one launch (start us, length us, event | category | flops | bytes accessed | tf_op | source)
XLA Modules:
  0.0 76.4 jit_solution(6336935366669088274)
XLA Ops:
  0.0 0.0 copy-start
  0.0 0.9 %iota_compare_fusion.3 = pred[4,256]{1,0:T(4,128)(4,1)S(1)} fusion(s32[4]{0:T(128)} %param.18), kind=kLoop, calls=%fused_computation.50 | loop fusion | flops 1024 | bytes 1040 | tf_op jit(solution)/shard_map/lt | solution.py:26
  0.9 0.8 %copy.26 = s32[4,2]{1,0:T(4,128)S(1)} copy(s32[4,2]{0,1:T(2,128)} %param.22) | data formatting | bytes 64 | tf_op args[9]
  1.6 0.1 eq.20
  1.7 0.2 convert_reduce_fusion.1
  1.9 0.1 reshape.68
  2.0 0.1 copy.28
  2.1 0.7 reshape.73
  2.8 0.7 convert_bitcast_fusion
  3.5 0.7 convert_element_type.48
  4.2 0.9 %reshape.63 = bf16[4,8,6,128]{3,2,1,0:T(8,128)(2,1)S(1)} reshape(bf16[4,6144]{1,0:T(4,128)(2,1)} %param.13) | data formatting | bytes 98304 | tf_op jit(solution)/shard_map/reshape | solution.py:17
  5.1 0.0 copy-start.3
  5.1 0.1 fusion.51
  5.3 0.0 copy-done
  5.3 0.7 fusion.50
  6.0 0.0 copy-start.1
  6.0 0.0 copy-start.4
  6.0 0.2 fusion.41
  6.2 0.0 copy-start.2
  6.3 0.4 copy-done.3
  6.7 0.4 fusion.31
  7.1 0.1 reshape.67
  7.2 0.0 copy-done.1
  7.2 0.2 multiply_reduce_fusion
  7.4 0.1 multiply_convert_fusion
  7.5 0.0 copy-done.4
  7.5 0.2 fusion.52
  7.7 0.0 copy-done.2
  7.7 0.2 select_reduce_fusion.1
  7.9 0.1 convert_reduce_fusion
  7.9 0.2 convolution_convert_fusion
  8.2 0.1 all_to_all.22
  8.3 12.0 %all_to_all.33 = bf16[4,2,6144]{2,1,0:T(2,128)(2,1)S(1)} all-to-all(bf16[4,2,6144]{2,1,0:T(2,128)(2,1)S(1)} %all_to_all.22), channel_id=1, replica_groups=mesh['side'=2,'grp'=4,'cuts'=4] {'grp'}, dimensions={0} | all-to-all | bytes 196608 | tf_op jit(solution)/shard_map/all_to_all | solution.py:94
  20.3 10.4 %all_gather.3 = bf16[64,6144]{1,0:T(8,128)(2,1)S(1)} all-gather(bf16[8,6144]{1,0:T(8,128)(2,1)S(1)} %all_to_all.24), channel_id=1, replica_groups=mesh['side'=2,'grp'=4,'cuts'=4] {'side','cuts'}, dimensions={0}, use_global_device_ids=true | all-gather | bytes 884736 | tf_op jit(solution)/shard_map/all_gather | solution.py:95
  30.7 6.9 %fusion.4 = f32[64,1024]{1,0:T(8,128)S(1)} fusion(bf16[64,6144]{1,0:T(8,128)(2,1)S(1)} %all_gather.3, bf16[1,6144,1024]{2,1,0:T(8,128)(2,1)} %param.23), kind=kOutput, calls=%fused_computation.4 | convolution fusion | flops 805306368 | bytes 13631488 | tf_op jit(solution)/shard_map/dot_general | solution.py:47
  37.5 13.5 %fusion.9 = bf16[8,8,6144]{2,1,0:T(8,128)(2,1)} fusion(bf16[1,1024,6144]{2,1,0:T(8,128)(2,1)} %param.25, bf16[64,6144]{1,0:T(8,128)(2,1)S(1)} %all_gather.3, bf16[1,6144,1024]{2,1,0:T(8,128)(2,1)} %param.24, f32[64,1024]{1,0:T(8,128)S(1)} %fusion.4), kind=kOutput, calls=%fused_computation.7 | convolution fusion | flops 1611399168 | bytes 27000832 | tf_op jit(solution)/shard_map/dot_general | solution.py:97
  51.1 16.0 %all_to_all.34 = bf16[8,8,6144]{2,1,0:T(8,128)(2,1)S(1)} all-to-all(bf16[8,8,6144]{2,1,0:T(8,128)(2,1)} %fusion.9), channel_id=1, replica_groups=mesh['side'=2,'grp'=4,'cuts'=4] {'side','cuts'}, dimensions={0} | all-to-all | bytes 1572864 | tf_op jit(solution)/shard_map/all_to_all | solution.py:98
  67.1 0.1 reduce_sum.72
  67.2 0.1 all_to_all.27
  67.3 8.2 %all_to_all.35 = bf16[4,2,6144]{2,1,0:T(2,128)(2,1)S(1)} all-to-all(bf16[4,2,6144]{2,1,0:T(2,128)(2,1)S(1)} %all_to_all.27), channel_id=1, replica_groups=mesh['side'=2,'grp'=4,'cuts'=4] {'grp'}, dimensions={0} | all-to-all | bytes 196608 | tf_op jit(solution)/shard_map/all_to_all | solution.py:102
  75.5 0.8 %fusion.12 = bf16[4,6144]{1,0:T(4,128)(2,1)} fusion(f32[4,8]{1,0:T(4,128)S(1)} %get-tuple-element.6, bf16[8,6144]{1,0:T(8,128)(2,1)S(1)} %all_to_all.29, f32[4,6144]{1,0:T(4,128)S(1)} %reshape.67, bf16[4,6144]{1,0:T(4,128)(2,1)S(1)} %copy-done.1), kind=kOutput, calls=%fused_computation.10 | convolution fusion | flops 2457600 | bytes 295040 | tf_op jit(solution)/shard_map/dot_general | solution.py:106
  (9 shorter events, 0.2 us)
Async XLA Ops:
  0.0 5.3 %copy-start = (bf16[4,256,1024]{2,1,0:T(8,128)(2,1)S(1)}, bf16[4,256,1024]{2,1,0:T(8,128)(2,1)}, u32[]{:S(2)}) copy-start(bf16[4,256,1024]{2,1,0:T(8,128)(2,1)} %param.14) | copy-start | bytes 6291460
  5.1 1.6 %copy-start.3 = (bf16[4,256,1024]{2,1,0:T(8,128)(2,1)S(1)}, bf16[4,256,1024]{2,1,0:T(8,128)(2,1)}, u32[]{:S(2)}) copy-start(bf16[4,256,1024]{2,1,0:T(8,128)(2,1)} %param.15) | copy-start | bytes 6291460
  6.0 1.2 %copy-start.1 = (bf16[4,6144]{1,0:T(4,128)(2,1)S(1)}, bf16[4,6144]{1,0:T(4,128)(2,1)}, u32[]{:S(2)}) copy-start(bf16[4,6144]{1,0:T(4,128)(2,1)} %param.19) | copy-start | bytes 147460
  6.0 1.5 %copy-start.4 = (bf16[6144,4]{0,1:T(4,128)(2,1)S(1)}, bf16[6144,4]{0,1:T(4,128)(2,1)}, u32[]{:S(2)}) copy-start(bf16[6144,4]{0,1:T(4,128)(2,1)} %param.21) | copy-start | bytes 147460
  6.2 1.4 %copy-start.2 = (s32[4,2]{0,1:T(2,128)S(1)}, s32[4,2]{0,1:T(2,128)}, u32[]{:S(2)}) copy-start(s32[4,2]{0,1:T(2,128)} %param.22) | copy-start | bytes 100

commit v2 on v1

v2 whole, which is shorter than its diff:
```python
import functools
import math

import jax
import jax.numpy as jnp
from jax import lax
from jax.experimental import pallas as pl
from jax.experimental.pallas import tpu as pltpu
from jax.sharding import PartitionSpec as P

Q_HEADS = 48
KV_HEADS = 8
HEAD_DIM = 128
GROUP = Q_HEADS // KV_HEADS
MIB = 2**20
VMEM = pl.BlockSpec(memory_space=pltpu.VMEM)
SMEM = pl.BlockSpec(memory_space=pltpu.SMEM)
HBM = pl.BlockSpec(memory_space=pltpu.HBM)
ANY = pl.BlockSpec(memory_space=pl.ANY)


def stacked_heads(x, first, copies=1):
    parts = [x[:, (first + j) * HEAD_DIM : (first + j + 1) * HEAD_DIM] for j in range(GROUP // copies)]
    return jnp.concatenate(parts * copies, axis=0)


def attend_kernel(experts, most, n_in, *refs):
    hbm_refs = refs[:n_in]
    out_refs = refs[n_in : n_in + experts]
    mixed_ref, mixing_ref = refs[n_in + experts : n_in + experts + 2]
    scratch = refs[n_in + experts + 2 : -2]
    sem, cache_sems = refs[-2:]
    k_any, v_any = hbm_refs[-2:]
    k_ref, v_ref = scratch[-2:]
    lengths, routes, q_ref, nk_ref, nv_ref, res_ref, gain_ref, router_ref = scratch[:-2]
    rows, width = q_ref.shape
    span = k_ref.shape[1]
    scale = 1.0 / math.sqrt(HEAD_DIM)
    small = [
        pltpu.make_async_copy(hbm_refs[i], scratch[i], sem.at[i]) for i in range(n_in - 2)
    ]
    loads_k = [
        pltpu.make_async_copy(k_any.at[r], k_ref.at[r], cache_sems.at[0, r]) for r in range(rows)
    ]
    loads_v = [
        pltpu.make_async_copy(v_any.at[r], v_ref.at[r], cache_sems.at[1, r]) for r in range(rows)
    ]
    for load in small + loads_k + loads_v:
        load.start()
    for load in small:
        load.wait()

    pair = 2
    pairs = KV_HEADS // pair
    stack = GROUP * rows
    tall = pair * stack
    wide = pair * HEAD_DIM
    row_of = lax.broadcasted_iota(jnp.int32, (tall, 1), 0) % rows
    length_of = jnp.zeros((tall, 1), jnp.int32)
    for r in range(rows):
        length_of = jnp.where(row_of == r, lengths[r], length_of)
    live = lax.broadcasted_iota(jnp.int32, (tall, span), 1) < length_of

    query = q_ref[...].astype(jnp.float32)
    new_key = nk_ref[...].astype(jnp.float32)
    new_value = nv_ref[...].astype(jnp.float32)
    blank = jnp.zeros((stack, HEAD_DIM), jnp.float32)
    lhs, own = [], []
    for p in range(pairs):
        heads = [stacked_heads(query, (pair * p + a) * GROUP) for a in range(pair)]
        keys = [stacked_heads(new_key, pair * p + a, GROUP) for a in range(pair)]
        lhs.append(
            jnp.concatenate(
                [
                    jnp.concatenate([heads[b] if a == b else blank for b in range(pair)], axis=1)
                    for a in range(pair)
                ],
                axis=0,
            ).astype(jnp.bfloat16)
        )
        own.append(
            jnp.sum(
                jnp.concatenate(heads, axis=0) * jnp.concatenate(keys, axis=0),
                axis=1,
                keepdims=True,
            )
            * scale
        )

    scores = [None] * pairs
    for r in range(rows):
        loads_k[r].wait()
        for p in range(pairs):
            part = lax.dot_general(
                lhs[p],
                k_ref[r, :, p * wide : (p + 1) * wide],
                (((1,), (1,)), ((), ())),
                preferred_element_type=jnp.float32,
            )
            scores[p] = part if r == 0 else jnp.where(row_of == r, part, scores[p])
    probs, own_probs = [], []
    for p in range(pairs):
        old = jnp.where(live, scores[p] * scale, -1e30)
        top = jnp.maximum(jnp.max(old, axis=1, keepdims=True), own[p])
        e_old = jnp.exp(old - top)
        e_own = jnp.exp(own[p] - top)
        share = 1.0 / (jnp.sum(e_old, axis=1, keepdims=True) + e_own)
        probs.append((e_old * share).astype(jnp.bfloat16))
        own_probs.append((e_own * share).astype(jnp.bfloat16).astype(jnp.float32))
    sums = [None] * pairs
    for r in range(rows):
        loads_v[r].wait()
        for p in range(pairs):
            part = jnp.dot(
                probs[p],
                v_ref[r, :, p * wide : (p + 1) * wide],
                preferred_element_type=jnp.float32,
            )
            sums[p] = part if r == 0 else jnp.where(row_of == r, part, sums[p])
    power = jnp.zeros((rows, HEAD_DIM), jnp.float32)
    for p in range(pairs):
        for a in range(pair):
            head = pair * p + a
            fresh = stacked_heads(new_value, head, GROUP)
            low = a * stack
            attended = (
                sums[p][low : low + stack, a * HEAD_DIM : (a + 1) * HEAD_DIM]
                + own_probs[p][low : low + stack] * fresh
            )
            for j in range(GROUP):
                at = pl.ds((head * GROUP + j) * HEAD_DIM, HEAD_DIM)
                mixed = res_ref[:, at].astype(jnp.float32) + attended[j * rows : (j + 1) * rows]
                mixed_ref[:, at] = mixed
                power = power + mixed * mixed
    mean = jnp.sum(power, axis=1, keepdims=True) * (1.0 / width)
    normed = mixed_ref[...] * lax.rsqrt(mean + 1e-05) * gain_ref[...].astype(jnp.float32).reshape(1, width)
    normed = normed.astype(jnp.bfloat16).astype(jnp.float32)

    router = router_ref[...].astype(jnp.float32)
    logits = [jnp.sum(normed * router[e : e + 1], axis=1, keepdims=True) for e in range(experts)]
    row_col = lax.broadcasted_iota(jnp.int32, (rows, 1), 0)

    def picked(i):
        value = jnp.zeros((rows, 1), jnp.float32)
        for r in range(rows):
            for e in range(experts):
                value = jnp.where((row_col == r) & (routes[i, r] == e), logits[e], value)
        return value

    first, second = picked(0), picked(1)
    share_of = [1.0 / (1.0 + jnp.exp(second - first)), 1.0 / (1.0 + jnp.exp(first - second))]

    here = lax.axis_index("grp")
    named = [(r, i, routes[i, r]) for r in range(rows) for i in range(2)]
    slots = []
    for at, (r, i, e) in enumerate(named):
        rank = jnp.int32(0)
        for _, _, other in named[:at]:
            rank = rank + (other == e).astype(jnp.int32)
        slots.append(jnp.bitwise_xor(e, here) * most + rank)
    slot_col = lax.broadcasted_iota(jnp.int32, (experts * most, 1), 0)
    slot_row = lax.broadcasted_iota(jnp.int32, (rows, experts * most), 1)
    outgoing = jnp.zeros((experts * most, width), jnp.float32)
    mixing = jnp.zeros((rows, experts * most), jnp.float32)
    for (r, i, _), slot in zip(named, slots, strict=True):
        outgoing = jnp.where(slot_col == slot, normed[r : r + 1], outgoing)
        mixing = jnp.where((slot_row == slot) & (row_col == r), share_of[i], mixing)
    outgoing = outgoing.astype(jnp.bfloat16)
    for j in range(experts):
        out_refs[j][...] = outgoing[j * most : (j + 1) * most]
    mixing_ref[...] = mixing


def load_kernel(w_ref, _, out_ref, sem):
    load = pltpu.make_async_copy(w_ref.at[0], out_ref, sem)
    load.start()
    load.wait()


def stack_kernel(*refs):
    refs[-1][...] = jnp.concatenate(
        [ref[...].astype(jnp.float32) for ref in refs[:-2]], axis=0
    ).astype(jnp.bfloat16)


def experts_kernel(
    own_ref,
    rest_ref,
    core_own_ref,
    core_rest_ref,
    gate_ref,
    up_ref,
    down_any,
    keep_ref,
    send_ref,
    x_ref,
    gate_sum,
    up_sum,
    down_ref,
    sems,
):
    loads = []
    wide = down_ref.shape[1] // sems.shape[0]
    for i in range(sems.shape[0]):
        at = pl.ds(i * wide, wide)
        loads.append(
            pltpu.make_async_copy(down_any.at[0, :, at], down_ref.at[:, at], sems.at[i])
        )
        loads[-1].start()
    width = x_ref.shape[1]
    half = keep_ref.shape[0]
    x_ref[:half] = jnp.concatenate([own_ref[...], rest_ref[...]], axis=0)
    x_ref[half:] = jnp.concatenate([core_own_ref[...], core_rest_ref[...]], axis=0)
    deep = 1024
    for step in range(width // deep):
        at = pl.ds(step * deep, deep)
        x = x_ref[:, at]
        gate = jnp.dot(x, gate_ref[at, :], preferred_element_type=jnp.float32)
        upper = jnp.dot(x, up_ref[at, :], preferred_element_type=jnp.float32)
        if step == 0:
            gate_sum[...] = gate
            up_sum[...] = upper
        else:
            gate_sum[...] += gate
            up_sum[...] += upper
    gate = gate_sum[...]
    hidden = (gate / (1.0 + jnp.exp(-gate)) * up_sum[...]).astype(jnp.bfloat16)
    for i, load in enumerate(loads):
        load.wait()
        for low in range(i * wide, (i + 1) * wide, deep):
            at = pl.ds(low, deep)
            piece = jnp.dot(hidden, down_ref[:, at], preferred_element_type=jnp.float32)
            piece = piece.astype(jnp.bfloat16)
            keep_ref[:, at] = piece[:half]
            send_ref[:, at] = piece[half:]


def chip_sum_kernel(keep_ref, got_ref, own_ref, *out_refs):
    total = keep_ref[...].astype(jnp.float32) + got_ref[...].astype(jnp.float32)
    part = own_ref.shape[0]
    own_ref[...] = total[:part]
    for i, ref in enumerate(out_refs):
        ref[...] = total[(i + 1) * part : (i + 2) * part].astype(jnp.bfloat16)


def plane_sum_kernel(got, own_ref, *refs):
    total = own_ref[...]
    for ref in refs[:got]:
        total = total + ref[...].astype(jnp.float32)
    total = total.astype(jnp.bfloat16)
    outs = refs[got:]
    most = outs[0].shape[0]
    for j, ref in enumerate(outs):
        ref[...] = total[j * most : (j + 1) * most]


def finish_kernel(mixed_ref, mixing_ref, *refs):
    total = mixed_ref[...]
    most = refs[0].shape[0]
    for j, ref in enumerate(refs[:-1]):
        rows = ref[...].astype(jnp.float32)
        for s in range(most):
            at = j * most + s
            total = total + mixing_ref[:, at : at + 1] * rows[s : s + 1]
    refs[-1][...] = total.astype(jnp.bfloat16)


def call(kernel, outs, in_specs, *args, scratch=(), limit=8, cost=None):
    return pl.pallas_call(
        kernel,
        out_shape=outs,
        in_specs=in_specs,
        out_specs=jax.tree.map(lambda _: VMEM, outs),
        scratch_shapes=list(scratch),
        compiler_params=pltpu.CompilerParams(vmem_limit_bytes=limit * MIB),
        cost_estimate=cost,
    )(*args)


def in_hbm(x):
    return pltpu.with_memory_space_constraint(x, pltpu.HBM)


def shape(extent, kind=jnp.bfloat16):
    return jax.ShapeDtypeStruct(extent, kind)


def local(
    query,
    k_cache,
    v_cache,
    new_key,
    new_value,
    lengths,
    residual,
    norm_gain,
    router,
    routes,
    w_gate,
    w_up,
    w_down,
):
    rows, width = query.shape
    experts = lax.axis_size("grp")
    n_side = lax.axis_size("side")
    n_cuts = lax.axis_size("cuts")
    most = max(2, 2 * rows // experts)
    slots = experts * most
    plane = ("side", "cuts")

    def to_grp(x, j):
        return lax.ppermute(x, "grp", [(i, i ^ j) for i in range(experts)])

    def to_plane(x, k):
        return lax.ppermute(x, plane, [(i, i ^ k) for i in range(n_side * n_cuts)])

    small = [
        lengths,
        routes.T,
        query,
        new_key,
        new_value,
        residual,
        norm_gain,
        router.T,
    ]
    *outgoing, mixed, mixing = call(
        functools.partial(attend_kernel, experts, most, len(small) + 2),
        [shape((most, width)) for _ in range(experts)]
        + [shape((rows, width), jnp.float32), shape((rows, slots), jnp.float32)],
        [HBM] * (len(small) + 2),
        *[in_hbm(x) for x in small],
        in_hbm(k_cache),
        in_hbm(v_cache),
        scratch=[
            (pltpu.SMEM if i < 2 else pltpu.VMEM)(x.shape, x.dtype) for i, x in enumerate(small)
        ]
        + [
            pltpu.VMEM(k_cache.shape, jnp.bfloat16),
            pltpu.VMEM(v_cache.shape, jnp.bfloat16),
            pltpu.SemaphoreType.DMA((len(small),)),
            pltpu.SemaphoreType.DMA((2, rows)),
        ],
        limit=14,
    )

    def load(weights, after):
        extent = weights.shape[1:]
        return call(
            load_kernel,
            pltpu.VMEM(extent, jnp.bfloat16),
            [HBM, ANY],
            in_hbm(weights),
            after,
            scratch=[pltpu.SemaphoreType.DMA],
            cost=pl.CostEstimate(
                flops=0, bytes_accessed=math.prod(extent) * 2, transcendentals=0
            ),
        )

    gate = load(w_gate, mixing)
    arrived = [outgoing[0]] + [to_grp(outgoing[j], j) for j in range(1, experts)]
    block = call(stack_kernel, shape((slots, width)), [VMEM] * experts + [ANY], *arrived, gate)
    upper = load(w_up, block)
    chips = range(0, n_side * n_cuts, 2)
    others = len(chips) - 1
    fetched = [to_plane(block, k) for k in chips[1:]]
    rest = call(
        stack_kernel, shape((others * slots, width)), [VMEM] * others + [ANY], *fetched, upper
    )
    parts = [block, rest, to_plane(block, 1), to_plane(rest, 1)]
    half = len(chips) * slots
    hidden = w_gate.shape[2]
    keep, send = call(
        experts_kernel,
        [shape((half, width))] * 2,
        [VMEM] * 6 + [HBM],
        *parts,
        gate,
        upper,
        in_hbm(w_down),
        scratch=[
            pltpu.VMEM((2 * half, width), jnp.bfloat16),
            pltpu.VMEM((2 * half, hidden), jnp.float32),
            pltpu.VMEM((2 * half, hidden), jnp.float32),
            pltpu.VMEM((hidden, width), jnp.bfloat16),
            pltpu.SemaphoreType.DMA((3,)),
        ],
        limit=24,
    )
    got = to_plane(send, 1)
    own, *partial = call(
        chip_sum_kernel,
        [shape((slots, width), jnp.float32)] + [shape((slots, width))] * others,
        [VMEM] * 2,
        keep,
        got,
    )
    gathered = [to_plane(x, k) for x, k in zip(partial, chips[1:], strict=True)]
    finished = call(
        functools.partial(plane_sum_kernel, len(gathered)),
        [shape((most, width)) for _ in range(experts)],
        [VMEM] * (1 + len(gathered)),
        own,
        *gathered,
    )
    returned = [finished[0]] + [to_grp(finished[j], j) for j in range(1, experts)]
    return call(
        finish_kernel,
        shape((rows, width)),
        [VMEM] * (2 + experts),
        mixed,
        mixing,
        *returned,
    )


def solution(mesh):
    placed = (
        P(("side", "grp", "cuts"), None),
        P(("side", "grp", "cuts"), None, None),
        P(("side", "grp", "cuts"), None, None),
        P(("side", "grp", "cuts"), None),
        P(("side", "grp", "cuts"), None),
        P(("side", "grp", "cuts")),
        P(("side", "grp", "cuts"), None),
        P(),
        P(),
        P(("side", "grp", "cuts"), None),
        P("grp", None, ("side", "cuts")),
        P("grp", None, ("side", "cuts")),
        P("grp", ("side", "cuts"), None),
    )
    return jax.shard_map(
        local,
        mesh=mesh,
        in_specs=placed,
        out_specs=P(("side", "grp", "cuts"), None),
        check_vma=False,
    )
```

time: 76.9 us -> 56.8 us (0.74)
  blocking collectives: 46.6 us -> 0 us
  Pallas kernels: 0 us -> 25 us
  matrix products: 22.9 us -> 0 us
  starting transfers between devices: 0 us -> 18 us
  waiting for transfers between devices: 0 us -> 13.5 us
  local copies, waits for them, and re-layouts: 3.37 us -> 0 us
  other arithmetic: 3.36 us -> 0 us
    all_to_all x3 -> x0, blocking collectives: 36.2 us -> none  [the longest x1 16 us: local(): lax.all_to_all(partial, ('side', 'cuts'), split_axis=0, concat_axis=0, ti...]
    pallas_call x0 -> x9, Pallas kernels: none -> 25 us  [call(): pl.pallas_call(kernel, out_shape=outs, in_specs=in_specs, out_specs=jax.t...]
    dot_general x8 -> x0, matrix products: 22.9 us -> none  [the longest x1 13.5 us: local(): jnp.dot(hidden, down_w, preferred_element_type=jnp.float32)]
    ppermute x0 -> x15, starting transfers between devices: none -> 18 us  [the longest x6 10.1 us: to_grp(): return lax.ppermute(x, 'grp', [(i, i ^ j) for i in range(experts)])]
    ppermute x0 -> x15, waiting for transfers between devices: none -> 13.5 us  [the longest x9 7.85 us: to_plane(): return lax.ppermute(x, plane, [(i, i ^ k) for i in range(n_side * n_cuts)])]
    all_gather x1 -> x0, blocking collectives: 10.4 us -> none  [local(): arrived = lax.all_gather(by_expert, ('side', 'cuts'), axis=0, tiled=True)]
    reshape x4 -> x0, local copies, waits for them, and re-layouts: 1.72 us -> none  [the longest x1 0.86 us: attend(): queries = query.reshape(rows, KV_HEADS, group, HEAD_DIM)]
    unnamed x12 -> x0, local copies, waits for them, and re-layouts: 1.23 us -> none
  transfers between devices with their start and end apart: 0 -> 15, of which waited for: 0 -> 8; matrix products, arithmetic and copies ran while one was open for 0% -> 0% of each run, Pallas kernels for 0% -> 16%
where the time goes in v2:
time: 56.8 us; the launch traced here: 56.6 us
  Pallas kernels  25 us (44%)
  starting transfers between devices  18 us (32%)
  waiting for transfers between devices  13.5 us (24%)
    pallas_call x9, Pallas kernels, call(): pl.pallas_call(kernel, out_shape=outs, in_specs=in_specs, out_specs=jax.t...  25 us
    ppermute x6, starting transfers between devices, to_grp(): return lax.ppermute(x, 'grp', [(i, i ^ j) for i in range(experts)])  10.1 us
    ppermute x9, starting transfers between devices, to_plane(): return lax.ppermute(x, plane, [(i, i ^ k) for i in range(n_side * n_cuts)])  7.88 us
    ppermute x9, waiting for transfers between devices, to_plane(): return lax.ppermute(x, plane, [(i, i ^ k) for i in range(n_side * n_cuts)])  7.85 us
    ppermute x6, waiting for transfers between devices, to_grp(): return lax.ppermute(x, 'grp', [(i, i ^ j) for i in range(experts)])  5.64 us
  transfers between devices with their start and end apart: 15, of which 8 were waited for; matrix products, arithmetic and copies ran while one was open for 0% of the time, Pallas kernels for 16%

profile of v2, /device:TPU:0, one launch (start us, length us, event | category | flops | bytes accessed | tf_op | source)
XLA Modules:
  0.0 56.6 jit_solution(16933348722975118992)
XLA Ops:
  0.0 4.9 %shard_map.127 = (bf16[2,6144]{1,0:T(2,128)(2,1)S(1)}, bf16[2,6144]{1,0:T(2,128)(2,1)S(1)}, bf16[2,6144]{1,0:T(2,128)(2,1)S(1)}, bf16[2,6144]{1,0:T(2,128)(2,1)S...) custom-call(s32[4]{0:T(128)} %refs_0_.1, s32[2,4]{1,0:T(2,128)} %bitcast.3, bf16[4,6144]{1,0:T(4,128)(2,1)} %refs_2_.1, ...), custom_call_target="tpu_custom_call" | custom-call | tf_op jit(solution)/shard_map/pallas_call | solution.py:269
  4.9 3.1 %collective-permute-start = (bf16[2,6144]{1,0:T(2,128)(2,1)S(1)}, bf16[2,6144]{1,0:T(2,128)(2,1)S(1)}, u32[]{:S(2)}, u32[]{:S(2)}) collective-permute-start(bf16[2,6144]{1,0:T(2,128)(2,1)S(1)} %get-tuple-element.24), channel_id=1, source_target_pairs={{0,4},{4,0},{8,12},{12,8},{1,5},{5,1},{9,13},{13,9},{2,6},{6,2},{1... | collective-permute-start | bytes 73736 | tf_op jit(solution)/shard_map/ppermute | solution.py:312
  8.0 2.6 %collective-permute-start.1 = (bf16[2,6144]{1,0:T(2,128)(2,1)S(1)}, bf16[2,6144]{1,0:T(2,128)(2,1)S(1)}, u32[]{:S(2)}, u32[]{:S(2)}) collective-permute-start(bf16[2,6144]{1,0:T(2,128)(2,1)S(1)} %get-tuple-element.25), channel_id=1, source_target_pairs={{0,8},{4,12},{8,0},{12,4},{1,9},{5,13},{9,1},{13,5},{2,10},{6,14},... | collective-permute-start | bytes 73736 | tf_op jit(solution)/shard_map/ppermute | solution.py:312
  10.5 0.0 collective-permute-start.2
  10.5 4.6 %shard_map.128.refs_4_.gate_ref = bf16[6144,1024]{1,0:T(8,128)(2,1)S(1)} custom-call(bf16[1,6144,1024]{2,1,0:T(8,128)(2,1)} %w_ref.2, f32[4,8]{1,0:T(4,128)S(1)} %get-tuple-element.22._.mixing_ref), custom_call_target="tpu_custom_call" | custom-call | bytes 12582912 | tf_op jit(solution)/shard_map/pallas_call | solution.py:269
  15.1 0.0 collective-permute-done.refs_1_
  15.1 0.0 collective-permute-done.1.refs_2_
  15.2 1.0 %collective-permute-done.2.refs_3_ = bf16[2,6144]{1,0:T(2,128)(2,1)S(1)} collective-permute-done((bf16[2,6144]{1,0:T(2,128)(2,1)S(1)}, bf16[2,6144]{1,0:T(2,128)(2,1)S(1)}, u32[]{:S(2)}, u32[]{:S(2)}) %collective-permute-start.2) | collective-permute-done | bytes 24608 | tf_op jit(solution)/shard_map/ppermute | solution.py:312
  16.2 0.1 shard_map.129._.own_ref
  16.2 2.5 %collective-permute-start.5 = (bf16[8,6144]{1,0:T(8,128)(2,1)S(1)}, bf16[8,6144]{1,0:T(8,128)(2,1)S(1)}, u32[]{:S(2)}, u32[]{:S(2)}) collective-permute-start(bf16[8,6144]{1,0:T(8,128)(2,1)S(1)} %shard_map.129._.own_ref), channel_id=1, source_target_pairs={{0,18},{1,19},{2,16},{3,17},{16,2},{17,3},{18,0},{19,1},{4,22},{5,... | collective-permute-start | bytes 294920 | tf_op jit(solution)/shard_map/ppermute | solution.py:315
  18.7 0.5 collective-permute-start.4
  19.3 0.5 collective-permute-start.3
  19.8 4.6 %shard_map.130.refs_3_.up_ref = bf16[6144,1024]{1,0:T(8,128)(2,1)S(1)} custom-call(bf16[1,6144,1024]{2,1,0:T(8,128)(2,1)} %w_ref.3, bf16[8,6144]{1,0:T(8,128)(2,1)S(1)} %shard_map.129._.own_ref), custom_call_target="tpu_custom_call" | custom-call | bytes 12582912 | tf_op jit(solution)/shard_map/pallas_call | solution.py:269
  24.4 0.0 collective-permute-done.5.refs_2_
  24.4 0.0 collective-permute-done.4.refs_1_
  24.4 0.0 collective-permute-done.3.refs_0_
  24.4 0.1 collective-permute-start.7
  24.5 0.5 collective-permute-start.6
  25.0 1.2 %collective-permute-done.6.core_own_ref = bf16[8,6144]{1,0:T(8,128)(2,1)S(1)} collective-permute-done((bf16[8,6144]{1,0:T(8,128)(2,1)S(1)}, bf16[8,6144]{1,0:T(8,128)(2,1)S(1)}, u32[]{:S(2)}, u32[]{:S(2)}) %collective-permute-start.6) | collective-permute-done | bytes 98336 | tf_op jit(solution)/shard_map/ppermute | solution.py:315
  26.2 0.0 collective-permute-done.7.core_rest_ref
  26.2 9.9 %shard_map.132 = (bf16[32,6144]{1,0:T(8,128)(2,1)S(1)}, bf16[32,6144]{1,0:T(8,128)(2,1)S(1)}) custom-call(bf16[8,6144]{1,0:T(8,128)(2,1)S(1)} %shard_map.129._.own_ref, bf16[24,6144]{1,0:T(8,128)(2,1)S(1)} %shard_map.131.rest_ref, bf16[8,6144]{1,0:T(8,128)(2,1)S(1)} %collective-permute-done.6.core_own_ref, ...), custom_call_target="tpu_custom_call" | custom-call | tf_op jit(solution)/shard_map/pallas_call | solution.py:269
  36.1 0.2 collective-permute-start.8
  36.3 1.6 %collective-permute-done.8.got_ref = bf16[32,6144]{1,0:T(8,128)(2,1)S(1)} collective-permute-done((bf16[32,6144]{1,0:T(8,128)(2,1)S(1)}, bf16[32,6144]{1,0:T(8,128)(2,1)S(1)}, u32[]{:S(2)}, u32[]{:S(2)}) %collective-permute-start.8) | collective-permute-done | bytes 393248 | tf_op jit(solution)/shard_map/ppermute | solution.py:315
  37.9 0.1 shard_map.133
  38.0 1.6 %collective-permute-start.9 = (bf16[8,6144]{1,0:T(8,128)(2,1)S(1)}, bf16[8,6144]{1,0:T(8,128)(2,1)S(1)}, u32[]{:S(2)}, u32[]{:S(2)}) collective-permute-start(bf16[8,6144]{1,0:T(8,128)(2,1)S(1)} %get-tuple-element.30), channel_id=1, source_target_pairs={{0,2},{1,3},{2,0},{3,1},{16,18},{17,19},{18,16},{19,17},{4,6},{5,7... | collective-permute-start | bytes 294920 | tf_op jit(solution)/shard_map/ppermute | solution.py:315
  39.5 1.5 %collective-permute-start.10 = (bf16[8,6144]{1,0:T(8,128)(2,1)S(1)}, bf16[8,6144]{1,0:T(8,128)(2,1)S(1)}, u32[]{:S(2)}, u32[]{:S(2)}) collective-permute-start(bf16[8,6144]{1,0:T(8,128)(2,1)S(1)} %get-tuple-element.31), channel_id=1, source_target_pairs={{0,16},{1,17},{2,18},{3,19},{16,0},{17,1},{18,2},{19,3},{4,20},{5,... | collective-permute-start | bytes 294920 | tf_op jit(solution)/shard_map/ppermute | solution.py:315
  41.1 0.5 collective-permute-start.11
  41.5 1.3 %collective-permute-done.9.refs_0_ = bf16[8,6144]{1,0:T(8,128)(2,1)S(1)} collective-permute-done((bf16[8,6144]{1,0:T(8,128)(2,1)S(1)}, bf16[8,6144]{1,0:T(8,128)(2,1)S(1)}, u32[]{:S(2)}, u32[]{:S(2)}) %collective-permute-start.9) | collective-permute-done | bytes 98336 | tf_op jit(solution)/shard_map/ppermute | solution.py:315
  42.9 2.4 %collective-permute-done.10.refs_1_ = bf16[8,6144]{1,0:T(8,128)(2,1)S(1)} collective-permute-done((bf16[8,6144]{1,0:T(8,128)(2,1)S(1)}, bf16[8,6144]{1,0:T(8,128)(2,1)S(1)}, u32[]{:S(2)}, u32[]{:S(2)}) %collective-permute-start.10) | collective-permute-done | bytes 98336 | tf_op jit(solution)/shard_map/ppermute | solution.py:315
  45.3 1.3 %collective-permute-done.11.refs_2_ = bf16[8,6144]{1,0:T(8,128)(2,1)S(1)} collective-permute-done((bf16[8,6144]{1,0:T(8,128)(2,1)S(1)}, bf16[8,6144]{1,0:T(8,128)(2,1)S(1)}, u32[]{:S(2)}, u32[]{:S(2)}) %collective-permute-start.11) | collective-permute-done | bytes 98336 | tf_op jit(solution)/shard_map/ppermute | solution.py:315
  46.6 0.1 shard_map.134
  46.6 0.1 collective-permute-start.12
  46.7 3.4 %collective-permute-start.13 = (bf16[2,6144]{1,0:T(2,128)(2,1)S(1)}, bf16[2,6144]{1,0:T(2,128)(2,1)S(1)}, u32[]{:S(2)}, u32[]{:S(2)}) collective-permute-start(bf16[2,6144]{1,0:T(2,128)(2,1)S(1)} %get-tuple-element.35), channel_id=1, source_target_pairs={{0,8},{4,12},{8,0},{12,4},{1,9},{5,13},{9,1},{13,5},{2,10},{6,14},... | collective-permute-start | bytes 73736 | tf_op jit(solution)/shard_map/ppermute | solution.py:312
  50.1 1.0 %collective-permute-start.14 = (bf16[2,6144]{1,0:T(2,128)(2,1)S(1)}, bf16[2,6144]{1,0:T(2,128)(2,1)S(1)}, u32[]{:S(2)}, u32[]{:S(2)}) collective-permute-start(bf16[2,6144]{1,0:T(2,128)(2,1)S(1)} %get-tuple-element.36), channel_id=1, source_target_pairs={{0,12},{4,8},{8,4},{12,0},{1,13},{5,9},{9,5},{13,1},{2,14},{6,10},... | collective-permute-start | bytes 73736 | tf_op jit(solution)/shard_map/ppermute | solution.py:312
  51.1 0.0 collective-permute-done.12.refs_1_
  51.1 0.8 %collective-permute-done.13.refs_2_ = bf16[2,6144]{1,0:T(2,128)(2,1)S(1)} collective-permute-done((bf16[2,6144]{1,0:T(2,128)(2,1)S(1)}, bf16[2,6144]{1,0:T(2,128)(2,1)S(1)}, u32[]{:S(2)}, u32[]{:S(2)}) %collective-permute-start.13) | collective-permute-done | bytes 24608 | tf_op jit(solution)/shard_map/ppermute | solution.py:312
  51.9 3.8 %collective-permute-done.14.refs_3_ = bf16[2,6144]{1,0:T(2,128)(2,1)S(1)} collective-permute-done((bf16[2,6144]{1,0:T(2,128)(2,1)S(1)}, bf16[2,6144]{1,0:T(2,128)(2,1)S(1)}, u32[]{:S(2)}, u32[]{:S(2)}) %collective-permute-start.14) | collective-permute-done | bytes 24608 | tf_op jit(solution)/shard_map/ppermute | solution.py:312
  55.7 0.9 %shard_map.135 = bf16[4,6144]{1,0:T(4,128)(2,1)} custom-call(f32[4,6144]{1,0:T(4,128)S(1)} %get-tuple-element.21.mixed_ref, f32[4,8]{1,0:T(4,128)S(1)} %get-tuple-element.22._.mixing_ref, bf16[2,6144]{1,0:T(2,128)(2,1)S(1)} %get-tuple-element.33.refs_0_, bf16[2,6144]{1,0:T(2,128)(2,1)S(1)} %collective-permute-done.12.refs_1_, ...), custom_call_target="tpu_custom_call" | custom-call | tf_op jit(solution)/shard_map/pallas_call | solution.py:269
  (1 shorter events, 0.0 us)
Async XLA Ops:
  4.9 10.3 %collective-permute-start = (bf16[2,6144]{1,0:T(2,128)(2,1)S(1)}, bf16[2,6144]{1,0:T(2,128)(2,1)S(1)}, u32[]{:S(2)}, u32[]{:S(2)}) collective-permute-start(bf16[2,6144]{1,0:T(2,128)(2,1)S(1)} %get-tuple-element.24), channel_id=1, source_target_pairs={{0,4},{4,0},{8,12},{12,8},{1,5},{5,1},{9,13},{13,9},{2,6},{6,2},{1... | collective-permute-start | bytes 73736 | tf_op jit(solution)/shard_map/ppermute | solution.py:312
  8.0 7.2 %collective-permute-start.1 = (bf16[2,6144]{1,0:T(2,128)(2,1)S(1)}, bf16[2,6144]{1,0:T(2,128)(2,1)S(1)}, u32[]{:S(2)}, u32[]{:S(2)}) collective-permute-start(bf16[2,6144]{1,0:T(2,128)(2,1)S(1)} %get-tuple-element.25), channel_id=1, source_target_pairs={{0,8},{4,12},{8,0},{12,4},{1,9},{5,13},{9,1},{13,5},{2,10},{6,14},... | collective-permute-start | bytes 73736 | tf_op jit(solution)/shard_map/ppermute | solution.py:312
  10.5 5.6 %collective-permute-start.2 = (bf16[2,6144]{1,0:T(2,128)(2,1)S(1)}, bf16[2,6144]{1,0:T(2,128)(2,1)S(1)}, u32[]{:S(2)}, u32[]{:S(2)}) collective-permute-start(bf16[2,6144]{1,0:T(2,128)(2,1)S(1)} %get-tuple-element.26), channel_id=1, source_target_pairs={{0,12},{4,8},{8,4},{12,0},{1,13},{5,9},{9,5},{13,1},{2,14},{6,10},... | collective-permute-start | bytes 73736 | tf_op jit(solution)/shard_map/ppermute | solution.py:312
  16.2 8.1 %collective-permute-start.5 = (bf16[8,6144]{1,0:T(8,128)(2,1)S(1)}, bf16[8,6144]{1,0:T(8,128)(2,1)S(1)}, u32[]{:S(2)}, u32[]{:S(2)}) collective-permute-start(bf16[8,6144]{1,0:T(8,128)(2,1)S(1)} %shard_map.129._.own_ref), channel_id=1, source_target_pairs={{0,18},{1,19},{2,16},{3,17},{16,2},{17,3},{18,0},{19,1},{4,22},{5,... | collective-permute-start | bytes 294920 | tf_op jit(solution)/shard_map/ppermute | solution.py:315
  18.7 5.6 %collective-permute-start.4 = (bf16[8,6144]{1,0:T(8,128)(2,1)S(1)}, bf16[8,6144]{1,0:T(8,128)(2,1)S(1)}, u32[]{:S(2)}, u32[]{:S(2)}) collective-permute-start(bf16[8,6144]{1,0:T(8,128)(2,1)S(1)} %shard_map.129._.own_ref), channel_id=1, source_target_pairs={{0,16},{1,17},{2,18},{3,19},{16,0},{17,1},{18,2},{19,3},{4,20},{5,... | collective-permute-start | bytes 294920 | tf_op jit(solution)/shard_map/ppermute | solution.py:315
  19.3 5.1 %collective-permute-start.3 = (bf16[8,6144]{1,0:T(8,128)(2,1)S(1)}, bf16[8,6144]{1,0:T(8,128)(2,1)S(1)}, u32[]{:S(2)}, u32[]{:S(2)}) collective-permute-start(bf16[8,6144]{1,0:T(8,128)(2,1)S(1)} %shard_map.129._.own_ref), channel_id=1, source_target_pairs={{0,2},{1,3},{2,0},{3,1},{16,18},{17,19},{18,16},{19,17},{4,6},{5,7... | collective-permute-start | bytes 294920 | tf_op jit(solution)/shard_map/ppermute | solution.py:315
  24.4 1.8 %collective-permute-start.7 = (bf16[24,6144]{1,0:T(8,128)(2,1)S(1)}, bf16[24,6144]{1,0:T(8,128)(2,1)S(1)}, u32[]{:S(2)}, u32[]{:S(2)}) collective-permute-start(bf16[24,6144]{1,0:T(8,128)(2,1)S(1)} %shard_map.131.rest_ref), channel_id=1, source_target_pairs={{0,1},{1,0},{2,3},{3,2},{16,17},{17,16},{18,19},{19,18},{4,5},{5,4... | collective-permute-start | bytes 884744 | tf_op jit(solution)/shard_map/ppermute | solution.py:315
  24.5 1.7 %collective-permute-start.6 = (bf16[8,6144]{1,0:T(8,128)(2,1)S(1)}, bf16[8,6144]{1,0:T(8,128)(2,1)S(1)}, u32[]{:S(2)}, u32[]{:S(2)}) collective-permute-start(bf16[8,6144]{1,0:T(8,128)(2,1)S(1)} %shard_map.129._.own_ref), channel_id=1, source_target_pairs={{0,1},{1,0},{2,3},{3,2},{16,17},{17,16},{18,19},{19,18},{4,5},{5,4... | collective-permute-start | bytes 294920 | tf_op jit(solution)/shard_map/ppermute | solution.py:315
  36.1 1.8 %collective-permute-start.8 = (bf16[32,6144]{1,0:T(8,128)(2,1)S(1)}, bf16[32,6144]{1,0:T(8,128)(2,1)S(1)}, u32[]{:S(2)}, u32[]{:S(2)}) collective-permute-start(bf16[32,6144]{1,0:T(8,128)(2,1)S(1)} %get-tuple-element.28), channel_id=1, source_target_pairs={{0,1},{1,0},{2,3},{3,2},{16,17},{17,16},{18,19},{19,18},{4,5},{5,4... | collective-permute-start | bytes 1179656 | tf_op jit(solution)/shard_map/ppermute | solution.py:315
  38.0 4.9 %collective-permute-start.9 = (bf16[8,6144]{1,0:T(8,128)(2,1)S(1)}, bf16[8,6144]{1,0:T(8,128)(2,1)S(1)}, u32[]{:S(2)}, u32[]{:S(2)}) collective-permute-start(bf16[8,6144]{1,0:T(8,128)(2,1)S(1)} %get-tuple-element.30), channel_id=1, source_target_pairs={{0,2},{1,3},{2,0},{3,1},{16,18},{17,19},{18,16},{19,17},{4,6},{5,7... | collective-permute-start | bytes 294920 | tf_op jit(solution)/shard_map/ppermute | solution.py:315
  39.5 5.8 %collective-permute-start.10 = (bf16[8,6144]{1,0:T(8,128)(2,1)S(1)}, bf16[8,6144]{1,0:T(8,128)(2,1)S(1)}, u32[]{:S(2)}, u32[]{:S(2)}) collective-permute-start(bf16[8,6144]{1,0:T(8,128)(2,1)S(1)} %get-tuple-element.31), channel_id=1, source_target_pairs={{0,16},{1,17},{2,18},{3,19},{16,0},{17,1},{18,2},{19,3},{4,20},{5,... | collective-permute-start | bytes 294920 | tf_op jit(solution)/shard_map/ppermute | solution.py:315
  41.1 5.5 %collective-permute-start.11 = (bf16[8,6144]{1,0:T(8,128)(2,1)S(1)}, bf16[8,6144]{1,0:T(8,128)(2,1)S(1)}, u32[]{:S(2)}, u32[]{:S(2)}) collective-permute-start(bf16[8,6144]{1,0:T(8,128)(2,1)S(1)} %get-tuple-element.32), channel_id=1, source_target_pairs={{0,18},{1,19},{2,16},{3,17},{16,2},{17,3},{18,0},{19,1},{4,22},{5,... | collective-permute-start | bytes 294920 | tf_op jit(solution)/shard_map/ppermute | solution.py:315
  46.6 4.5 %collective-permute-start.12 = (bf16[2,6144]{1,0:T(2,128)(2,1)S(1)}, bf16[2,6144]{1,0:T(2,128)(2,1)S(1)}, u32[]{:S(2)}, u32[]{:S(2)}) collective-permute-start(bf16[2,6144]{1,0:T(2,128)(2,1)S(1)} %get-tuple-element.34), channel_id=1, source_target_pairs={{0,4},{4,0},{8,12},{12,8},{1,5},{5,1},{9,13},{13,9},{2,6},{6,2},{1... | collective-permute-start | bytes 73736 | tf_op jit(solution)/shard_map/ppermute | solution.py:312
  46.7 5.2 %collective-permute-start.13 = (bf16[2,6144]{1,0:T(2,128)(2,1)S(1)}, bf16[2,6144]{1,0:T(2,128)(2,1)S(1)}, u32[]{:S(2)}, u32[]{:S(2)}) collective-permute-start(bf16[2,6144]{1,0:T(2,128)(2,1)S(1)} %get-tuple-element.35), channel_id=1, source_target_pairs={{0,8},{4,12},{8,0},{12,4},{1,9},{5,13},{9,1},{13,5},{2,10},{6,14},... | collective-permute-start | bytes 73736 | tf_op jit(solution)/shard_map/ppermute | solution.py:312
  50.1 5.6 %collective-permute-start.14 = (bf16[2,6144]{1,0:T(2,128)(2,1)S(1)}, bf16[2,6144]{1,0:T(2,128)(2,1)S(1)}, u32[]{:S(2)}, u32[]{:S(2)}) collective-permute-start(bf16[2,6144]{1,0:T(2,128)(2,1)S(1)} %get-tuple-element.36), channel_id=1, source_target_pairs={{0,12},{4,8},{8,4},{12,0},{1,13},{5,9},{9,5},{13,1},{2,14},{6,10},... | collective-permute-start | bytes 73736 | tf_op jit(solution)/shard_map/ppermute | solution.py:312

commit v3 on v2

--- a/solution.py
+++ b/solution.py
@@ -39,14 +39,24 @@
     small = [
         pltpu.make_async_copy(hbm_refs[i], scratch[i], sem.at[i]) for i in range(n_in - 2)
     ]
-    loads_k = [
-        pltpu.make_async_copy(k_any.at[r], k_ref.at[r], cache_sems.at[0, r]) for r in range(rows)
-    ]
-    loads_v = [
-        pltpu.make_async_copy(v_any.at[r], v_ref.at[r], cache_sems.at[1, r]) for r in range(rows)
-    ]
-    for load in small + loads_k + loads_v:
+
+    def load_k(r):
+        return pltpu.make_async_copy(k_any.at[r], k_ref.at[r], cache_sems.at[0, r])
+
+    def load_v(r):
+        return pltpu.make_async_copy(v_any.at[r], v_ref.at[r], cache_sems.at[1, r])
+
+    for load in small:
         load.start()
+
+    @pl.loop(0, rows)
+    def _(r):
+        load_k(r).start()
+
+    @pl.loop(0, rows)
+    def _(r):
+        load_v(r).start()
+
     for load in small:
         load.wait()
 
@@ -88,8 +98,8 @@
         )
 
     scores = [None] * pairs
+    pl.loop(0, rows)(lambda r: load_k(r).wait())
     for r in range(rows):
-        loads_k[r].wait()
         for p in range(pairs):
             part = lax.dot_general(
                 lhs[p],
@@ -108,8 +118,8 @@
         probs.append((e_old * share).astype(jnp.bfloat16))
         own_probs.append((e_own * share).astype(jnp.bfloat16).astype(jnp.float32))
     sums = [None] * pairs
+    pl.loop(0, rows)(lambda r: load_v(r).wait())
     for r in range(rows):
-        loads_v[r].wait()
         for p in range(pairs):
             part = jnp.dot(
                 probs[p],
@@ -171,15 +181,15 @@
     mixing_ref[...] = mixing
 
 
-def load_kernel(w_ref, _, out_ref, sem):
-    load = pltpu.make_async_copy(w_ref.at[0], out_ref, sem)
+def load_kernel(first, w_any, _, out_ref, sem):
+    load = pltpu.make_async_copy(w_any.at[0, pl.ds(first, out_ref.shape[0])], out_ref, sem)
     load.start()
     load.wait()
 
 
-def stack_kernel(*refs):
+def stack_kernel(count, *refs):
     refs[-1][...] = jnp.concatenate(
-        [ref[...].astype(jnp.float32) for ref in refs[:-2]], axis=0
+        [ref[...].astype(jnp.float32) for ref in refs[:count][::-1]], axis=0
     ).astype(jnp.bfloat16)
 
 
@@ -189,7 +199,8 @@
     core_own_ref,
     core_rest_ref,
     gate_ref,
-    up_ref,
+    up_low_ref,
+    up_high_ref,
     down_any,
     keep_ref,
     send_ref,
@@ -199,40 +210,39 @@
     down_ref,
     sems,
 ):
-    loads = []
-    wide = down_ref.shape[1] // sems.shape[0]
-    for i in range(sems.shape[0]):
-        at = pl.ds(i * wide, wide)
-        loads.append(
-            pltpu.make_async_copy(down_any.at[0, :, at], down_ref.at[:, at], sems.at[i])
-        )
-        loads[-1].start()
+    chunks = sems.shape[0]
+    part = down_ref.shape[0] // chunks
+
+    def load(i):
+        at = pl.ds(i * part, part)
+        return pltpu.make_async_copy(down_any.at[0, at], down_ref.at[at], sems.at[i])
+
+    pl.loop(0, chunks)(lambda i: load(i).start())
     width = x_ref.shape[1]
     half = keep_ref.shape[0]
     x_ref[:half] = jnp.concatenate([own_ref[...], rest_ref[...]], axis=0)
     x_ref[half:] = jnp.concatenate([core_own_ref[...], core_rest_ref[...]], axis=0)
+    first = 0
+    for ref in (up_low_ref, up_high_ref):
+        tall = ref.shape[0] // 3
+        for i in range(3):
+            x = x_ref[:, first : first + tall]
+            at = pl.ds(i * tall, tall)
+            gate = jnp.dot(x, gate_ref[0, pl.ds(first, tall)], preferred_element_type=jnp.float32)
+            upper = jnp.dot(x, ref[at], preferred_element_type=jnp.float32)
+            gate_sum[...] = gate if first == 0 else gate_sum[...] + gate
+            up_sum[...] = upper if first == 0 else up_sum[...] + upper
+            first += tall
+    gate = gate_sum[...]
+    hidden = (gate / (1.0 + jnp.exp(-gate)) * up_sum[...]).astype(jnp.bfloat16)
+    pl.loop(0, chunks)(lambda i: load(i).wait())
     deep = 1024
     for step in range(width // deep):
         at = pl.ds(step * deep, deep)
-        x = x_ref[:, at]
-        gate = jnp.dot(x, gate_ref[at, :], preferred_element_type=jnp.float32)
-        upper = jnp.dot(x, up_ref[at, :], preferred_element_type=jnp.float32)
-        if step == 0:
-            gate_sum[...] = gate
-            up_sum[...] = upper
-        else:
-            gate_sum[...] += gate
-            up_sum[...] += upper
-    gate = gate_sum[...]
-    hidden = (gate / (1.0 + jnp.exp(-gate)) * up_sum[...]).astype(jnp.bfloat16)
-    for i, load in enumerate(loads):
-        load.wait()
-        for low in range(i * wide, (i + 1) * wide, deep):
-            at = pl.ds(low, deep)
-            piece = jnp.dot(hidden, down_ref[:, at], preferred_element_type=jnp.float32)
-            piece = piece.astype(jnp.bfloat16)
-            keep_ref[:, at] = piece[:half]
-            send_ref[:, at] = piece[half:]
+        piece = jnp.dot(hidden, down_ref[:, at], preferred_element_type=jnp.float32)
+        piece = piece.astype(jnp.bfloat16)
+        keep_ref[:, at] = piece[:half]
+        send_ref[:, at] = piece[half:]
 
 
 def chip_sum_kernel(keep_ref, got_ref, own_ref, *out_refs):
@@ -254,15 +264,16 @@
         ref[...] = total[j * most : (j + 1) * most]
 
 
-def finish_kernel(mixed_ref, mixing_ref, *refs):
+def finish_kernel(*refs):
+    *got, mixed_ref, mixing_ref, out_ref = refs
     total = mixed_ref[...]
-    most = refs[0].shape[0]
-    for j, ref in enumerate(refs[:-1]):
+    most = got[0].shape[0]
+    for j, ref in enumerate(got[::-1]):
         rows = ref[...].astype(jnp.float32)
         for s in range(most):
             at = j * most + s
             total = total + mixing_ref[:, at : at + 1] * rows[s : s + 1]
-    refs[-1][...] = total.astype(jnp.bfloat16)
+    out_ref[...] = total.astype(jnp.bfloat16)
 
 
 def call(kernel, outs, in_specs, *args, scratch=(), limit=8, cost=None):
@@ -314,6 +325,302 @@
     def to_plane(x, k):
         return lax.ppermute(x, plane, [(i, i ^ k) for i in range(n_side * n_cuts)])
 
+    hidden = w_gate.shape[2]
+
+    small = [
+        pltpu.make_async_copy(hbm_refs[i], scratch[i], sem.at[i]) for i in range(n_in - 2)
+    ]
+
+    def load_k(r):
+        return pltpu.make_async_copy(k_any.at[r], k_ref.at[r], cache_sems.at[0, r])
+
+    def load_v(r):
+        return pltpu.make_async_copy(v_any.at[r], v_ref.at[r], cache_sems.at[1, r])
+
+    for load in small:
+        load.start()
+
+    @pl.loop(0, rows)
+    def _(r):
+        load_k(r).start()
+
+    @pl.loop(0, rows)
+    def _(r):
+        load_v(r).start()
+
+    for load in small:
+        load.wait()
+
+    pair = 2
+    pairs = KV_HEADS // pair
+    stack = GROUP * rows
+    tall = pair * stack
+    wide = pair * HEAD_DIM
+    row_of = lax.broadcasted_iota(jnp.int32, (tall, 1), 0) % rows
+    length_of = jnp.zeros((tall, 1), jnp.int32)
+    for r in range(rows):
+        length_of = jnp.where(row_of == r, lengths[r], length_of)
+    live = lax.broadcasted_iota(jnp.int32, (tall, span), 1) < length_of
+
+    query = q_ref[...].astype(jnp.float32)
+    new_key = nk_ref[...].astype(jnp.float32)
+    new_value = nv_ref[...].astype(jnp.float32)
+    blank = jnp.zeros((stack, HEAD_DIM), jnp.float32)
+    lhs, own = [], []
+    for p in range(pairs):
+        heads = [stacked_heads(query, (pair * p + a) * GROUP) for a in range(pair)]
+        keys = [stacked_heads(new_key, pair * p + a, GROUP) for a in range(pair)]
+        lhs.append(
+            jnp.concatenate(
+                [
+                    jnp.concatenate([heads[b] if a == b else blank for b in range(pair)], axis=1)
+                    for a in range(pair)
+                ],
+                axis=0,
+            ).astype(jnp.bfloat16)
+        )
+        own.append(
+            jnp.sum(
+                jnp.concatenate(heads, axis=0) * jnp.concatenate(keys, axis=0),
+                axis=1,
+                keepdims=True,
+            )
+            * scale
+        )
+
+    scores = [None] * pairs
+    pl.loop(0, rows)(lambda r: load_k(r).wait())
+    for r in range(rows):
+        for p in range(pairs):
+            part = lax.dot_general(
+                lhs[p],
+                k_ref[r, :, p * wide : (p + 1) * wide],
+                (((1,), (1,)), ((), ())),
+                preferred_element_type=jnp.float32,
+            )
+            scores[p] = part if r == 0 else jnp.where(row_of == r, part, scores[p])
+    probs, own_probs = [], []
+    for p in range(pairs):
+        old = jnp.where(live, scores[p] * scale, -1e30)
+        top = jnp.maximum(jnp.max(old, axis=1, keepdims=True), own[p])
+        e_old = jnp.exp(old - top)
+        e_own = jnp.exp(own[p] - top)
+        share = 1.0 / (jnp.sum(e_old, axis=1, keepdims=True) + e_own)
+        probs.append((e_old * share).astype(jnp.bfloat16))
+        own_probs.append((e_own * share).astype(jnp.bfloat16).astype(jnp.float32))
+    sums = [None] * pairs
+    pl.loop(0, rows)(lambda r: load_v(r).wait())
+    for r in range(rows):
+        for p in range(pairs):
+            part = jnp.dot(
+                probs[p],
+                v_ref[r, :, p * wide : (p + 1) * wide],
+                preferred_element_type=jnp.float32,
+            )
+            sums[p] = part if r == 0 else jnp.where(row_of == r, part, sums[p])
+    power = jnp.zeros((rows, HEAD_DIM), jnp.float32)
+    for p in range(pairs):
+        for a in range(pair):
+            head = pair * p + a
+            fresh = stacked_heads(new_value, head, GROUP)
+            low = a * stack
+            attended = (
+                sums[p][low : low + stack, a * HEAD_DIM : (a + 1) * HEAD_DIM]
+                + own_probs[p][low : low + stack] * fresh
+            )
+            for j in range(GROUP):
+                at = pl.ds((head * GROUP + j) * HEAD_DIM, HEAD_DIM)
+                mixed = res_ref[:, at].astype(jnp.float32) + attended[j * rows : (j + 1) * rows]
+                mixed_ref[:, at] = mixed
+                power = power + mixed * mixed
+    mean = jnp.sum(power, axis=1, keepdims=True) * (1.0 / width)
+    normed = mixed_ref[...] * lax.rsqrt(mean + 1e-05) * gain_ref[...].astype(jnp.float32).reshape(1, width)
+    normed = normed.astype(jnp.bfloat16).astype(jnp.float32)
+
+    router = router_ref[...].astype(jnp.float32)
+    logits = [jnp.sum(normed * router[e : e + 1], axis=1, keepdims=True) for e in range(experts)]
+    row_col = lax.broadcasted_iota(jnp.int32, (rows, 1), 0)
+
+    def picked(i):
+        value = jnp.zeros((rows, 1), jnp.float32)
+        for r in range(rows):
+            for e in range(experts):
+                value = jnp.where((row_col == r) & (routes[i, r] == e), logits[e], value)
+        return value
+
+    first, second = picked(0), picked(1)
+    share_of = [1.0 / (1.0 + jnp.exp(second - first)), 1.0 / (1.0 + jnp.exp(first - second))]
+
+    here = lax.axis_index("grp")
+    named = [(r, i, routes[i, r]) for r in range(rows) for i in range(2)]
+    slots = []
+    for at, (r, i, e) in enumerate(named):
+        rank = jnp.int32(0)
+        for _, _, other in named[:at]:
+            rank = rank + (other == e).astype(jnp.int32)
+        slots.append(jnp.bitwise_xor(e, here) * most + rank)
+    slot_col = lax.broadcasted_iota(jnp.int32, (experts * most, 1), 0)
+    slot_row = lax.broadcasted_iota(jnp.int32, (rows, experts * most), 1)
+    outgoing = jnp.zeros((experts * most, width), jnp.float32)
+    mixing = jnp.zeros((rows, experts * most), jnp.float32)
+    for (r, i, _), slot in zip(named, slots, strict=True):
+        outgoing = jnp.where(slot_col == slot, normed[r : r + 1], outgoing)
+        mixing = jnp.where((slot_row == slot) & (row_col == r), share_of[i], mixing)
+    outgoing = outgoing.astype(jnp.bfloat16)
+    for j in range(experts):
+        out_refs[j][...] = outgoing[j * most : (j + 1) * most]
+    mixing_ref[...] = mixing
+
+
+def load_kernel(first, w_any, _, out_ref, sem):
+    load = pltpu.make_async_copy(w_any.at[0, pl.ds(first, out_ref.shape[0])], out_ref, sem)
+    load.start()
+    load.wait()
+
+
+def stack_kernel(count, *refs):
+    refs[-1][...] = jnp.concatenate(
+        [ref[...].astype(jnp.float32) for ref in refs[:count][::-1]], axis=0
+    ).astype(jnp.bfloat16)
+
+
+def experts_kernel(
+    own_ref,
+    rest_ref,
+    core_own_ref,
+    core_rest_ref,
+    gate_ref,
+    up_low_ref,
+    up_high_ref,
+    down_any,
+    keep_ref,
+    send_ref,
+    x_ref,
+    gate_sum,
+    up_sum,
+    down_ref,
+    sems,
+):
+    chunks = sems.shape[0]
+    part = down_ref.shape[0] // chunks
+
+    def load(i):
+        at = pl.ds(i * part, part)
+        return pltpu.make_async_copy(down_any.at[0, at], down_ref.at[at], sems.at[i])
+
+    pl.loop(0, chunks)(lambda i: load(i).start())
+    width = x_ref.shape[1]
+    half = keep_ref.shape[0]
+    x_ref[:half] = jnp.concatenate([own_ref[...], rest_ref[...]], axis=0)
+    x_ref[half:] = jnp.concatenate([core_own_ref[...], core_rest_ref[...]], axis=0)
+    first = 0
+    for ref in (up_low_ref, up_high_ref):
+        tall = ref.shape[0] // 3
+        for i in range(3):
+            x = x_ref[:, first : first + tall]
+            at = pl.ds(i * tall, tall)
+            gate = jnp.dot(x, gate_ref[0, pl.ds(first, tall)], preferred_element_type=jnp.float32)
+            upper = jnp.dot(x, ref[at], preferred_element_type=jnp.float32)
+            gate_sum[...] = gate if first == 0 else gate_sum[...] + gate
+            up_sum[...] = upper if first == 0 else up_sum[...] + upper
+            first += tall
+    gate = gate_sum[...]
+    hidden = (gate / (1.0 + jnp.exp(-gate)) * up_sum[...]).astype(jnp.bfloat16)
+    pl.loop(0, chunks)(lambda i: load(i).wait())
+    deep = 1024
+    for step in range(width // deep):
+        at = pl.ds(step * deep, deep)
+        piece = jnp.dot(hidden, down_ref[:, at], preferred_element_type=jnp.float32)
+        piece = piece.astype(jnp.bfloat16)
+        keep_ref[:, at] = piece[:half]
+        send_ref[:, at] = piece[half:]
+
+
+def chip_sum_kernel(keep_ref, got_ref, own_ref, *out_refs):
+    total = keep_ref[...].astype(jnp.float32) + got_ref[...].astype(jnp.float32)
+    part = own_ref.shape[0]
+    own_ref[...] = total[:part]
+    for i, ref in enumerate(out_refs):
+        ref[...] = total[(i + 1) * part : (i + 2) * part].astype(jnp.bfloat16)
+
+
+def plane_sum_kernel(got, own_ref, *refs):
+    total = own_ref[...]
+    for ref in refs[:got]:
+        total = total + ref[...].astype(jnp.float32)
+    total = total.astype(jnp.bfloat16)
+    outs = refs[got:]
+    most = outs[0].shape[0]
+    for j, ref in enumerate(outs):
+        ref[...] = total[j * most : (j + 1) * most]
+
+
+def finish_kernel(*refs):
+    *got, mixed_ref, mixing_ref, out_ref = refs
+    total = mixed_ref[...]
+    most = got[0].shape[0]
+    for j, ref in enumerate(got[::-1]):
+        rows = ref[...].astype(jnp.float32)
+        for s in range(most):
+            at = j * most + s
+            total = total + mixing_ref[:, at : at + 1] * rows[s : s + 1]
+    out_ref[...] = total.astype(jnp.bfloat16)
+
+
+def call(kernel, outs, in_specs, *args, scratch=(), limit=8, cost=None):
+    return pl.pallas_call(
+        kernel,
+        out_shape=outs,
+        in_specs=in_specs,
+        out_specs=jax.tree.map(lambda _: VMEM, outs),
+        scratch_shapes=list(scratch),
+        compiler_params=pltpu.CompilerParams(vmem_limit_bytes=limit * MIB),
+        cost_estimate=cost,
+    )(*args)
+
+
+def in_hbm(x):
+    return pltpu.with_memory_space_constraint(x, pltpu.HBM)
+
+
+def shape(extent, kind=jnp.bfloat16):
+    return jax.ShapeDtypeStruct(extent, kind)
+
+
+def local(
+    query,
+    k_cache,
+    v_cache,
+    new_key,
+    new_value,
+    lengths,
+    residual,
+    norm_gain,
+    router,
+    routes,
+    w_gate,
+    w_up,
+    w_down,
+):
+    rows, width = query.shape
+    experts = lax.axis_size("grp")
+    n_side = lax.axis_size("side")
+    n_cuts = lax.axis_size("cuts")
+    most = max(2, 2 * rows // experts)
+    slots = experts * most
+    plane = ("side", "cuts")
+
+    def to_grp(x, j):
+        return lax.ppermute(x, "grp", [(i, i ^ j) for i in range(experts)])
+
+    def to_plane(x, k):
+        return lax.ppermute(x, plane, [(i, i ^ k) for i in range(n_side * n_cuts)])
+
+    hidden = w_gate.shape[2]
+
+    def weight_piece(count):
+        return pltpu.VMEM((count * width // 8, hidden), jnp.bfloat16)
+
     small = [
         lengths,
         routes.T,
@@ -327,7 +634,10 @@
     *outgoing, mixed, mixing = call(
         functools.partial(attend_kernel, experts, most, len(small) + 2),
         [shape((most, width)) for _ in range(experts)]
-        + [shape((rows, width), jnp.float32), shape((rows, slots), jnp.float32)],
+        + [
+            shape((rows, width), jnp.float32),
+            shape((rows, slots), jnp.float32),
+        ],
         [HBM] * (len(small) + 2),
         *[in_hbm(x) for x in small],
         in_hbm(k_cache),
@@ -344,13 +654,13 @@
         limit=14,
     )
 
-    def load(weights, after):
-        extent = weights.shape[1:]
+    def load(first, after):
+        extent = (width // 2, w_up.shape[2])
         return call(
-            load_kernel,
+            functools.partial(load_kernel, first),
             pltpu.VMEM(extent, jnp.bfloat16),
             [HBM, ANY],
-            in_hbm(weights),
+            in_hbm(w_up),
             after,
             scratch=[pltpu.SemaphoreType.DMA],
             cost=pl.CostEstimate(
@@ -358,35 +668,47 @@
             ),
         )
 
-    gate = load(w_gate, mixing)
-    arrived = [outgoing[0]] + [to_grp(outgoing[j], j) for j in range(1, experts)]
-    block = call(stack_kernel, shape((slots, width)), [VMEM] * experts + [ANY], *arrived, gate)
-    upper = load(w_up, block)
+    up_low = load(0, mixing)
+    arrived = [to_grp(outgoing[j], j) for j in range(experts - 1, 0, -1)]
+    block = call(
+        functools.partial(stack_kernel, experts),
+        shape((slots, width)),
+        [VMEM] * experts + [ANY],
+        *arrived,
+        outgoing[0],
+        up_low,
+        cost=pl.CostEstimate(flops=0, bytes_accessed=16 * MIB, transcendentals=0),
+    )
+    up_high = load(width // 2, block)
     chips = range(0, n_side * n_cuts, 2)
     others = len(chips) - 1
-    fetched = [to_plane(block, k) for k in chips[1:]]
+    fetched = [to_plane(block, k) for k in chips[:0:-1]]
     rest = call(
-        stack_kernel, shape((others * slots, width)), [VMEM] * others + [ANY], *fetched, upper
+        functools.partial(stack_kernel, others),
+        shape((others * slots, width)),
+        [VMEM] * others + [ANY],
+        *fetched,
+        up_high,
     )
     parts = [block, rest, to_plane(block, 1), to_plane(rest, 1)]
     half = len(chips) * slots
-    hidden = w_gate.shape[2]
     keep, send = call(
         experts_kernel,
         [shape((half, width))] * 2,
-        [VMEM] * 6 + [HBM],
+        [VMEM] * 7 + [HBM],
         *parts,
-        gate,
-        upper,
+        w_gate,
+        up_low,
+        up_high,
         in_hbm(w_down),
         scratch=[
             pltpu.VMEM((2 * half, width), jnp.bfloat16),
             pltpu.VMEM((2 * half, hidden), jnp.float32),
             pltpu.VMEM((2 * half, hidden), jnp.float32),
             pltpu.VMEM((hidden, width), jnp.bfloat16),
-            pltpu.SemaphoreType.DMA((3,)),
+            pltpu.SemaphoreType.DMA((4,)),
         ],
-        limit=24,
+        limit=28,
     )
     got = to_plane(send, 1)
     own, *partial = call(
@@ -396,7 +718,7 @@
         keep,
         got,
     )
-    gathered = [to_plane(x, k) for x, k in zip(partial, chips[1:], strict=True)]
+    gathered = [to_plane(x, k) for x, k in zip(partial[::-1], chips[:0:-1], strict=True)]
     finished = call(
         functools.partial(plane_sum_kernel, len(gathered)),
         [shape((most, width)) for _ in range(experts)],
@@ -404,14 +726,15 @@
         own,
         *gathered,
     )
-    returned = [finished[0]] + [to_grp(finished[j], j) for j in range(1, experts)]
+    returned = [to_grp(finished[j], j) for j in range(experts - 1, 0, -1)]
     return call(
         finish_kernel,
         shape((rows, width)),
         [VMEM] * (2 + experts),
+        *returned,
+        finished[0],
         mixed,
         mixing,
-        *returned,
     )
 
 

time: 56.8 us -> 48.6 us (0.86)
  Pallas kernels: 25 us -> 17.4 us
  waiting for transfers between devices: 13.5 us -> 12.8 us
    pallas_call x9, Pallas kernels: 25 us -> 17.4 us  [call(): pl.pallas_call(kernel, out_shape=outs, in_specs=in_specs, out_specs=jax.t...]
    ppermute x6, waiting for transfers between devices: 5.64 us -> 4.12 us  [to_grp(): return lax.ppermute(x, 'grp', [(i, i ^ j) for i in range(experts)])]
    ppermute x9, waiting for transfers between devices: 7.85 us -> 8.69 us  [to_plane(): return lax.ppermute(x, plane, [(i, i ^ k) for i in range(n_side * n_cuts)])]
  transfers between devices with their start and end apart: 15 -> 15, of which waited for: 8 -> 9; matrix products, arithmetic and copies ran while one was open for 0% -> 0% of each run, Pallas kernels for 16% -> 12%
where the time goes in v3:
time: 48.6 us; the launch traced here: 48.4 us
  starting transfers between devices  18.1 us (37%)
  Pallas kernels  17.4 us (36%)
  waiting for transfers between devices  12.8 us (26%)
    pallas_call x9, Pallas kernels, call(): pl.pallas_call(kernel, out_shape=outs, in_specs=in_specs, out_specs=jax.t...  17.4 us
    ppermute x6, starting transfers between devices, to_grp(): return lax.ppermute(x, 'grp', [(i, i ^ j) for i in range(experts)])  10.2 us
    ppermute x9, waiting for transfers between devices, to_plane(): return lax.ppermute(x, plane, [(i, i ^ k) for i in range(n_side * n_cuts)])  8.69 us
    ppermute x9, starting transfers between devices, to_plane(): return lax.ppermute(x, plane, [(i, i ^ k) for i in range(n_side * n_cuts)])  7.87 us
    ppermute x6, waiting for transfers between devices, to_grp(): return lax.ppermute(x, 'grp', [(i, i ^ j) for i in range(experts)])  4.12 us
  transfers between devices with their start and end apart: 15, of which 9 were waited for; matrix products, arithmetic and copies ran while one was open for 0% of the time, Pallas kernels for 12%

profile of v3, /device:TPU:0, one launch (start us, length us, event | category | flops | bytes accessed | tf_op | source)
XLA Modules:
  0.0 48.4 jit_solution(2920218408142129209)
XLA Ops:
  0.0 3.7 %shard_map.127 = (bf16[2,6144]{1,0:T(2,128)(2,1)S(1)}, bf16[2,6144]{1,0:T(2,128)(2,1)S(1)}, bf16[2,6144]{1,0:T(2,128)(2,1)S(1)}, bf16[2,6144]{1,0:T(2,128)(2,1)S...) custom-call(s32[4]{0:T(128)} %refs_0_.1, s32[2,4]{1,0:T(2,128)} %bitcast.5, bf16[4,6144]{1,0:T(4,128)(2,1)} %refs_2_.1, ...), custom_call_target="tpu_custom_call" | custom-call | tf_op jit(solution)/shard_map/pallas_call | solution.py:571
  3.7 5.1 %collective-permute-start = (bf16[2,6144]{1,0:T(2,128)(2,1)S(1)}, bf16[2,6144]{1,0:T(2,128)(2,1)S(1)}, u32[]{:S(2)}, u32[]{:S(2)}) collective-permute-start(bf16[2,6144]{1,0:T(2,128)(2,1)S(1)} %get-tuple-element.21), channel_id=1, source_target_pairs={{0,12},{4,8},{8,4},{12,0},{1,13},{5,9},{9,5},{13,1},{2,14},{6,10},... | collective-permute-start | bytes 73736 | tf_op jit(solution)/shard_map/ppermute | solution.py:614
  8.9 0.0 collective-permute-start.1
  8.9 0.6 %collective-permute-start.2 = (bf16[2,6144]{1,0:T(2,128)(2,1)S(1)}, bf16[2,6144]{1,0:T(2,128)(2,1)S(1)}, u32[]{:S(2)}, u32[]{:S(2)}) collective-permute-start(bf16[2,6144]{1,0:T(2,128)(2,1)S(1)} %get-tuple-element.23), channel_id=1, source_target_pairs={{0,4},{4,0},{8,12},{12,8},{1,5},{5,1},{9,13},{13,9},{2,6},{6,2},{1... | collective-permute-start | bytes 73736 | tf_op jit(solution)/shard_map/ppermute | solution.py:614
  9.5 2.8 %shard_map.128.refs_4_.up_low_ref = bf16[3072,1024]{1,0:T(8,128)(2,1)S(1)} custom-call(bf16[1,6144,1024]{2,1,0:T(8,128)(2,1)} %w_any.3, f32[4,8]{1,0:T(4,128)S(1)} %get-tuple-element.25._.refs_5_), custom_call_target="tpu_custom_call" | custom-call | bytes 6291456 | tf_op jit(solution)/shard_map/pallas_call | solution.py:571
  12.3 0.0 collective-permute-done.refs_0_
  12.3 1.3 %collective-permute-done.1.refs_1_ = bf16[2,6144]{1,0:T(2,128)(2,1)S(1)} collective-permute-done((bf16[2,6144]{1,0:T(2,128)(2,1)S(1)}, bf16[2,6144]{1,0:T(2,128)(2,1)S(1)}, u32[]{:S(2)}, u32[]{:S(2)}) %collective-permute-start.1) | collective-permute-done | bytes 24608 | tf_op jit(solution)/shard_map/ppermute | solution.py:614
  13.6 0.0 collective-permute-done.2.refs_2_
  13.6 0.0 slice-start
  13.6 0.1 shard_map.129._.own_ref
  13.7 0.0 slice-start.1
  13.7 0.0 slice-start.2
  13.7 1.6 %collective-permute-start.5 = (bf16[8,6144]{1,0:T(8,128)(2,1)S(1)}, bf16[8,6144]{1,0:T(8,128)(2,1)S(1)}, u32[]{:S(2)}, u32[]{:S(2)}) collective-permute-start(bf16[8,6144]{1,0:T(8,128)(2,1)S(1)} %shard_map.129._.own_ref), channel_id=1, source_target_pairs={{0,2},{1,3},{2,0},{3,1},{16,18},{17,19},{18,16},{19,17},{4,6},{5,7... | collective-permute-start | bytes 294920 | tf_op jit(solution)/shard_map/ppermute | solution.py:617
  15.2 1.5 %collective-permute-start.4 = (bf16[8,6144]{1,0:T(8,128)(2,1)S(1)}, bf16[8,6144]{1,0:T(8,128)(2,1)S(1)}, u32[]{:S(2)}, u32[]{:S(2)}) collective-permute-start(bf16[8,6144]{1,0:T(8,128)(2,1)S(1)} %shard_map.129._.own_ref), channel_id=1, source_target_pairs={{0,16},{1,17},{2,18},{3,19},{16,0},{17,1},{18,2},{19,3},{4,20},{5,... | collective-permute-start | bytes 294920 | tf_op jit(solution)/shard_map/ppermute | solution.py:617
  16.8 0.5 collective-permute-start.3
  17.2 2.8 %shard_map.130.refs_3_.up_high_ref = bf16[3072,1024]{1,0:T(8,128)(2,1)S(1)} custom-call(bf16[1,6144,1024]{2,1,0:T(8,128)(2,1)} %w_any.3, bf16[8,6144]{1,0:T(8,128)(2,1)S(1)} %shard_map.129._.own_ref), custom_call_target="tpu_custom_call" | custom-call | bytes 6291456 | tf_op jit(solution)/shard_map/pallas_call | solution.py:571
  20.0 0.0 collective-permute-done.5.refs_2_
  20.0 0.4 collective-permute-done.4.refs_1_
  20.5 1.8 %collective-permute-done.3.refs_0_ = bf16[8,6144]{1,0:T(8,128)(2,1)S(1)} collective-permute-done((bf16[8,6144]{1,0:T(8,128)(2,1)S(1)}, bf16[8,6144]{1,0:T(8,128)(2,1)S(1)}, u32[]{:S(2)}, u32[]{:S(2)}) %collective-permute-start.3) | collective-permute-done | bytes 98336 | tf_op jit(solution)/shard_map/ppermute | solution.py:617
  22.3 0.1 collective-permute-start.7
  22.4 0.5 %collective-permute-start.6 = (bf16[8,6144]{1,0:T(8,128)(2,1)S(1)}, bf16[8,6144]{1,0:T(8,128)(2,1)S(1)}, u32[]{:S(2)}, u32[]{:S(2)}) collective-permute-start(bf16[8,6144]{1,0:T(8,128)(2,1)S(1)} %shard_map.129._.own_ref), channel_id=1, source_target_pairs={{0,1},{1,0},{2,3},{3,2},{16,17},{17,16},{18,19},{19,18},{4,5},{5,4... | collective-permute-start | bytes 294920 | tf_op jit(solution)/shard_map/ppermute | solution.py:617
  22.9 1.2 %collective-permute-done.6.core_own_ref = bf16[8,6144]{1,0:T(8,128)(2,1)S(1)} collective-permute-done((bf16[8,6144]{1,0:T(8,128)(2,1)S(1)}, bf16[8,6144]{1,0:T(8,128)(2,1)S(1)}, u32[]{:S(2)}, u32[]{:S(2)}) %collective-permute-start.6) | collective-permute-done | bytes 98336 | tf_op jit(solution)/shard_map/ppermute | solution.py:617
  24.1 0.0 collective-permute-done.7.core_rest_ref
  24.1 0.0 slice-done
  24.1 0.0 slice-done.1
  24.1 0.0 slice-done.2
  24.1 7.0 %shard_map.132 = (bf16[32,6144]{1,0:T(8,128)(2,1)S(1)}, bf16[32,6144]{1,0:T(8,128)(2,1)S(1)}) custom-call(bf16[8,6144]{1,0:T(8,128)(2,1)S(1)} %shard_map.129._.own_ref, bf16[24,6144]{1,0:T(8,128)(2,1)S(1)} %shard_map.131.rest_ref, bf16[8,6144]{1,0:T(8,128)(2,1)S(1)} %collective-permute-done.6.core_own_ref, ...), custom_call_target="tpu_custom_call" | custom-call | tf_op jit(solution)/shard_map/pallas_call | solution.py:571
  31.1 0.2 collective-permute-start.8
  31.3 1.6 %collective-permute-done.8.got_ref = bf16[32,6144]{1,0:T(8,128)(2,1)S(1)} collective-permute-done((bf16[32,6144]{1,0:T(8,128)(2,1)S(1)}, bf16[32,6144]{1,0:T(8,128)(2,1)S(1)}, u32[]{:S(2)}, u32[]{:S(2)}) %collective-permute-start.8) | collective-permute-done | bytes 393248 | tf_op jit(solution)/shard_map/ppermute | solution.py:617
  32.9 0.1 shard_map.133
  33.0 0.5 %collective-permute-start.9 = (bf16[8,6144]{1,0:T(8,128)(2,1)S(1)}, bf16[8,6144]{1,0:T(8,128)(2,1)S(1)}, u32[]{:S(2)}, u32[]{:S(2)}) collective-permute-start(bf16[8,6144]{1,0:T(8,128)(2,1)S(1)} %get-tuple-element.29), channel_id=1, source_target_pairs={{0,18},{1,19},{2,16},{3,17},{16,2},{17,3},{18,0},{19,1},{4,22},{5,... | collective-permute-start | bytes 294920 | tf_op jit(solution)/shard_map/ppermute | solution.py:617
  33.5 1.5 %collective-permute-start.10 = (bf16[8,6144]{1,0:T(8,128)(2,1)S(1)}, bf16[8,6144]{1,0:T(8,128)(2,1)S(1)}, u32[]{:S(2)}, u32[]{:S(2)}) collective-permute-start(bf16[8,6144]{1,0:T(8,128)(2,1)S(1)} %get-tuple-element.30), channel_id=1, source_target_pairs={{0,16},{1,17},{2,18},{3,19},{16,0},{17,1},{18,2},{19,3},{4,20},{5,... | collective-permute-start | bytes 294920 | tf_op jit(solution)/shard_map/ppermute | solution.py:617
  35.0 1.5 %collective-permute-start.11 = (bf16[8,6144]{1,0:T(8,128)(2,1)S(1)}, bf16[8,6144]{1,0:T(8,128)(2,1)S(1)}, u32[]{:S(2)}, u32[]{:S(2)}) collective-permute-start(bf16[8,6144]{1,0:T(8,128)(2,1)S(1)} %get-tuple-element.31), channel_id=1, source_target_pairs={{0,2},{1,3},{2,0},{3,1},{16,18},{17,19},{18,16},{19,17},{4,6},{5,7... | collective-permute-start | bytes 294920 | tf_op jit(solution)/shard_map/ppermute | solution.py:617
  36.5 3.1 %collective-permute-done.9.refs_0_ = bf16[8,6144]{1,0:T(8,128)(2,1)S(1)} collective-permute-done((bf16[8,6144]{1,0:T(8,128)(2,1)S(1)}, bf16[8,6144]{1,0:T(8,128)(2,1)S(1)}, u32[]{:S(2)}, u32[]{:S(2)}) %collective-permute-start.9) | collective-permute-done | bytes 98336 | tf_op jit(solution)/shard_map/ppermute | solution.py:617
  39.6 0.6 %collective-permute-done.10.refs_1_ = bf16[8,6144]{1,0:T(8,128)(2,1)S(1)} collective-permute-done((bf16[8,6144]{1,0:T(8,128)(2,1)S(1)}, bf16[8,6144]{1,0:T(8,128)(2,1)S(1)}, u32[]{:S(2)}, u32[]{:S(2)}) %collective-permute-start.10) | collective-permute-done | bytes 98336 | tf_op jit(solution)/shard_map/ppermute | solution.py:617
  40.2 0.0 collective-permute-done.11.refs_2_
  40.2 0.1 shard_map.134
  40.2 2.6 %collective-permute-start.12 = (bf16[2,6144]{1,0:T(2,128)(2,1)S(1)}, bf16[2,6144]{1,0:T(2,128)(2,1)S(1)}, u32[]{:S(2)}, u32[]{:S(2)}) collective-permute-start(bf16[2,6144]{1,0:T(2,128)(2,1)S(1)} %get-tuple-element.32), channel_id=1, source_target_pairs={{0,12},{4,8},{8,4},{12,0},{1,13},{5,9},{9,5},{13,1},{2,14},{6,10},... | collective-permute-start | bytes 73736 | tf_op jit(solution)/shard_map/ppermute | solution.py:614
  42.8 0.0 collective-permute-start.13
  42.8 1.9 %collective-permute-start.14 = (bf16[2,6144]{1,0:T(2,128)(2,1)S(1)}, bf16[2,6144]{1,0:T(2,128)(2,1)S(1)}, u32[]{:S(2)}, u32[]{:S(2)}) collective-permute-start(bf16[2,6144]{1,0:T(2,128)(2,1)S(1)} %get-tuple-element.34), channel_id=1, source_target_pairs={{0,4},{4,0},{8,12},{12,8},{1,5},{5,1},{9,13},{13,9},{2,6},{6,2},{1... | collective-permute-start | bytes 73736 | tf_op jit(solution)/shard_map/ppermute | solution.py:614
  44.7 1.2 %collective-permute-done.12.refs_0_ = bf16[2,6144]{1,0:T(2,128)(2,1)S(1)} collective-permute-done((bf16[2,6144]{1,0:T(2,128)(2,1)S(1)}, bf16[2,6144]{1,0:T(2,128)(2,1)S(1)}, u32[]{:S(2)}, u32[]{:S(2)}) %collective-permute-start.12) | collective-permute-done | bytes 24608 | tf_op jit(solution)/shard_map/ppermute | solution.py:614
  45.9 1.6 %collective-permute-done.13.refs_1_ = bf16[2,6144]{1,0:T(2,128)(2,1)S(1)} collective-permute-done((bf16[2,6144]{1,0:T(2,128)(2,1)S(1)}, bf16[2,6144]{1,0:T(2,128)(2,1)S(1)}, u32[]{:S(2)}, u32[]{:S(2)}) %collective-permute-start.13) | collective-permute-done | bytes 24608 | tf_op jit(solution)/shard_map/ppermute | solution.py:614
  47.5 0.0 collective-permute-done.14.refs_2_
  47.5 0.9 %shard_map.135 = bf16[4,6144]{1,0:T(4,128)(2,1)} custom-call(bf16[2,6144]{1,0:T(2,128)(2,1)S(1)} %collective-permute-done.12.refs_0_, bf16[2,6144]{1,0:T(2,128)(2,1)S(1)} %collective-permute-done.13.refs_1_, bf16[2,6144]{1,0:T(2,128)(2,1)S(1)} %collective-permute-done.14.refs_2_, bf16[2,6144]{1,0:T(2,128)(2,1)S(1)} %get-tuple-element.35.refs_3_, ...), custom_call_target="tpu_custom_call" | custom-call | tf_op jit(solution)/shard_map/pallas_call | solution.py:571
  (2 shorter events, 0.0 us)
Async XLA Ops:
  3.7 8.6 %collective-permute-start = (bf16[2,6144]{1,0:T(2,128)(2,1)S(1)}, bf16[2,6144]{1,0:T(2,128)(2,1)S(1)}, u32[]{:S(2)}, u32[]{:S(2)}) collective-permute-start(bf16[2,6144]{1,0:T(2,128)(2,1)S(1)} %get-tuple-element.21), channel_id=1, source_target_pairs={{0,12},{4,8},{8,4},{12,0},{1,13},{5,9},{9,5},{13,1},{2,14},{6,10},... | collective-permute-start | bytes 73736 | tf_op jit(solution)/shard_map/ppermute | solution.py:614
  8.9 4.7 %collective-permute-start.1 = (bf16[2,6144]{1,0:T(2,128)(2,1)S(1)}, bf16[2,6144]{1,0:T(2,128)(2,1)S(1)}, u32[]{:S(2)}, u32[]{:S(2)}) collective-permute-start(bf16[2,6144]{1,0:T(2,128)(2,1)S(1)} %get-tuple-element.22), channel_id=1, source_target_pairs={{0,8},{4,12},{8,0},{12,4},{1,9},{5,13},{9,1},{13,5},{2,10},{6,14},... | collective-permute-start | bytes 73736 | tf_op jit(solution)/shard_map/ppermute | solution.py:614
  8.9 4.7 %collective-permute-start.2 = (bf16[2,6144]{1,0:T(2,128)(2,1)S(1)}, bf16[2,6144]{1,0:T(2,128)(2,1)S(1)}, u32[]{:S(2)}, u32[]{:S(2)}) collective-permute-start(bf16[2,6144]{1,0:T(2,128)(2,1)S(1)} %get-tuple-element.23), channel_id=1, source_target_pairs={{0,4},{4,0},{8,12},{12,8},{1,5},{5,1},{9,13},{13,9},{2,6},{6,2},{1... | collective-permute-start | bytes 73736 | tf_op jit(solution)/shard_map/ppermute | solution.py:614
  13.6 10.5 %slice-start = ((s8[12582912]{0:T(1024)(128)(4,1)}), s8[4194304]{0:T(1024)(128)(4,1)S(1)}, s32[]{:S(2)}) async-start(s8[12582912]{0:T(1024)(128)(4,1)} %bitcast.2), calls=%async_computation | async-start | bytes 8388608
  13.7 10.4 %slice-start.1 = ((s8[12582912]{0:T(1024)(128)(4,1)}), s8[4194304]{0:T(1024)(128)(4,1)S(1)}, s32[]{:S(2)}) async-start(s8[12582912]{0:T(1024)(128)(4,1)} %bitcast.2), calls=%async_computation.1 | async-start | bytes 8388608
  13.7 10.4 %slice-start.2 = ((s8[12582912]{0:T(1024)(128)(4,1)}), s8[4194304]{0:T(1024)(128)(4,1)S(1)}, s32[]{:S(2)}) async-start(s8[12582912]{0:T(1024)(128)(4,1)} %bitcast.2), calls=%async_computation.2 | async-start | bytes 8388608
  13.7 6.4 %collective-permute-start.5 = (bf16[8,6144]{1,0:T(8,128)(2,1)S(1)}, bf16[8,6144]{1,0:T(8,128)(2,1)S(1)}, u32[]{:S(2)}, u32[]{:S(2)}) collective-permute-start(bf16[8,6144]{1,0:T(8,128)(2,1)S(1)} %shard_map.129._.own_ref), channel_id=1, source_target_pairs={{0,2},{1,3},{2,0},{3,1},{16,18},{17,19},{18,16},{19,17},{4,6},{5,7... | collective-permute-start | bytes 294920 | tf_op jit(solution)/shard_map/ppermute | solution.py:617
  15.2 5.2 %collective-permute-start.4 = (bf16[8,6144]{1,0:T(8,128)(2,1)S(1)}, bf16[8,6144]{1,0:T(8,128)(2,1)S(1)}, u32[]{:S(2)}, u32[]{:S(2)}) collective-permute-start(bf16[8,6144]{1,0:T(8,128)(2,1)S(1)} %shard_map.129._.own_ref), channel_id=1, source_target_pairs={{0,16},{1,17},{2,18},{3,19},{16,0},{17,1},{18,2},{19,3},{4,20},{5,... | collective-permute-start | bytes 294920 | tf_op jit(solution)/shard_map/ppermute | solution.py:617
  16.8 5.5 %collective-permute-start.3 = (bf16[8,6144]{1,0:T(8,128)(2,1)S(1)}, bf16[8,6144]{1,0:T(8,128)(2,1)S(1)}, u32[]{:S(2)}, u32[]{:S(2)}) collective-permute-start(bf16[8,6144]{1,0:T(8,128)(2,1)S(1)} %shard_map.129._.own_ref), channel_id=1, source_target_pairs={{0,18},{1,19},{2,16},{3,17},{16,2},{17,3},{18,0},{19,1},{4,22},{5,... | collective-permute-start | bytes 294920 | tf_op jit(solution)/shard_map/ppermute | solution.py:617
  22.3 1.8 %collective-permute-start.7 = (bf16[24,6144]{1,0:T(8,128)(2,1)S(1)}, bf16[24,6144]{1,0:T(8,128)(2,1)S(1)}, u32[]{:S(2)}, u32[]{:S(2)}) collective-permute-start(bf16[24,6144]{1,0:T(8,128)(2,1)S(1)} %shard_map.131.rest_ref), channel_id=1, source_target_pairs={{0,1},{1,0},{2,3},{3,2},{16,17},{17,16},{18,19},{19,18},{4,5},{5,4... | collective-permute-start | bytes 884744 | tf_op jit(solution)/shard_map/ppermute | solution.py:617
  22.4 1.7 %collective-permute-start.6 = (bf16[8,6144]{1,0:T(8,128)(2,1)S(1)}, bf16[8,6144]{1,0:T(8,128)(2,1)S(1)}, u32[]{:S(2)}, u32[]{:S(2)}) collective-permute-start(bf16[8,6144]{1,0:T(8,128)(2,1)S(1)} %shard_map.129._.own_ref), channel_id=1, source_target_pairs={{0,1},{1,0},{2,3},{3,2},{16,17},{17,16},{18,19},{19,18},{4,5},{5,4... | collective-permute-start | bytes 294920 | tf_op jit(solution)/shard_map/ppermute | solution.py:617
  31.1 1.8 %collective-permute-start.8 = (bf16[32,6144]{1,0:T(8,128)(2,1)S(1)}, bf16[32,6144]{1,0:T(8,128)(2,1)S(1)}, u32[]{:S(2)}, u32[]{:S(2)}) collective-permute-start(bf16[32,6144]{1,0:T(8,128)(2,1)S(1)} %get-tuple-element.27), channel_id=1, source_target_pairs={{0,1},{1,0},{2,3},{3,2},{16,17},{17,16},{18,19},{19,18},{4,5},{5,4... | collective-permute-start | bytes 1179656 | tf_op jit(solution)/shard_map/ppermute | solution.py:617
  33.0 6.6 %collective-permute-start.9 = (bf16[8,6144]{1,0:T(8,128)(2,1)S(1)}, bf16[8,6144]{1,0:T(8,128)(2,1)S(1)}, u32[]{:S(2)}, u32[]{:S(2)}) collective-permute-start(bf16[8,6144]{1,0:T(8,128)(2,1)S(1)} %get-tuple-element.29), channel_id=1, source_target_pairs={{0,18},{1,19},{2,16},{3,17},{16,2},{17,3},{18,0},{19,1},{4,22},{5,... | collective-permute-start | bytes 294920 | tf_op jit(solution)/shard_map/ppermute | solution.py:617
  33.5 6.7 %collective-permute-start.10 = (bf16[8,6144]{1,0:T(8,128)(2,1)S(1)}, bf16[8,6144]{1,0:T(8,128)(2,1)S(1)}, u32[]{:S(2)}, u32[]{:S(2)}) collective-permute-start(bf16[8,6144]{1,0:T(8,128)(2,1)S(1)} %get-tuple-element.30), channel_id=1, source_target_pairs={{0,16},{1,17},{2,18},{3,19},{16,0},{17,1},{18,2},{19,3},{4,20},{5,... | collective-permute-start | bytes 294920 | tf_op jit(solution)/shard_map/ppermute | solution.py:617
  35.0 5.1 %collective-permute-start.11 = (bf16[8,6144]{1,0:T(8,128)(2,1)S(1)}, bf16[8,6144]{1,0:T(8,128)(2,1)S(1)}, u32[]{:S(2)}, u32[]{:S(2)}) collective-permute-start(bf16[8,6144]{1,0:T(8,128)(2,1)S(1)} %get-tuple-element.31), channel_id=1, source_target_pairs={{0,2},{1,3},{2,0},{3,1},{16,18},{17,19},{18,16},{19,17},{4,6},{5,7... | collective-permute-start | bytes 294920 | tf_op jit(solution)/shard_map/ppermute | solution.py:617
  40.2 5.7 %collective-permute-start.12 = (bf16[2,6144]{1,0:T(2,128)(2,1)S(1)}, bf16[2,6144]{1,0:T(2,128)(2,1)S(1)}, u32[]{:S(2)}, u32[]{:S(2)}) collective-permute-start(bf16[2,6144]{1,0:T(2,128)(2,1)S(1)} %get-tuple-element.32), channel_id=1, source_target_pairs={{0,12},{4,8},{8,4},{12,0},{1,13},{5,9},{9,5},{13,1},{2,14},{6,10},... | collective-permute-start | bytes 73736 | tf_op jit(solution)/shard_map/ppermute | solution.py:614
  42.8 4.7 %collective-permute-start.13 = (bf16[2,6144]{1,0:T(2,128)(2,1)S(1)}, bf16[2,6144]{1,0:T(2,128)(2,1)S(1)}, u32[]{:S(2)}, u32[]{:S(2)}) collective-permute-start(bf16[2,6144]{1,0:T(2,128)(2,1)S(1)} %get-tuple-element.33), channel_id=1, source_target_pairs={{0,8},{4,12},{8,0},{12,4},{1,9},{5,13},{9,1},{13,5},{2,10},{6,14},... | collective-permute-start | bytes 73736 | tf_op jit(solution)/shard_map/ppermute | solution.py:614
  42.8 4.7 %collective-permute-start.14 = (bf16[2,6144]{1,0:T(2,128)(2,1)S(1)}, bf16[2,6144]{1,0:T(2,128)(2,1)S(1)}, u32[]{:S(2)}, u32[]{:S(2)}) collective-permute-start(bf16[2,6144]{1,0:T(2,128)(2,1)S(1)} %get-tuple-element.34), channel_id=1, source_target_pairs={{0,4},{4,0},{8,12},{12,8},{1,5},{5,1},{9,13},{13,9},{2,6},{6,2},{1... | collective-permute-start | bytes 73736 | tf_op jit(solution)/shard_map/ppermute | solution.py:614

commit v4 on v2

--- a/solution.py
+++ b/solution.py
@@ -27,26 +27,36 @@
 def attend_kernel(experts, most, n_in, *refs):
     hbm_refs = refs[:n_in]
     out_refs = refs[n_in : n_in + experts]
-    mixed_ref, mixing_ref = refs[n_in + experts : n_in + experts + 2]
+    mixed_ref, normed_ref = refs[n_in + experts : n_in + experts + 2]
     scratch = refs[n_in + experts + 2 : -2]
     sem, cache_sems = refs[-2:]
     k_any, v_any = hbm_refs[-2:]
     k_ref, v_ref = scratch[-2:]
-    lengths, routes, q_ref, nk_ref, nv_ref, res_ref, gain_ref, router_ref = scratch[:-2]
+    lengths, routes, q_ref, nk_ref, nv_ref, res_ref, gain_ref = scratch[:-2]
     rows, width = q_ref.shape
     span = k_ref.shape[1]
     scale = 1.0 / math.sqrt(HEAD_DIM)
     small = [
         pltpu.make_async_copy(hbm_refs[i], scratch[i], sem.at[i]) for i in range(n_in - 2)
     ]
-    loads_k = [
-        pltpu.make_async_copy(k_any.at[r], k_ref.at[r], cache_sems.at[0, r]) for r in range(rows)
-    ]
-    loads_v = [
-        pltpu.make_async_copy(v_any.at[r], v_ref.at[r], cache_sems.at[1, r]) for r in range(rows)
-    ]
-    for load in small + loads_k + loads_v:
+
+    def load_k(r):
+        return pltpu.make_async_copy(k_any.at[r], k_ref.at[r], cache_sems.at[0, r])
+
+    def load_v(r):
+        return pltpu.make_async_copy(v_any.at[r], v_ref.at[r], cache_sems.at[1, r])
+
+    for load in small:
         load.start()
+
+    @pl.loop(0, rows)
+    def _(r):
+        load_k(r).start()
+
+    @pl.loop(0, rows)
+    def _(r):
+        load_v(r).start()
+
     for load in small:
         load.wait()
 
@@ -88,8 +98,8 @@
         )
 
     scores = [None] * pairs
+    pl.loop(0, rows)(lambda r: load_k(r).wait())
     for r in range(rows):
-        loads_k[r].wait()
         for p in range(pairs):
             part = lax.dot_general(
                 lhs[p],
@@ -108,8 +118,8 @@
         probs.append((e_old * share).astype(jnp.bfloat16))
         own_probs.append((e_own * share).astype(jnp.bfloat16).astype(jnp.float32))
     sums = [None] * pairs
+    pl.loop(0, rows)(lambda r: load_v(r).wait())
     for r in range(rows):
-        loads_v[r].wait()
         for p in range(pairs):
             part = jnp.dot(
                 probs[p],
@@ -133,9 +143,34 @@
                 mixed_ref[:, at] = mixed
                 power = power + mixed * mixed
     mean = jnp.sum(power, axis=1, keepdims=True) * (1.0 / width)
-    normed = mixed_ref[...] * lax.rsqrt(mean + 1e-05) * gain_ref[...].astype(jnp.float32).reshape(1, width)
-    normed = normed.astype(jnp.bfloat16).astype(jnp.float32)
-
+    gain = gain_ref[...].astype(jnp.float32).reshape(1, width)
+    normed = (mixed_ref[...] * lax.rsqrt(mean + 1e-05) * gain).astype(jnp.bfloat16)
+    normed_ref[...] = normed
+    normed = normed.astype(jnp.float32)
+    slot_col = lax.broadcasted_iota(jnp.int32, (experts * most, 1), 0)
+    outgoing = jnp.zeros((experts * most, width), jnp.float32)
+    for r, _, slot in slots_of(routes, rows, most):
+        outgoing = jnp.where(slot_col == slot, normed[r : r + 1], outgoing)
+    outgoing = outgoing.astype(jnp.bfloat16)
+    for j in range(experts):
+        out_refs[j][...] = outgoing[j * most : (j + 1) * most]
+
+
+def slots_of(routes, rows, most):
+    here = lax.axis_index("grp")
+    named = [(r, i, routes[i, r]) for r in range(rows) for i in range(2)]
+    placed = []
+    for at, (r, i, e) in enumerate(named):
+        rank = jnp.int32(0)
+        for _, _, other in named[:at]:
+            rank = rank + (other == e).astype(jnp.int32)
+        placed.append((r, i, jnp.bitwise_xor(e, here) * most + rank))
+    return placed
+
+
+def mixing_kernel(experts, most, routes, normed_ref, router_ref, mixing_ref):
+    rows = normed_ref.shape[0]
+    normed = normed_ref[...].astype(jnp.float32)
     router = router_ref[...].astype(jnp.float32)
     logits = [jnp.sum(normed * router[e : e + 1], axis=1, keepdims=True) for e in range(experts)]
     row_col = lax.broadcasted_iota(jnp.int32, (rows, 1), 0)
@@ -149,37 +184,22 @@
 
     first, second = picked(0), picked(1)
     share_of = [1.0 / (1.0 + jnp.exp(second - first)), 1.0 / (1.0 + jnp.exp(first - second))]
-
-    here = lax.axis_index("grp")
-    named = [(r, i, routes[i, r]) for r in range(rows) for i in range(2)]
-    slots = []
-    for at, (r, i, e) in enumerate(named):
-        rank = jnp.int32(0)
-        for _, _, other in named[:at]:
-            rank = rank + (other == e).astype(jnp.int32)
-        slots.append(jnp.bitwise_xor(e, here) * most + rank)
-    slot_col = lax.broadcasted_iota(jnp.int32, (experts * most, 1), 0)
     slot_row = lax.broadcasted_iota(jnp.int32, (rows, experts * most), 1)
-    outgoing = jnp.zeros((experts * most, width), jnp.float32)
     mixing = jnp.zeros((rows, experts * most), jnp.float32)
-    for (r, i, _), slot in zip(named, slots, strict=True):
-        outgoing = jnp.where(slot_col == slot, normed[r : r + 1], outgoing)
+    for r, i, slot in slots_of(routes, rows, most):
         mixing = jnp.where((slot_row == slot) & (row_col == r), share_of[i], mixing)
-    outgoing = outgoing.astype(jnp.bfloat16)
-    for j in range(experts):
-        out_refs[j][...] = outgoing[j * most : (j + 1) * most]
     mixing_ref[...] = mixing
 
 
-def load_kernel(w_ref, _, out_ref, sem):
-    load = pltpu.make_async_copy(w_ref.at[0], out_ref, sem)
+def load_kernel(first, w_any, _, out_ref, sem):
+    load = pltpu.make_async_copy(w_any.at[0, pl.ds(first, out_ref.shape[0])], out_ref, sem)
     load.start()
     load.wait()
 
 
-def stack_kernel(*refs):
+def stack_kernel(count, *refs):
     refs[-1][...] = jnp.concatenate(
-        [ref[...].astype(jnp.float32) for ref in refs[:-2]], axis=0
+        [ref[...].astype(jnp.float32) for ref in refs[:count]], axis=0
     ).astype(jnp.bfloat16)
 
 
@@ -189,80 +209,73 @@
     core_own_ref,
     core_rest_ref,
     gate_ref,
-    up_ref,
+    up_low_ref,
+    up_high_ref,
     down_any,
-    keep_ref,
-    send_ref,
-    x_ref,
-    gate_sum,
-    up_sum,
-    down_ref,
-    sems,
+    *refs,
 ):
-    loads = []
-    wide = down_ref.shape[1] // sems.shape[0]
-    for i in range(sems.shape[0]):
-        at = pl.ds(i * wide, wide)
-        loads.append(
-            pltpu.make_async_copy(down_any.at[0, :, at], down_ref.at[:, at], sems.at[i])
-        )
-        loads[-1].start()
+    *out_refs, x_ref, gate_sum, up_sum, down_ref, sems = refs
+    chunks = sems.shape[0]
+    part = down_ref.shape[0] // chunks
+
+    def load(i):
+        at = pl.ds(i * part, part)
+        return pltpu.make_async_copy(down_any.at[0, at], down_ref.at[at], sems.at[i])
+
+    pl.loop(0, chunks)(lambda i: load(i).start())
     width = x_ref.shape[1]
-    half = keep_ref.shape[0]
+    slots = own_ref.shape[0]
+    half = x_ref.shape[0] // 2
     x_ref[:half] = jnp.concatenate([own_ref[...], rest_ref[...]], axis=0)
     x_ref[half:] = jnp.concatenate([core_own_ref[...], core_rest_ref[...]], axis=0)
+    first = 0
+    tall = up_low_ref.shape[0]
+    for ref in (up_low_ref, up_high_ref):
+        for i in range(ref.shape[0] // tall):
+            x = x_ref[:, first : first + tall]
+            at = pl.ds(i * tall, tall)
+            gate = jnp.dot(x, gate_ref[0, pl.ds(first, tall)], preferred_element_type=jnp.float32)
+            upper = jnp.dot(x, ref[at], preferred_element_type=jnp.float32)
+            gate_sum[...] = gate if first == 0 else gate_sum[...] + gate
+            up_sum[...] = upper if first == 0 else up_sum[...] + upper
+            first += tall
+    gate = gate_sum[...]
+    hidden = (gate / (1.0 + jnp.exp(-gate)) * up_sum[...]).astype(jnp.bfloat16)
+    pl.loop(0, chunks)(lambda i: load(i).wait())
     deep = 1024
     for step in range(width // deep):
         at = pl.ds(step * deep, deep)
-        x = x_ref[:, at]
-        gate = jnp.dot(x, gate_ref[at, :], preferred_element_type=jnp.float32)
-        upper = jnp.dot(x, up_ref[at, :], preferred_element_type=jnp.float32)
-        if step == 0:
-            gate_sum[...] = gate
-            up_sum[...] = upper
-        else:
-            gate_sum[...] += gate
-            up_sum[...] += upper
-    gate = gate_sum[...]
-    hidden = (gate / (1.0 + jnp.exp(-gate)) * up_sum[...]).astype(jnp.bfloat16)
-    for i, load in enumerate(loads):
-        load.wait()
-        for low in range(i * wide, (i + 1) * wide, deep):
-            at = pl.ds(low, deep)
-            piece = jnp.dot(hidden, down_ref[:, at], preferred_element_type=jnp.float32)
-            piece = piece.astype(jnp.bfloat16)
-            keep_ref[:, at] = piece[:half]
-            send_ref[:, at] = piece[half:]
-
-
-def chip_sum_kernel(keep_ref, got_ref, own_ref, *out_refs):
-    total = keep_ref[...].astype(jnp.float32) + got_ref[...].astype(jnp.float32)
-    part = own_ref.shape[0]
-    own_ref[...] = total[:part]
-    for i, ref in enumerate(out_refs):
-        ref[...] = total[(i + 1) * part : (i + 2) * part].astype(jnp.bfloat16)
-
-
-def plane_sum_kernel(got, own_ref, *refs):
-    total = own_ref[...]
-    for ref in refs[:got]:
+        piece = jnp.dot(hidden, down_ref[:, at], preferred_element_type=jnp.float32)
+        for i, ref in enumerate(out_refs):
+            ref[:, at] = piece[i * slots : (i + 1) * slots].astype(jnp.bfloat16)
+
+
+def add_kernel(a_ref, b_ref, out_ref):
+    total = a_ref[...].astype(jnp.float32) + b_ref[...].astype(jnp.float32)
+    out_ref[...] = total.astype(jnp.bfloat16)
+
+
+def plane_sum_kernel(count, *refs):
+    total = refs[0][...].astype(jnp.float32)
+    for ref in refs[1:count]:
         total = total + ref[...].astype(jnp.float32)
     total = total.astype(jnp.bfloat16)
-    outs = refs[got:]
+    outs = refs[count:]
     most = outs[0].shape[0]
     for j, ref in enumerate(outs):
         ref[...] = total[j * most : (j + 1) * most]
 
 
-def finish_kernel(mixed_ref, mixing_ref, *refs):
+def finish_kernel(*refs):
+    *got, mixed_ref, mixing_ref, out_ref = refs
     total = mixed_ref[...]
-    most = refs[0].shape[0]
-    for j, ref in enumerate(refs[:-1]):
+    most = got[0].shape[0]
+    for j, ref in enumerate(got[::-1]):
         rows = ref[...].astype(jnp.float32)
         for s in range(most):
             at = j * most + s
             total = total + mixing_ref[:, at : at + 1] * rows[s : s + 1]
-    refs[-1][...] = total.astype(jnp.bfloat16)
+    out_ref[...] = total.astype(jnp.bfloat16)
 
 
 def call(kernel, outs, in_specs, *args, scratch=(), limit=8, cost=None):
@@ -314,6 +327,19 @@
     def to_plane(x, k):
         return lax.ppermute(x, plane, [(i, i ^ k) for i in range(n_side * n_cuts)])
 
+    def to_core(x):
+        return to_plane(x, 1)
+
+    def stack(*parts, after, cost=None):
+        return call(
+            functools.partial(stack_kernel, len(parts)),
+            shape((sum(x.shape[0] for x in parts), width)),
+            [VMEM] * len(parts) + [ANY] * len(after),
+            *parts,
+            *after,
+            cost=cost and pl.CostEstimate(flops=0, bytes_accessed=cost, transcendentals=0),
+        )
+
     small = [
         lengths,
         routes.T,
@@ -322,12 +348,14 @@
         new_value,
         residual,
         norm_gain,
-        router.T,
     ]
-    *outgoing, mixed, mixing = call(
+    *outgoing, mixed, normed = call(
         functools.partial(attend_kernel, experts, most, len(small) + 2),
         [shape((most, width)) for _ in range(experts)]
-        + [shape((rows, width), jnp.float32), shape((rows, slots), jnp.float32)],
+        + [
+            shape((rows, width), jnp.float32),
+            shape((rows, width)),
+        ],
         [HBM] * (len(small) + 2),
         *[in_hbm(x) for x in small],
         in_hbm(k_cache),
@@ -344,13 +372,13 @@
         limit=14,
     )
 
-    def load(weights, after):
-        extent = weights.shape[1:]
+    def load(first, count, after):
+        extent = (count * width // 4, w_up.shape[2])
         return call(
-            load_kernel,
+            functools.partial(load_kernel, first * width // 4),
             pltpu.VMEM(extent, jnp.bfloat16),
             [HBM, ANY],
-            in_hbm(weights),
+            in_hbm(w_up),
             after,
             scratch=[pltpu.SemaphoreType.DMA],
             cost=pl.CostEstimate(
@@ -358,60 +386,69 @@
             ),
         )
 
-    gate = load(w_gate, mixing)
-    arrived = [outgoing[0]] + [to_grp(outgoing[j], j) for j in range(1, experts)]
-    block = call(stack_kernel, shape((slots, width)), [VMEM] * experts + [ANY], *arrived, gate)
-    upper = load(w_up, block)
+    up_low = load(0, 1, normed)
+    mixing = call(
+        functools.partial(mixing_kernel, experts, most),
+        shape((rows, slots), jnp.float32),
+        [SMEM, VMEM, VMEM],
+        routes.T,
+        normed,
+        router.T,
+    )
+    arrived = [to_grp(outgoing[j], j) for j in range(experts - 1, 0, -1)]
+    block = stack(*arrived, outgoing[0], after=[up_low], cost=16 * MIB)
+    up_high = load(1, 3, block)
     chips = range(0, n_side * n_cuts, 2)
-    others = len(chips) - 1
+    core_block = to_core(block)
     fetched = [to_plane(block, k) for k in chips[1:]]
-    rest = call(
-        stack_kernel, shape((others * slots, width)), [VMEM] * others + [ANY], *fetched, upper
-    )
-    parts = [block, rest, to_plane(block, 1), to_plane(rest, 1)]
+    rest = stack(*fetched, after=[up_high, core_block])
     half = len(chips) * slots
     hidden = w_gate.shape[2]
-    keep, send = call(
+    outs = call(
         experts_kernel,
-        [shape((half, width))] * 2,
-        [VMEM] * 6 + [HBM],
-        *parts,
-        gate,
-        upper,
+        [shape((slots, width))] * (2 * len(chips)),
+        [VMEM] * 7 + [HBM],
+        block,
+        rest,
+        core_block,
+        to_core(rest),
+        w_gate,
+        up_low,
+        up_high,
         in_hbm(w_down),
         scratch=[
             pltpu.VMEM((2 * half, width), jnp.bfloat16),
             pltpu.VMEM((2 * half, hidden), jnp.float32),
             pltpu.VMEM((2 * half, hidden), jnp.float32),
             pltpu.VMEM((hidden, width), jnp.bfloat16),
-            pltpu.SemaphoreType.DMA((3,)),
+            pltpu.SemaphoreType.DMA((4,)),
         ],
-        limit=24,
-    )
-    got = to_plane(send, 1)
-    own, *partial = call(
-        chip_sum_kernel,
-        [shape((slots, width), jnp.float32)] + [shape((slots, width))] * others,
-        [VMEM] * 2,
-        keep,
-        got,
-    )
-    gathered = [to_plane(x, k) for x, k in zip(partial, chips[1:], strict=True)]
-    finished = call(
-        functools.partial(plane_sum_kernel, len(gathered)),
+        limit=28,
+    )
+    keep, send = outs[: len(chips)], outs[len(chips) :]
+    got = [to_core(x) for x in send[::-1]][::-1]
+    sums = [
+        call(add_kernel, shape((slots, width)), [VMEM] * 2, keep[i], got[i])
+        for i in range(1, len(chips))
+    ]
+    gathered = [to_plane(x, k) for x, k in zip(sums[::-1], chips[:0:-1], strict=True)]
+    *finished, finished_own = call(
+        functools.partial(plane_sum_kernel, 2 + len(gathered)),
         [shape((most, width)) for _ in range(experts)],
-        [VMEM] * (1 + len(gathered)),
-        own,
+        [VMEM] * (2 + len(gathered)),
         *gathered,
-    )
-    returned = [finished[0]] + [to_grp(finished[j], j) for j in range(1, experts)]
+        keep[0],
+        got[0],
+    )
+    returned = [to_grp(x, experts - 1 - i) for i, x in enumerate(finished)]
     return call(
         finish_kernel,
         shape((rows, width)),
         [VMEM] * (2 + experts),
+        *returned,
+        finished_own,
         mixed,
         mixing,
-        *returned,
     )
 
 

time: 56.8 us -> 47.4 us (0.83)
  Pallas kernels: 25 us -> 17.9 us
  waiting for transfers between devices: 13.5 us -> 10.4 us
  starting transfers between devices: 18 us -> 18.7 us
    pallas_call x9 -> x12, Pallas kernels: 25 us -> 17.9 us  [call(): pl.pallas_call(kernel, out_shape=outs, in_specs=in_specs, out_specs=jax.t...]
    ppermute x6, waiting for transfers between devices: 5.64 us -> 3.41 us  [to_grp(): return lax.ppermute(x, 'grp', [(i, i ^ j) for i in range(experts)])]
    ppermute x9 -> x12, waiting for transfers between devices: 7.85 us -> 7.04 us  [to_plane(): return lax.ppermute(x, plane, [(i, i ^ k) for i in range(n_side * n_cuts)])]
    ppermute x9 -> x12, starting transfers between devices: 7.88 us -> 8.47 us  [to_plane(): return lax.ppermute(x, plane, [(i, i ^ k) for i in range(n_side * n_cuts)])]
  transfers between devices with their start and end apart: 15 -> 18, of which waited for: 8 -> 10; matrix products, arithmetic and copies ran while one was open for 0% -> 0% of each run, Pallas kernels for 16% -> 14%
where the time goes in v4:
time: 47.4 us; the launch traced here: 47.3 us
  starting transfers between devices  18.7 us (39%)
  Pallas kernels  17.9 us (38%)
  waiting for transfers between devices  10.4 us (22%)
    pallas_call x12, Pallas kernels, call(): pl.pallas_call(kernel, out_shape=outs, in_specs=in_specs, out_specs=jax.t...  17.9 us
    ppermute x6, starting transfers between devices, to_grp(): return lax.ppermute(x, 'grp', [(i, i ^ j) for i in range(experts)])  10.2 us
    ppermute x12, starting transfers between devices, to_plane(): return lax.ppermute(x, plane, [(i, i ^ k) for i in range(n_side * n_cuts)])  8.47 us
    ppermute x12, waiting for transfers between devices, to_plane(): return lax.ppermute(x, plane, [(i, i ^ k) for i in range(n_side * n_cuts)])  7.04 us
    ppermute x6, waiting for transfers between devices, to_grp(): return lax.ppermute(x, 'grp', [(i, i ^ j) for i in range(experts)])  3.41 us
  transfers between devices with their start and end apart: 18, of which 10 were waited for; matrix products, arithmetic and copies ran while one was open for 0% of the time, Pallas kernels for 14%

profile of v4, /device:TPU:0, one launch (start us, length us, event | category | flops | bytes accessed | tf_op | source)
XLA Modules:
  0.0 47.3 jit_solution(16722522840556242682)
XLA Ops:
  0.0 3.4 %shard_map.127 = (bf16[2,6144]{1,0:T(2,128)(2,1)S(1)}, bf16[2,6144]{1,0:T(2,128)(2,1)S(1)}, bf16[2,6144]{1,0:T(2,128)(2,1)S(1)}, bf16[2,6144]{1,0:T(2,128)(2,1)S...) custom-call(s32[4]{0:T(128)} %refs_0_.1, s32[2,4]{1,0:T(2,128)} %bitcast.5, bf16[4,6144]{1,0:T(4,128)(2,1)} %refs_2_.1, ...), custom_call_target="tpu_custom_call" | custom-call | tf_op jit(solution)/shard_map/pallas_call | solution.py:282
  3.4 5.1 %collective-permute-start = (bf16[2,6144]{1,0:T(2,128)(2,1)S(1)}, bf16[2,6144]{1,0:T(2,128)(2,1)S(1)}, u32[]{:S(2)}, u32[]{:S(2)}) collective-permute-start(bf16[2,6144]{1,0:T(2,128)(2,1)S(1)} %get-tuple-element.23), channel_id=1, source_target_pairs={{0,12},{4,8},{8,4},{12,0},{1,13},{5,9},{9,5},{13,1},{2,14},{6,10},... | collective-permute-start | bytes 73736 | tf_op jit(solution)/shard_map/ppermute | solution.py:325
  8.6 0.0 collective-permute-start.1
  8.6 0.6 %collective-permute-start.2 = (bf16[2,6144]{1,0:T(2,128)(2,1)S(1)}, bf16[2,6144]{1,0:T(2,128)(2,1)S(1)}, u32[]{:S(2)}, u32[]{:S(2)}) collective-permute-start(bf16[2,6144]{1,0:T(2,128)(2,1)S(1)} %get-tuple-element.25), channel_id=1, source_target_pairs={{0,4},{4,0},{8,12},{12,8},{1,5},{5,1},{9,13},{13,9},{2,6},{6,2},{1... | collective-permute-start | bytes 73736 | tf_op jit(solution)/shard_map/ppermute | solution.py:325
  9.2 1.9 %shard_map.128.refs_4_.up_low_ref = bf16[1536,1024]{1,0:T(8,128)(2,1)S(1)} custom-call(bf16[1,6144,1024]{2,1,0:T(8,128)(2,1)} %w_any.3, bf16[4,6144]{1,0:T(4,128)(2,1)S(1)} %get-tuple-element.27._.normed_ref), custom_call_target="tpu_custom_call" | custom-call | bytes 3145728 | tf_op jit(solution)/shard_map/pallas_call | solution.py:282
  11.1 0.0 collective-permute-done.refs_0_
  11.1 2.2 %collective-permute-done.1.refs_1_ = bf16[2,6144]{1,0:T(2,128)(2,1)S(1)} collective-permute-done((bf16[2,6144]{1,0:T(2,128)(2,1)S(1)}, bf16[2,6144]{1,0:T(2,128)(2,1)S(1)}, u32[]{:S(2)}, u32[]{:S(2)}) %collective-permute-start.1) | collective-permute-done | bytes 24608 | tf_op jit(solution)/shard_map/ppermute | solution.py:325
  13.3 0.0 collective-permute-done.2.refs_2_
  13.3 0.0 slice-start
  13.3 0.1 shard_map.129._.own_ref
  13.4 0.0 slice-start.1
  13.4 0.0 slice-start.2
  13.4 0.1 collective-permute-start.6
  13.5 2.5 %collective-permute-start.5 = (bf16[8,6144]{1,0:T(8,128)(2,1)S(1)}, bf16[8,6144]{1,0:T(8,128)(2,1)S(1)}, u32[]{:S(2)}, u32[]{:S(2)}) collective-permute-start(bf16[8,6144]{1,0:T(8,128)(2,1)S(1)} %shard_map.129._.own_ref), channel_id=1, source_target_pairs={{0,18},{1,19},{2,16},{3,17},{16,2},{17,3},{18,0},{19,1},{4,22},{5,... | collective-permute-start | bytes 294920 | tf_op jit(solution)/shard_map/ppermute | solution.py:328
  16.0 0.5 %collective-permute-start.4 = (bf16[8,6144]{1,0:T(8,128)(2,1)S(1)}, bf16[8,6144]{1,0:T(8,128)(2,1)S(1)}, u32[]{:S(2)}, u32[]{:S(2)}) collective-permute-start(bf16[8,6144]{1,0:T(8,128)(2,1)S(1)} %shard_map.129._.own_ref), channel_id=1, source_target_pairs={{0,16},{1,17},{2,18},{3,19},{16,0},{17,1},{18,2},{19,3},{4,20},{5,... | collective-permute-start | bytes 294920 | tf_op jit(solution)/shard_map/ppermute | solution.py:328
  16.5 0.5 %collective-permute-start.3 = (bf16[8,6144]{1,0:T(8,128)(2,1)S(1)}, bf16[8,6144]{1,0:T(8,128)(2,1)S(1)}, u32[]{:S(2)}, u32[]{:S(2)}) collective-permute-start(bf16[8,6144]{1,0:T(8,128)(2,1)S(1)} %shard_map.129._.own_ref), channel_id=1, source_target_pairs={{0,2},{1,3},{2,0},{3,1},{16,18},{17,19},{18,16},{19,17},{4,6},{5,7... | collective-permute-start | bytes 294920 | tf_op jit(solution)/shard_map/ppermute | solution.py:328
  17.0 3.7 %shard_map.130.refs_3_.up_high_ref = bf16[4608,1024]{1,0:T(8,128)(2,1)S(1)} custom-call(bf16[1,6144,1024]{2,1,0:T(8,128)(2,1)} %w_any.3, bf16[8,6144]{1,0:T(8,128)(2,1)S(1)} %shard_map.129._.own_ref), custom_call_target="tpu_custom_call" | custom-call | bytes 9437184 | tf_op jit(solution)/shard_map/pallas_call | solution.py:282
  20.7 0.0 collective-permute-done.6.refs_4_.core_own_ref
  20.7 0.0 collective-permute-done.5.refs_2_
  20.7 0.9 %collective-permute-done.4.refs_1_ = bf16[8,6144]{1,0:T(8,128)(2,1)S(1)} collective-permute-done((bf16[8,6144]{1,0:T(8,128)(2,1)S(1)}, bf16[8,6144]{1,0:T(8,128)(2,1)S(1)}, u32[]{:S(2)}, u32[]{:S(2)}) %collective-permute-start.4) | collective-permute-done | bytes 98336 | tf_op jit(solution)/shard_map/ppermute | solution.py:328
  21.7 0.1 collective-permute-done.3.refs_0_
  21.8 0.0 copy-start
  21.8 0.0 copy-start.1
  21.8 0.1 collective-permute-start.7
  21.9 1.6 %collective-permute-done.7.core_rest_ref = bf16[24,6144]{1,0:T(8,128)(2,1)S(1)} collective-permute-done((bf16[24,6144]{1,0:T(8,128)(2,1)S(1)}, bf16[24,6144]{1,0:T(8,128)(2,1)S(1)}, u32[]{:S(2)}, u32[]{:S(2)}) %collective-permute-start.7) | collective-permute-done | bytes 294944 | tf_op jit(solution)/shard_map/ppermute | solution.py:328
  23.4 0.0 slice-done
  23.4 0.0 slice-done.1
  23.4 0.0 slice-done.2
  23.4 7.0 %shard_map.132 = (bf16[8,6144]{1,0:T(8,128)(2,1)S(1)}, bf16[8,6144]{1,0:T(8,128)(2,1)S(1)}, bf16[8,6144]{1,0:T(8,128)(2,1)S(1)}, bf16[8,6144]{1,0:T(8,128)(2,1)S...) custom-call(bf16[8,6144]{1,0:T(8,128)(2,1)S(1)} %shard_map.129._.own, ...), custom_call_target="tpu_custom_call" | custom-call | tf_op jit(solution)/shard_map/pallas_call | solution.py:282
  30.4 0.2 collective-permute-start.8
  30.6 0.4 collective-permute-start.10
  31.0 0.1 collective-permute-start.12
  31.1 0.4 collective-permute-start.14
  31.5 0.3 collective-permute-done.8.b_ref
  31.8 1.8 %collective-permute-start.9 = (bf16[8,6144]{1,0:T(8,128)(2,1)S(1)}, bf16[8,6144]{1,0:T(8,128)(2,1)S(1)}, u32[]{:S(2)}, u32[]{:S(2)}) collective-permute-start(bf16[8,6144]{1,0:T(8,128)(2,1)S(1)} %shard_map.133), channel_id=1, source_target_pairs={{0,18},{1,19},{2,16},{3,17},{16,2},{17,3},{18,0},{19,1},{4,22},{5,... | collective-permute-start | bytes 294920 | tf_op jit(solution)/shard_map/ppermute | solution.py:328
  33.6 0.0 collective-permute-done.10.b_ref
  33.6 1.4 %collective-permute-start.11 = (bf16[8,6144]{1,0:T(8,128)(2,1)S(1)}, bf16[8,6144]{1,0:T(8,128)(2,1)S(1)}, u32[]{:S(2)}, u32[]{:S(2)}) collective-permute-start(bf16[8,6144]{1,0:T(8,128)(2,1)S(1)} %shard_map.134), channel_id=1, source_target_pairs={{0,16},{1,17},{2,18},{3,19},{16,0},{17,1},{18,2},{19,3},{4,20},{5,... | collective-permute-start | bytes 294920 | tf_op jit(solution)/shard_map/ppermute | solution.py:328
  35.0 0.0 collective-permute-done.12.b_ref
  35.0 0.6 %collective-permute-start.13 = (bf16[8,6144]{1,0:T(8,128)(2,1)S(1)}, bf16[8,6144]{1,0:T(8,128)(2,1)S(1)}, u32[]{:S(2)}, u32[]{:S(2)}) collective-permute-start(bf16[8,6144]{1,0:T(8,128)(2,1)S(1)} %shard_map.135), channel_id=1, source_target_pairs={{0,2},{1,3},{2,0},{3,1},{16,18},{17,19},{18,16},{19,17},{4,6},{5,7... | collective-permute-start | bytes 294920 | tf_op jit(solution)/shard_map/ppermute | solution.py:328
  35.6 0.0 collective-permute-done.14.refs_4_
  35.6 2.3 %collective-permute-done.9.refs_0_ = bf16[8,6144]{1,0:T(8,128)(2,1)S(1)} collective-permute-done((bf16[8,6144]{1,0:T(8,128)(2,1)S(1)}, bf16[8,6144]{1,0:T(8,128)(2,1)S(1)}, u32[]{:S(2)}, u32[]{:S(2)}) %collective-permute-start.9) | collective-permute-done | bytes 98336 | tf_op jit(solution)/shard_map/ppermute | solution.py:328
  37.8 1.9 %collective-permute-done.11.refs_1_ = bf16[8,6144]{1,0:T(8,128)(2,1)S(1)} collective-permute-done((bf16[8,6144]{1,0:T(8,128)(2,1)S(1)}, bf16[8,6144]{1,0:T(8,128)(2,1)S(1)}, u32[]{:S(2)}, u32[]{:S(2)}) %collective-permute-start.11) | collective-permute-done | bytes 98336 | tf_op jit(solution)/shard_map/ppermute | solution.py:328
  39.7 0.0 collective-permute-done.13.refs_2_
  39.8 0.1 shard_map.136
  39.8 1.7 %collective-permute-start.15 = (bf16[2,6144]{1,0:T(2,128)(2,1)S(1)}, bf16[2,6144]{1,0:T(2,128)(2,1)S(1)}, u32[]{:S(2)}, u32[]{:S(2)}) collective-permute-start(bf16[2,6144]{1,0:T(2,128)(2,1)S(1)} %get-tuple-element.36), channel_id=1, source_target_pairs={{0,12},{4,8},{8,4},{12,0},{1,13},{5,9},{9,5},{13,1},{2,14},{6,10},... | collective-permute-start | bytes 73736 | tf_op jit(solution)/shard_map/ppermute | solution.py:325
  41.5 0.5 %collective-permute-start.16 = (bf16[2,6144]{1,0:T(2,128)(2,1)S(1)}, bf16[2,6144]{1,0:T(2,128)(2,1)S(1)}, u32[]{:S(2)}, u32[]{:S(2)}) collective-permute-start(bf16[2,6144]{1,0:T(2,128)(2,1)S(1)} %get-tuple-element.37), channel_id=1, source_target_pairs={{0,8},{4,12},{8,0},{12,4},{1,9},{5,13},{9,1},{13,5},{2,10},{6,14},... | collective-permute-start | bytes 73736 | tf_op jit(solution)/shard_map/ppermute | solution.py:325
  42.0 2.3 %collective-permute-start.17 = (bf16[2,6144]{1,0:T(2,128)(2,1)S(1)}, bf16[2,6144]{1,0:T(2,128)(2,1)S(1)}, u32[]{:S(2)}, u32[]{:S(2)}) collective-permute-start(bf16[2,6144]{1,0:T(2,128)(2,1)S(1)} %get-tuple-element.38), channel_id=1, source_target_pairs={{0,4},{4,0},{8,12},{12,8},{1,5},{5,1},{9,13},{13,9},{2,6},{6,2},{1... | collective-permute-start | bytes 73736 | tf_op jit(solution)/shard_map/ppermute | solution.py:325
  44.3 0.0 copy-done
  44.3 0.0 copy-done.1
  44.3 0.8 %shard_map.137.refs_5_ = f32[4,8]{1,0:T(4,128)S(1)} custom-call(s32[2,4]{1,0:T(2,128)S(1)} %bitcast.6, bf16[4,6144]{1,0:T(4,128)(2,1)S(1)} %get-tuple-element.27._.normed_ref, bf16[4,6144]{1,0:T(4,128)(2,1)S(1)} %bitcast.4), custom_call_target="tpu_custom_call" | custom-call | tf_op jit(solution)/shard_map/pallas_call | solution.py:282
  45.1 0.6 %collective-permute-done.15.refs_0_ = bf16[2,6144]{1,0:T(2,128)(2,1)S(1)} collective-permute-done((bf16[2,6144]{1,0:T(2,128)(2,1)S(1)}, bf16[2,6144]{1,0:T(2,128)(2,1)S(1)}, u32[]{:S(2)}, u32[]{:S(2)}) %collective-permute-start.15) | collective-permute-done | bytes 24608 | tf_op jit(solution)/shard_map/ppermute | solution.py:325
  45.7 0.6 %collective-permute-done.16.refs_1_ = bf16[2,6144]{1,0:T(2,128)(2,1)S(1)} collective-permute-done((bf16[2,6144]{1,0:T(2,128)(2,1)S(1)}, bf16[2,6144]{1,0:T(2,128)(2,1)S(1)}, u32[]{:S(2)}, u32[]{:S(2)}) %collective-permute-start.16) | collective-permute-done | bytes 24608 | tf_op jit(solution)/shard_map/ppermute | solution.py:325
  46.3 0.1 collective-permute-done.17.refs_2_
  46.4 0.9 %shard_map.138 = bf16[4,6144]{1,0:T(4,128)(2,1)} custom-call(bf16[2,6144]{1,0:T(2,128)(2,1)S(1)} %collective-permute-done.15.refs_0_, bf16[2,6144]{1,0:T(2,128)(2,1)S(1)} %collective-permute-done.16.refs_1_, bf16[2,6144]{1,0:T(2,128)(2,1)S(1)} %collective-permute-done.17.refs_2_, bf16[2,6144]{1,0:T(2,128)(2,1)S(1)} %get-tuple-element.39.refs_3_, ...), custom_call_target="tpu_custom_call" | custom-call | tf_op jit(solution)/shard_map/pallas_call | solution.py:282
  (5 shorter events, 0.1 us)
Async XLA Ops:
  3.4 7.7 %collective-permute-start = (bf16[2,6144]{1,0:T(2,128)(2,1)S(1)}, bf16[2,6144]{1,0:T(2,128)(2,1)S(1)}, u32[]{:S(2)}, u32[]{:S(2)}) collective-permute-start(bf16[2,6144]{1,0:T(2,128)(2,1)S(1)} %get-tuple-element.23), channel_id=1, source_target_pairs={{0,12},{4,8},{8,4},{12,0},{1,13},{5,9},{9,5},{13,1},{2,14},{6,10},... | collective-permute-start | bytes 73736 | tf_op jit(solution)/shard_map/ppermute | solution.py:325
  8.6 4.7 %collective-permute-start.1 = (bf16[2,6144]{1,0:T(2,128)(2,1)S(1)}, bf16[2,6144]{1,0:T(2,128)(2,1)S(1)}, u32[]{:S(2)}, u32[]{:S(2)}) collective-permute-start(bf16[2,6144]{1,0:T(2,128)(2,1)S(1)} %get-tuple-element.24), channel_id=1, source_target_pairs={{0,8},{4,12},{8,0},{12,4},{1,9},{5,13},{9,1},{13,5},{2,10},{6,14},... | collective-permute-start | bytes 73736 | tf_op jit(solution)/shard_map/ppermute | solution.py:325
  8.6 4.7 %collective-permute-start.2 = (bf16[2,6144]{1,0:T(2,128)(2,1)S(1)}, bf16[2,6144]{1,0:T(2,128)(2,1)S(1)}, u32[]{:S(2)}, u32[]{:S(2)}) collective-permute-start(bf16[2,6144]{1,0:T(2,128)(2,1)S(1)} %get-tuple-element.25), channel_id=1, source_target_pairs={{0,4},{4,0},{8,12},{12,8},{1,5},{5,1},{9,13},{13,9},{2,6},{6,2},{1... | collective-permute-start | bytes 73736 | tf_op jit(solution)/shard_map/ppermute | solution.py:325
  13.3 10.1 %slice-start = ((s8[12582912]{0:T(1024)(128)(4,1)}), s8[4194304]{0:T(1024)(128)(4,1)S(1)}, s32[]{:S(2)}) async-start(s8[12582912]{0:T(1024)(128)(4,1)} %bitcast.2), calls=%async_computation | async-start | bytes 8388608
  13.4 10.1 %slice-start.1 = ((s8[12582912]{0:T(1024)(128)(4,1)}), s8[4194304]{0:T(1024)(128)(4,1)S(1)}, s32[]{:S(2)}) async-start(s8[12582912]{0:T(1024)(128)(4,1)} %bitcast.2), calls=%async_computation.1 | async-start | bytes 8388608
  13.4 10.1 %slice-start.2 = ((s8[12582912]{0:T(1024)(128)(4,1)}), s8[4194304]{0:T(1024)(128)(4,1)S(1)}, s32[]{:S(2)}) async-start(s8[12582912]{0:T(1024)(128)(4,1)} %bitcast.2), calls=%async_computation.2 | async-start | bytes 8388608
  13.4 7.3 %collective-permute-start.6 = (bf16[8,6144]{1,0:T(8,128)(2,1)S(1)}, bf16[8,6144]{1,0:T(8,128)(2,1)S(1)}, u32[]{:S(2)}, u32[]{:S(2)}) collective-permute-start(bf16[8,6144]{1,0:T(8,128)(2,1)S(1)} %shard_map.129._.own_ref), channel_id=1, source_target_pairs={{0,1},{1,0},{2,3},{3,2},{16,17},{17,16},{18,19},{19,18},{4,5},{5,4... | collective-permute-start | bytes 294920 | tf_op jit(solution)/shard_map/ppermute | solution.py:328
  13.5 7.3 %collective-permute-start.5 = (bf16[8,6144]{1,0:T(8,128)(2,1)S(1)}, bf16[8,6144]{1,0:T(8,128)(2,1)S(1)}, u32[]{:S(2)}, u32[]{:S(2)}) collective-permute-start(bf16[8,6144]{1,0:T(8,128)(2,1)S(1)} %shard_map.129._.own_ref), channel_id=1, source_target_pairs={{0,18},{1,19},{2,16},{3,17},{16,2},{17,3},{18,0},{19,1},{4,22},{5,... | collective-permute-start | bytes 294920 | tf_op jit(solution)/shard_map/ppermute | solution.py:328
  16.0 5.7 %collective-permute-start.4 = (bf16[8,6144]{1,0:T(8,128)(2,1)S(1)}, bf16[8,6144]{1,0:T(8,128)(2,1)S(1)}, u32[]{:S(2)}, u32[]{:S(2)}) collective-permute-start(bf16[8,6144]{1,0:T(8,128)(2,1)S(1)} %shard_map.129._.own_ref), channel_id=1, source_target_pairs={{0,16},{1,17},{2,18},{3,19},{16,0},{17,1},{18,2},{19,3},{4,20},{5,... | collective-permute-start | bytes 294920 | tf_op jit(solution)/shard_map/ppermute | solution.py:328
  16.5 5.3 %collective-permute-start.3 = (bf16[8,6144]{1,0:T(8,128)(2,1)S(1)}, bf16[8,6144]{1,0:T(8,128)(2,1)S(1)}, u32[]{:S(2)}, u32[]{:S(2)}) collective-permute-start(bf16[8,6144]{1,0:T(8,128)(2,1)S(1)} %shard_map.129._.own_ref), channel_id=1, source_target_pairs={{0,2},{1,3},{2,0},{3,1},{16,18},{17,19},{18,16},{19,17},{4,6},{5,7... | collective-permute-start | bytes 294920 | tf_op jit(solution)/shard_map/ppermute | solution.py:328
  21.8 22.5 %copy-start = (bf16[6144,4]{0,1:T(4,128)(2,1)S(1)}, bf16[6144,4]{0,1:T(4,128)(2,1)}, u32[]{:S(2)}) copy-start(bf16[6144,4]{0,1:T(4,128)(2,1)} %param.21) | copy-start | bytes 147460
  21.8 22.5 %copy-start.1 = (s32[4,2]{0,1:T(2,128)S(1)}, s32[4,2]{0,1:T(2,128)}, u32[]{:S(2)}) copy-start(s32[4,2]{0,1:T(2,128)} %param.22) | copy-start | bytes 100
  21.8 1.6 %collective-permute-start.7 = (bf16[24,6144]{1,0:T(8,128)(2,1)S(1)}, bf16[24,6144]{1,0:T(8,128)(2,1)S(1)}, u32[]{:S(2)}, u32[]{:S(2)}) collective-permute-start(bf16[24,6144]{1,0:T(8,128)(2,1)S(1)} %shard_map.131.rest_ref), channel_id=1, source_target_pairs={{0,1},{1,0},{2,3},{3,2},{16,17},{17,16},{18,19},{19,18},{4,5},{5,4... | collective-permute-start | bytes 884744 | tf_op jit(solution)/shard_map/ppermute | solution.py:328
  30.4 1.4 %collective-permute-start.8 = (bf16[8,6144]{1,0:T(8,128)(2,1)S(1)}, bf16[8,6144]{1,0:T(8,128)(2,1)S(1)}, u32[]{:S(2)}, u32[]{:S(2)}) collective-permute-start(bf16[8,6144]{1,0:T(8,128)(2,1)S(1)} %get-tuple-element.29), channel_id=1, source_target_pairs={{0,1},{1,0},{2,3},{3,2},{16,17},{17,16},{18,19},{19,18},{4,5},{5,4... | collective-permute-start | bytes 294920 | tf_op jit(solution)/shard_map/ppermute | solution.py:328
  30.6 3.0 %collective-permute-start.10 = (bf16[8,6144]{1,0:T(8,128)(2,1)S(1)}, bf16[8,6144]{1,0:T(8,128)(2,1)S(1)}, u32[]{:S(2)}, u32[]{:S(2)}) collective-permute-start(bf16[8,6144]{1,0:T(8,128)(2,1)S(1)} %get-tuple-element.31), channel_id=1, source_target_pairs={{0,1},{1,0},{2,3},{3,2},{16,17},{17,16},{18,19},{19,18},{4,5},{5,4... | collective-permute-start | bytes 294920 | tf_op jit(solution)/shard_map/ppermute | solution.py:328
  31.0 4.0 %collective-permute-start.12 = (bf16[8,6144]{1,0:T(8,128)(2,1)S(1)}, bf16[8,6144]{1,0:T(8,128)(2,1)S(1)}, u32[]{:S(2)}, u32[]{:S(2)}) collective-permute-start(bf16[8,6144]{1,0:T(8,128)(2,1)S(1)} %get-tuple-element.33), channel_id=1, source_target_pairs={{0,1},{1,0},{2,3},{3,2},{16,17},{17,16},{18,19},{19,18},{4,5},{5,4... | collective-permute-start | bytes 294920 | tf_op jit(solution)/shard_map/ppermute | solution.py:328
  31.1 4.4 %collective-permute-start.14 = (bf16[8,6144]{1,0:T(8,128)(2,1)S(1)}, bf16[8,6144]{1,0:T(8,128)(2,1)S(1)}, u32[]{:S(2)}, u32[]{:S(2)}) collective-permute-start(bf16[8,6144]{1,0:T(8,128)(2,1)S(1)} %get-tuple-element.35), channel_id=1, source_target_pairs={{0,1},{1,0},{2,3},{3,2},{16,17},{17,16},{18,19},{19,18},{4,5},{5,4... | collective-permute-start | bytes 294920 | tf_op jit(solution)/shard_map/ppermute | solution.py:328
  31.8 6.0 %collective-permute-start.9 = (bf16[8,6144]{1,0:T(8,128)(2,1)S(1)}, bf16[8,6144]{1,0:T(8,128)(2,1)S(1)}, u32[]{:S(2)}, u32[]{:S(2)}) collective-permute-start(bf16[8,6144]{1,0:T(8,128)(2,1)S(1)} %shard_map.133), channel_id=1, source_target_pairs={{0,18},{1,19},{2,16},{3,17},{16,2},{17,3},{18,0},{19,1},{4,22},{5,... | collective-permute-start | bytes 294920 | tf_op jit(solution)/shard_map/ppermute | solution.py:328
  33.6 6.1 %collective-permute-start.11 = (bf16[8,6144]{1,0:T(8,128)(2,1)S(1)}, bf16[8,6144]{1,0:T(8,128)(2,1)S(1)}, u32[]{:S(2)}, u32[]{:S(2)}) collective-permute-start(bf16[8,6144]{1,0:T(8,128)(2,1)S(1)} %shard_map.134), channel_id=1, source_target_pairs={{0,16},{1,17},{2,18},{3,19},{16,0},{17,1},{18,2},{19,3},{4,20},{5,... | collective-permute-start | bytes 294920 | tf_op jit(solution)/shard_map/ppermute | solution.py:328
  35.0 4.7 %collective-permute-start.13 = (bf16[8,6144]{1,0:T(8,128)(2,1)S(1)}, bf16[8,6144]{1,0:T(8,128)(2,1)S(1)}, u32[]{:S(2)}, u32[]{:S(2)}) collective-permute-start(bf16[8,6144]{1,0:T(8,128)(2,1)S(1)} %shard_map.135), channel_id=1, source_target_pairs={{0,2},{1,3},{2,0},{3,1},{16,18},{17,19},{18,16},{19,17},{4,6},{5,7... | collective-permute-start | bytes 294920 | tf_op jit(solution)/shard_map/ppermute | solution.py:328
  39.8 5.8 %collective-permute-start.15 = (bf16[2,6144]{1,0:T(2,128)(2,1)S(1)}, bf16[2,6144]{1,0:T(2,128)(2,1)S(1)}, u32[]{:S(2)}, u32[]{:S(2)}) collective-permute-start(bf16[2,6144]{1,0:T(2,128)(2,1)S(1)} %get-tuple-element.36), channel_id=1, source_target_pairs={{0,12},{4,8},{8,4},{12,0},{1,13},{5,9},{9,5},{13,1},{2,14},{6,10},... | collective-permute-start | bytes 73736 | tf_op jit(solution)/shard_map/ppermute | solution.py:325
  41.5 4.8 %collective-permute-start.16 = (bf16[2,6144]{1,0:T(2,128)(2,1)S(1)}, bf16[2,6144]{1,0:T(2,128)(2,1)S(1)}, u32[]{:S(2)}, u32[]{:S(2)}) collective-permute-start(bf16[2,6144]{1,0:T(2,128)(2,1)S(1)} %get-tuple-element.37), channel_id=1, source_target_pairs={{0,8},{4,12},{8,0},{12,4},{1,9},{5,13},{9,1},{13,5},{2,10},{6,14},... | collective-permute-start | bytes 73736 | tf_op jit(solution)/shard_map/ppermute | solution.py:325
  42.0 4.4 %collective-permute-start.17 = (bf16[2,6144]{1,0:T(2,128)(2,1)S(1)}, bf16[2,6144]{1,0:T(2,128)(2,1)S(1)}, u32[]{:S(2)}, u32[]{:S(2)}) collective-permute-start(bf16[2,6144]{1,0:T(2,128)(2,1)S(1)} %get-tuple-element.38), channel_id=1, source_target_pairs={{0,4},{4,0},{8,12},{12,8},{1,5},{5,1},{9,13},{13,9},{2,6},{6,2},{1... | collective-permute-start | bytes 73736 | tf_op jit(solution)/shard_map/ppermute | solution.py:325

commit v5 on v4

--- a/solution.py
+++ b/solution.py
@@ -26,18 +26,18 @@
 
 def attend_kernel(experts, most, n_in, *refs):
     hbm_refs = refs[:n_in]
-    out_refs = refs[n_in : n_in + experts]
-    mixed_ref, normed_ref = refs[n_in + experts : n_in + experts + 2]
-    scratch = refs[n_in + experts + 2 : -2]
+    mixed_ref, power_ref, picks_ref, gain_ref = refs[n_in : n_in + 4]
+    scratch = refs[n_in + 4 : -2]
     sem, cache_sems = refs[-2:]
     k_any, v_any = hbm_refs[-2:]
     k_ref, v_ref = scratch[-2:]
-    lengths, routes, q_ref, nk_ref, nv_ref, res_ref, gain_ref = scratch[:-2]
+    staged = list(scratch[:-2]) + [gain_ref]
+    lengths, routes, q_ref, nk_ref, nv_ref, res_ref, _ = staged
     rows, width = q_ref.shape
     span = k_ref.shape[1]
     scale = 1.0 / math.sqrt(HEAD_DIM)
     small = [
-        pltpu.make_async_copy(hbm_refs[i], scratch[i], sem.at[i]) for i in range(n_in - 2)
+        pltpu.make_async_copy(hbm_refs[i], staged[i], sem.at[i]) for i in range(n_in - 2)
     ]
 
     def load_k(r):
@@ -45,13 +45,13 @@
 
     def load_v(r):
         return pltpu.make_async_copy(v_any.at[r], v_ref.at[r], cache_sems.at[1, r])
-
-    for load in small:
-        load.start()
 
     @pl.loop(0, rows)
     def _(r):
         load_k(r).start()
+
+    for load in small:
+        load.start()
 
     @pl.loop(0, rows)
     def _(r):
@@ -142,18 +142,30 @@
                 mixed = res_ref[:, at].astype(jnp.float32) + attended[j * rows : (j + 1) * rows]
                 mixed_ref[:, at] = mixed
                 power = power + mixed * mixed
-    mean = jnp.sum(power, axis=1, keepdims=True) * (1.0 / width)
+    power_ref[...] = power
+    slot_col = lax.broadcasted_iota(jnp.int32, picks_ref.shape, 0)
+    row_col = lax.broadcasted_iota(jnp.int32, picks_ref.shape, 1)
+    picks = jnp.zeros(picks_ref.shape, jnp.float32)
+    for r, _, slot in slots_of(routes, rows, most):
+        picks = jnp.where((slot_col == slot) & (row_col == r), 1.0, picks)
+    picks_ref[...] = picks
+
+
+def norm_kernel(mixed_ref, power_ref, picks_ref, gain_ref, normed_ref, *out_refs):
+    rows, width = mixed_ref.shape
+    mean = jnp.sum(power_ref[...], axis=1, keepdims=True) * (1.0 / width)
     gain = gain_ref[...].astype(jnp.float32).reshape(1, width)
     normed = (mixed_ref[...] * lax.rsqrt(mean + 1e-05) * gain).astype(jnp.bfloat16)
     normed_ref[...] = normed
     normed = normed.astype(jnp.float32)
-    slot_col = lax.broadcasted_iota(jnp.int32, (experts * most, 1), 0)
-    outgoing = jnp.zeros((experts * most, width), jnp.float32)
-    for r, _, slot in slots_of(routes, rows, most):
-        outgoing = jnp.where(slot_col == slot, normed[r : r + 1], outgoing)
+    picks = picks_ref[...]
+    outgoing = jnp.zeros((picks.shape[0], width), jnp.float32)
+    for r in range(rows):
+        outgoing = jnp.where(picks[:, r : r + 1] > 0, normed[r : r + 1], outgoing)
     outgoing = outgoing.astype(jnp.bfloat16)
-    for j in range(experts):
-        out_refs[j][...] = outgoing[j * most : (j + 1) * most]
+    most = out_refs[0].shape[0]
+    for j, ref in enumerate(out_refs):
+        ref[...] = outgoing[j * most : (j + 1) * most]
 
 
 def slots_of(routes, rows, most):
@@ -205,9 +217,11 @@
 
 def experts_kernel(
     own_ref,
-    rest_ref,
+    corner_ref,
+    sides_ref,
     core_own_ref,
-    core_rest_ref,
+    core_corner_ref,
+    core_sides_ref,
     gate_ref,
     up_low_ref,
     up_high_ref,
@@ -226,10 +240,12 @@
     width = x_ref.shape[1]
     slots = own_ref.shape[0]
     half = x_ref.shape[0] // 2
-    x_ref[:half] = jnp.concatenate([own_ref[...], rest_ref[...]], axis=0)
-    x_ref[half:] = jnp.concatenate([core_own_ref[...], core_rest_ref[...]], axis=0)
+    x_ref[:half] = jnp.concatenate([own_ref[...], corner_ref[...], sides_ref[...]], axis=0)
+    x_ref[half:] = jnp.concatenate(
+        [core_own_ref[...], core_corner_ref[...], core_sides_ref[...]], axis=0
+    )
     first = 0
-    tall = up_low_ref.shape[0]
+    tall = math.gcd(up_low_ref.shape[0], up_high_ref.shape[0])
     for ref in (up_low_ref, up_high_ref):
         for i in range(ref.shape[0] // tall):
             x = x_ref[:, first : first + tall]
@@ -330,14 +346,13 @@
     def to_core(x):
         return to_plane(x, 1)
 
-    def stack(*parts, after, cost=None):
+    def stack(*parts, after):
         return call(
             functools.partial(stack_kernel, len(parts)),
             shape((sum(x.shape[0] for x in parts), width)),
             [VMEM] * len(parts) + [ANY] * len(after),
             *parts,
             *after,
-            cost=cost and pl.CostEstimate(flops=0, bytes_accessed=cost, transcendentals=0),
         )
 
     small = [
@@ -349,19 +364,21 @@
         residual,
         norm_gain,
     ]
-    *outgoing, mixed, normed = call(
+    mixed, power, picks, gain = call(
         functools.partial(attend_kernel, experts, most, len(small) + 2),
-        [shape((most, width)) for _ in range(experts)]
-        + [
+        [
             shape((rows, width), jnp.float32),
-            shape((rows, width)),
+            shape((rows, HEAD_DIM), jnp.float32),
+            shape((slots, rows), jnp.float32),
+            shape((width,)),
         ],
         [HBM] * (len(small) + 2),
         *[in_hbm(x) for x in small],
         in_hbm(k_cache),
         in_hbm(v_cache),
         scratch=[
-            (pltpu.SMEM if i < 2 else pltpu.VMEM)(x.shape, x.dtype) for i, x in enumerate(small)
+            (pltpu.SMEM if i < 2 else pltpu.VMEM)(x.shape, x.dtype)
+            for i, x in enumerate(small[:-1])
         ]
         + [
             pltpu.VMEM(k_cache.shape, jnp.bfloat16),
@@ -370,6 +387,17 @@
             pltpu.SemaphoreType.DMA((2, rows)),
         ],
         limit=14,
+    )
+
+    normed, *outgoing = call(
+        norm_kernel,
+        [shape((rows, width))] + [shape((most, width)) for _ in range(experts)],
+        [VMEM] * 4,
+        mixed,
+        power,
+        picks,
+        gain,
+        cost=pl.CostEstimate(flops=0, bytes_accessed=16 * MIB, transcendentals=0),
     )
 
     def load(first, count, after):
@@ -381,9 +409,6 @@
             in_hbm(w_up),
             after,
             scratch=[pltpu.SemaphoreType.DMA],
-            cost=pl.CostEstimate(
-                flops=0, bytes_accessed=math.prod(extent) * 2, transcendentals=0
-            ),
         )
 
     up_low = load(0, 1, normed)
@@ -396,22 +421,25 @@
         router.T,
     )
     arrived = [to_grp(outgoing[j], j) for j in range(experts - 1, 0, -1)]
-    block = stack(*arrived, outgoing[0], after=[up_low], cost=16 * MIB)
+    block = stack(*arrived, outgoing[0], after=[up_low])
     up_high = load(1, 3, block)
     chips = range(0, n_side * n_cuts, 2)
     core_block = to_core(block)
-    fetched = [to_plane(block, k) for k in chips[1:]]
-    rest = stack(*fetched, after=[up_high, core_block])
+    order = [0, chips[-1]] + list(chips[1:-1])
+    sides = stack(*[to_plane(block, k) for k in order[2:]], after=[up_high, core_block])
+    corner = to_plane(block, order[1])
     half = len(chips) * slots
     hidden = w_gate.shape[2]
     outs = call(
         experts_kernel,
         [shape((slots, width))] * (2 * len(chips)),
-        [VMEM] * 7 + [HBM],
+        [VMEM] * 9 + [HBM],
         block,
-        rest,
+        corner,
+        sides,
         core_block,
-        to_core(rest),
+        to_core(corner),
+        to_core(sides),
         w_gate,
         up_low,
         up_high,
@@ -426,12 +454,13 @@
         limit=28,
     )
     keep, send = outs[: len(chips)], outs[len(chips) :]
-    got = [to_core(x) for x in send[::-1]][::-1]
-    sums = [
-        call(add_kernel, shape((slots, width)), [VMEM] * 2, keep[i], got[i])
-        for i in range(1, len(chips))
-    ]
-    gathered = [to_plane(x, k) for x, k in zip(sums[::-1], chips[:0:-1], strict=True)]
+    keep, send = dict(zip(order, keep, strict=True)), dict(zip(order, send, strict=True))
+    got = {k: to_core(send[k]) for k in chips[::-1]}
+    sums = {
+        k: call(add_kernel, shape((slots, width)), [VMEM] * 2, keep[k], got[k])
+        for k in chips[:0:-1]
+    }
+    gathered = [to_plane(sums[k], k) for k in chips[:0:-1]]
     *finished, finished_own = call(
         functools.partial(plane_sum_kernel, 2 + len(gathered)),
         [shape((most, width)) for _ in range(experts)],

time: 47.4 us -> 47.3 us (level)
    ppermute x12 -> x13, waiting for transfers between devices: 7.04 us -> 6.95 us  [to_plane(): return lax.ppermute(x, plane, [(i, i ^ k) for i in range(n_side * n_cuts)])]
    pallas_call x12 -> x13, Pallas kernels: 17.9 us -> 17.9 us  [call(): pl.pallas_call(kernel, out_shape=outs, in_specs=in_specs, out_specs=jax.t...]
    ppermute x12 -> x13, starting transfers between devices: 8.47 us -> 8.47 us  [to_plane(): return lax.ppermute(x, plane, [(i, i ^ k) for i in range(n_side * n_cuts)])]
  transfers between devices with their start and end apart: 18 -> 19, of which waited for: 10 -> 8; matrix products, arithmetic and copies ran while one was open for 0% -> 0% of each run, Pallas kernels for 14% -> 14%
where the time goes in v5:
time: 47.3 us; the launch traced here: 47.1 us
  starting transfers between devices  18.7 us (40%)
  Pallas kernels  17.9 us (38%)
  waiting for transfers between devices  10.4 us (22%)
    pallas_call x13, Pallas kernels, call(): pl.pallas_call(kernel, out_shape=outs, in_specs=in_specs, out_specs=jax.t...  17.9 us
    ppermute x6, starting transfers between devices, to_grp(): return lax.ppermute(x, 'grp', [(i, i ^ j) for i in range(experts)])  10.2 us
    ppermute x13, starting transfers between devices, to_plane(): return lax.ppermute(x, plane, [(i, i ^ k) for i in range(n_side * n_cuts)])  8.47 us
    ppermute x13, waiting for transfers between devices, to_plane(): return lax.ppermute(x, plane, [(i, i ^ k) for i in range(n_side * n_cuts)])  6.95 us
    ppermute x6, waiting for transfers between devices, to_grp(): return lax.ppermute(x, 'grp', [(i, i ^ j) for i in range(experts)])  3.41 us
  transfers between devices with their start and end apart: 19, of which 8 were waited for; matrix products, arithmetic and copies ran while one was open for 0% of the time, Pallas kernels for 14%

profile of v5, /device:TPU:0, one launch (start us, length us, event | category | flops | bytes accessed | tf_op | source)
XLA Modules:
  0.0 47.1 jit_solution(17403563307424530250)
XLA Ops:
  0.0 3.1 %shard_map.127 = (f32[4,6144]{1,0:T(4,128)S(1)}, f32[4,128]{1,0:T(4,128)S(1)}, f32[8,4]{1,0:T(8,128)S(1)}, bf16[6144]{0:T(1024)(128)(2,1)S(1)}) custom-call(s32[4]{0:T(128)} %refs_0_.1, s32[2,4]{1,0:T(2,128)} %bitcast.5, bf16[4,6144]{1,0:T(4,128)(2,1)} %refs_2_.1, bf16[4,1024]{1,0:T(4,128)(2,1)} %refs_3_.1, bf16[4,1024]{1,0:T(4,128)(2,1)} %refs_4_.1, ...), custom_call_target="tpu_custom_call" | custom-call | tf_op jit(solution)/shard_map/pallas_call | solution.py:298
  3.1 0.2 shard_map.128
  3.4 5.1 %collective-permute-start = (bf16[2,6144]{1,0:T(2,128)(2,1)S(1)}, bf16[2,6144]{1,0:T(2,128)(2,1)S(1)}, u32[]{:S(2)}, u32[]{:S(2)}) collective-permute-start(bf16[2,6144]{1,0:T(2,128)(2,1)S(1)} %get-tuple-element.30), channel_id=1, source_target_pairs={{0,12},{4,8},{8,4},{12,0},{1,13},{5,9},{9,5},{13,1},{2,14},{6,10},... | collective-permute-start | bytes 73736 | tf_op jit(solution)/shard_map/ppermute | solution.py:341
  8.5 0.0 collective-permute-start.1
  8.5 0.6 %collective-permute-start.2 = (bf16[2,6144]{1,0:T(2,128)(2,1)S(1)}, bf16[2,6144]{1,0:T(2,128)(2,1)S(1)}, u32[]{:S(2)}, u32[]{:S(2)}) collective-permute-start(bf16[2,6144]{1,0:T(2,128)(2,1)S(1)} %get-tuple-element.32), channel_id=1, source_target_pairs={{0,4},{4,0},{8,12},{12,8},{1,5},{5,1},{9,13},{13,9},{2,6},{6,2},{1... | collective-permute-start | bytes 73736 | tf_op jit(solution)/shard_map/ppermute | solution.py:341
  9.1 1.9 %shard_map.129.refs_4_.up_low_ref = bf16[1536,1024]{1,0:T(8,128)(2,1)S(1)} custom-call(bf16[1,6144,1024]{2,1,0:T(8,128)(2,1)} %w_any.3, bf16[4,6144]{1,0:T(4,128)(2,1)S(1)} %get-tuple-element.34._.normed_ref), custom_call_target="tpu_custom_call" | custom-call | tf_op jit(solution)/shard_map/pallas_call | solution.py:298
  11.0 0.0 collective-permute-done.refs_0_
  11.1 2.2 %collective-permute-done.1.refs_1_ = bf16[2,6144]{1,0:T(2,128)(2,1)S(1)} collective-permute-done((bf16[2,6144]{1,0:T(2,128)(2,1)S(1)}, bf16[2,6144]{1,0:T(2,128)(2,1)S(1)}, u32[]{:S(2)}, u32[]{:S(2)}) %collective-permute-start.1) | collective-permute-done | bytes 24608 | tf_op jit(solution)/shard_map/ppermute | solution.py:341
  13.2 0.0 collective-permute-done.2.refs_2_
  13.2 0.0 slice-start
  13.2 0.1 shard_map.130._.own_ref
  13.3 0.0 slice-start.1
  13.3 0.0 slice-start.2
  13.3 0.1 collective-permute-start.6
  13.4 1.6 %collective-permute-start.5 = (bf16[8,6144]{1,0:T(8,128)(2,1)S(1)}, bf16[8,6144]{1,0:T(8,128)(2,1)S(1)}, u32[]{:S(2)}, u32[]{:S(2)}) collective-permute-start(bf16[8,6144]{1,0:T(8,128)(2,1)S(1)} %shard_map.130._.own_ref), channel_id=1, source_target_pairs={{0,16},{1,17},{2,18},{3,19},{16,0},{17,1},{18,2},{19,3},{4,20},{5,... | collective-permute-start | bytes 294920 | tf_op jit(solution)/shard_map/ppermute | solution.py:344
  15.0 1.5 %collective-permute-start.4 = (bf16[8,6144]{1,0:T(8,128)(2,1)S(1)}, bf16[8,6144]{1,0:T(8,128)(2,1)S(1)}, u32[]{:S(2)}, u32[]{:S(2)}) collective-permute-start(bf16[8,6144]{1,0:T(8,128)(2,1)S(1)} %shard_map.130._.own_ref), channel_id=1, source_target_pairs={{0,2},{1,3},{2,0},{3,1},{16,18},{17,19},{18,16},{19,17},{4,6},{5,7... | collective-permute-start | bytes 294920 | tf_op jit(solution)/shard_map/ppermute | solution.py:344
  16.5 0.5 %collective-permute-start.3 = (bf16[8,6144]{1,0:T(8,128)(2,1)S(1)}, bf16[8,6144]{1,0:T(8,128)(2,1)S(1)}, u32[]{:S(2)}, u32[]{:S(2)}) collective-permute-start(bf16[8,6144]{1,0:T(8,128)(2,1)S(1)} %shard_map.130._.own_ref), channel_id=1, source_target_pairs={{0,18},{1,19},{2,16},{3,17},{16,2},{17,3},{18,0},{19,1},{4,22},{5,... | collective-permute-start | bytes 294920 | tf_op jit(solution)/shard_map/ppermute | solution.py:344
  17.0 3.7 %shard_map.131.refs_2_.up_high_ref = bf16[4608,1024]{1,0:T(8,128)(2,1)S(1)} custom-call(bf16[1,6144,1024]{2,1,0:T(8,128)(2,1)} %w_any.3, bf16[8,6144]{1,0:T(8,128)(2,1)S(1)} %shard_map.130._.own_ref), custom_call_target="tpu_custom_call" | custom-call | tf_op jit(solution)/shard_map/pallas_call | solution.py:298
  20.6 0.0 collective-permute-done.6.refs_3_.core_own_ref
  20.7 0.0 collective-permute-done.5.refs_1_
  20.7 0.0 collective-permute-done.4.refs_0_
  20.7 0.0 copy-start
  20.7 0.0 copy-start.1
  20.7 0.1 collective-permute-start.8
  20.8 1.2 %collective-permute-done.3.corner_ref = bf16[8,6144]{1,0:T(8,128)(2,1)S(1)} collective-permute-done((bf16[8,6144]{1,0:T(8,128)(2,1)S(1)}, bf16[8,6144]{1,0:T(8,128)(2,1)S(1)}, u32[]{:S(2)}, u32[]{:S(2)}) %collective-permute-start.3) | collective-permute-done | bytes 98336 | tf_op jit(solution)/shard_map/ppermute | solution.py:344
  22.0 0.0 collective-permute-start.7
  22.0 1.3 %collective-permute-done.7.core_corner_ref = bf16[8,6144]{1,0:T(8,128)(2,1)S(1)} collective-permute-done((bf16[8,6144]{1,0:T(8,128)(2,1)S(1)}, bf16[8,6144]{1,0:T(8,128)(2,1)S(1)}, u32[]{:S(2)}, u32[]{:S(2)}) %collective-permute-start.7) | collective-permute-done | bytes 98336 | tf_op jit(solution)/shard_map/ppermute | solution.py:344
  23.3 0.0 collective-permute-done.8.core_sides_ref
  23.3 0.0 slice-done
  23.3 0.0 slice-done.1
  23.3 0.0 slice-done.2
  23.3 7.0 %shard_map.133 = (bf16[8,6144]{1,0:T(8,128)(2,1)S(1)}, bf16[8,6144]{1,0:T(8,128)(2,1)S(1)}, bf16[8,6144]{1,0:T(8,128)(2,1)S(1)}, bf16[8,6144]{1,0:T(8,128)(2,1)S...) custom-call(bf16[8,6144]{1,0:T(8,128)(2,1)S(1)} %shard_map.130._.own, ...), custom_call_target="tpu_custom_call" | custom-call | tf_op jit(solution)/shard_map/pallas_call | solution.py:298
  30.3 0.2 collective-permute-start.9
  30.5 0.4 collective-permute-start.11
  30.9 0.1 collective-permute-start.13
  31.0 0.4 collective-permute-start.15
  31.4 0.3 collective-permute-done.9.b_ref
  31.7 2.4 %collective-permute-start.10 = (bf16[8,6144]{1,0:T(8,128)(2,1)S(1)}, bf16[8,6144]{1,0:T(8,128)(2,1)S(1)}, u32[]{:S(2)}, u32[]{:S(2)}) collective-permute-start(bf16[8,6144]{1,0:T(8,128)(2,1)S(1)} %shard_map.134), channel_id=1, source_target_pairs={{0,18},{1,19},{2,16},{3,17},{16,2},{17,3},{18,0},{19,1},{4,22},{5,... | collective-permute-start | bytes 294920 | tf_op jit(solution)/shard_map/ppermute | solution.py:344
  34.1 0.0 collective-permute-done.11.b_ref
  34.2 0.6 %collective-permute-start.12 = (bf16[8,6144]{1,0:T(8,128)(2,1)S(1)}, bf16[8,6144]{1,0:T(8,128)(2,1)S(1)}, u32[]{:S(2)}, u32[]{:S(2)}) collective-permute-start(bf16[8,6144]{1,0:T(8,128)(2,1)S(1)} %shard_map.135), channel_id=1, source_target_pairs={{0,16},{1,17},{2,18},{3,19},{16,0},{17,1},{18,2},{19,3},{4,20},{5,... | collective-permute-start | bytes 294920 | tf_op jit(solution)/shard_map/ppermute | solution.py:344
  34.7 0.0 collective-permute-done.13.b_ref
  34.8 0.7 %collective-permute-start.14 = (bf16[8,6144]{1,0:T(8,128)(2,1)S(1)}, bf16[8,6144]{1,0:T(8,128)(2,1)S(1)}, u32[]{:S(2)}, u32[]{:S(2)}) collective-permute-start(bf16[8,6144]{1,0:T(8,128)(2,1)S(1)} %shard_map.136), channel_id=1, source_target_pairs={{0,2},{1,3},{2,0},{3,1},{16,18},{17,19},{18,16},{19,17},{4,6},{5,7... | collective-permute-start | bytes 294920 | tf_op jit(solution)/shard_map/ppermute | solution.py:344
  35.4 0.0 collective-permute-done.15.refs_4_
  35.5 2.2 %collective-permute-done.10.refs_0_ = bf16[8,6144]{1,0:T(8,128)(2,1)S(1)} collective-permute-done((bf16[8,6144]{1,0:T(8,128)(2,1)S(1)}, bf16[8,6144]{1,0:T(8,128)(2,1)S(1)}, u32[]{:S(2)}, u32[]{:S(2)}) %collective-permute-start.10) | collective-permute-done | bytes 98336 | tf_op jit(solution)/shard_map/ppermute | solution.py:344
  37.6 2.0 %collective-permute-done.12.refs_1_ = bf16[8,6144]{1,0:T(8,128)(2,1)S(1)} collective-permute-done((bf16[8,6144]{1,0:T(8,128)(2,1)S(1)}, bf16[8,6144]{1,0:T(8,128)(2,1)S(1)}, u32[]{:S(2)}, u32[]{:S(2)}) %collective-permute-start.12) | collective-permute-done | bytes 98336 | tf_op jit(solution)/shard_map/ppermute | solution.py:344
  39.6 0.0 collective-permute-done.14.refs_2_
  39.6 0.1 shard_map.137
  39.7 1.7 %collective-permute-start.16 = (bf16[2,6144]{1,0:T(2,128)(2,1)S(1)}, bf16[2,6144]{1,0:T(2,128)(2,1)S(1)}, u32[]{:S(2)}, u32[]{:S(2)}) collective-permute-start(bf16[2,6144]{1,0:T(2,128)(2,1)S(1)} %get-tuple-element.43), channel_id=1, source_target_pairs={{0,12},{4,8},{8,4},{12,0},{1,13},{5,9},{9,5},{13,1},{2,14},{6,10},... | collective-permute-start | bytes 73736 | tf_op jit(solution)/shard_map/ppermute | solution.py:341
  41.4 0.5 %collective-permute-start.17 = (bf16[2,6144]{1,0:T(2,128)(2,1)S(1)}, bf16[2,6144]{1,0:T(2,128)(2,1)S(1)}, u32[]{:S(2)}, u32[]{:S(2)}) collective-permute-start(bf16[2,6144]{1,0:T(2,128)(2,1)S(1)} %get-tuple-element.44), channel_id=1, source_target_pairs={{0,8},{4,12},{8,0},{12,4},{1,9},{5,13},{9,1},{13,5},{2,10},{6,14},... | collective-permute-start | bytes 73736 | tf_op jit(solution)/shard_map/ppermute | solution.py:341
  41.9 2.3 %collective-permute-start.18 = (bf16[2,6144]{1,0:T(2,128)(2,1)S(1)}, bf16[2,6144]{1,0:T(2,128)(2,1)S(1)}, u32[]{:S(2)}, u32[]{:S(2)}) collective-permute-start(bf16[2,6144]{1,0:T(2,128)(2,1)S(1)} %get-tuple-element.45), channel_id=1, source_target_pairs={{0,4},{4,0},{8,12},{12,8},{1,5},{5,1},{9,13},{13,9},{2,6},{6,2},{1... | collective-permute-start | bytes 73736 | tf_op jit(solution)/shard_map/ppermute | solution.py:341
  44.2 0.0 copy-done
  44.2 0.0 copy-done.1
  44.2 0.8 %shard_map.138.refs_5_ = f32[4,8]{1,0:T(4,128)S(1)} custom-call(s32[2,4]{1,0:T(2,128)S(1)} %bitcast.6, bf16[4,6144]{1,0:T(4,128)(2,1)S(1)} %get-tuple-element.34._.normed_ref, bf16[4,6144]{1,0:T(4,128)(2,1)S(1)} %bitcast.4), custom_call_target="tpu_custom_call" | custom-call | tf_op jit(solution)/shard_map/pallas_call | solution.py:298
  45.0 0.4 collective-permute-done.16.refs_0_
  45.4 0.8 %collective-permute-done.17.refs_1_ = bf16[2,6144]{1,0:T(2,128)(2,1)S(1)} collective-permute-done((bf16[2,6144]{1,0:T(2,128)(2,1)S(1)}, bf16[2,6144]{1,0:T(2,128)(2,1)S(1)}, u32[]{:S(2)}, u32[]{:S(2)}) %collective-permute-start.17) | collective-permute-done | bytes 24608 | tf_op jit(solution)/shard_map/ppermute | solution.py:341
  46.2 0.0 collective-permute-done.18.refs_2_
  46.2 0.9 %shard_map.139 = bf16[4,6144]{1,0:T(4,128)(2,1)} custom-call(bf16[2,6144]{1,0:T(2,128)(2,1)S(1)} %collective-permute-done.16.refs_0_, bf16[2,6144]{1,0:T(2,128)(2,1)S(1)} %collective-permute-done.17.refs_1_, bf16[2,6144]{1,0:T(2,128)(2,1)S(1)} %collective-permute-done.18.refs_2_, bf16[2,6144]{1,0:T(2,128)(2,1)S(1)} %get-tuple-element.46.refs_3_, ...), custom_call_target="tpu_custom_call" | custom-call | tf_op jit(solution)/shard_map/pallas_call | solution.py:298
  (5 shorter events, 0.1 us)
Async XLA Ops:
  3.4 7.7 %collective-permute-start = (bf16[2,6144]{1,0:T(2,128)(2,1)S(1)}, bf16[2,6144]{1,0:T(2,128)(2,1)S(1)}, u32[]{:S(2)}, u32[]{:S(2)}) collective-permute-start(bf16[2,6144]{1,0:T(2,128)(2,1)S(1)} %get-tuple-element.30), channel_id=1, source_target_pairs={{0,12},{4,8},{8,4},{12,0},{1,13},{5,9},{9,5},{13,1},{2,14},{6,10},... | collective-permute-start | bytes 73736 | tf_op jit(solution)/shard_map/ppermute | solution.py:341
  8.5 4.7 %collective-permute-start.1 = (bf16[2,6144]{1,0:T(2,128)(2,1)S(1)}, bf16[2,6144]{1,0:T(2,128)(2,1)S(1)}, u32[]{:S(2)}, u32[]{:S(2)}) collective-permute-start(bf16[2,6144]{1,0:T(2,128)(2,1)S(1)} %get-tuple-element.31), channel_id=1, source_target_pairs={{0,8},{4,12},{8,0},{12,4},{1,9},{5,13},{9,1},{13,5},{2,10},{6,14},... | collective-permute-start | bytes 73736 | tf_op jit(solution)/shard_map/ppermute | solution.py:341
  8.5 4.7 %collective-permute-start.2 = (bf16[2,6144]{1,0:T(2,128)(2,1)S(1)}, bf16[2,6144]{1,0:T(2,128)(2,1)S(1)}, u32[]{:S(2)}, u32[]{:S(2)}) collective-permute-start(bf16[2,6144]{1,0:T(2,128)(2,1)S(1)} %get-tuple-element.32), channel_id=1, source_target_pairs={{0,4},{4,0},{8,12},{12,8},{1,5},{5,1},{9,13},{13,9},{2,6},{6,2},{1... | collective-permute-start | bytes 73736 | tf_op jit(solution)/shard_map/ppermute | solution.py:341
  13.2 10.1 %slice-start = ((s8[12582912]{0:T(1024)(128)(4,1)}), s8[4194304]{0:T(1024)(128)(4,1)S(1)}, s32[]{:S(2)}) async-start(s8[12582912]{0:T(1024)(128)(4,1)} %bitcast.2), calls=%async_computation | async-start | bytes 8388608
  13.3 10.0 %slice-start.1 = ((s8[12582912]{0:T(1024)(128)(4,1)}), s8[4194304]{0:T(1024)(128)(4,1)S(1)}, s32[]{:S(2)}) async-start(s8[12582912]{0:T(1024)(128)(4,1)} %bitcast.2), calls=%async_computation.1 | async-start | bytes 8388608
  13.3 10.0 %slice-start.2 = ((s8[12582912]{0:T(1024)(128)(4,1)}), s8[4194304]{0:T(1024)(128)(4,1)S(1)}, s32[]{:S(2)}) async-start(s8[12582912]{0:T(1024)(128)(4,1)} %bitcast.2), calls=%async_computation.2 | async-start | bytes 8388608
  13.3 7.3 %collective-permute-start.6 = (bf16[8,6144]{1,0:T(8,128)(2,1)S(1)}, bf16[8,6144]{1,0:T(8,128)(2,1)S(1)}, u32[]{:S(2)}, u32[]{:S(2)}) collective-permute-start(bf16[8,6144]{1,0:T(8,128)(2,1)S(1)} %shard_map.130._.own_ref), channel_id=1, source_target_pairs={{0,1},{1,0},{2,3},{3,2},{16,17},{17,16},{18,19},{19,18},{4,5},{5,4... | collective-permute-start | bytes 294920 | tf_op jit(solution)/shard_map/ppermute | solution.py:344
  13.4 7.3 %collective-permute-start.5 = (bf16[8,6144]{1,0:T(8,128)(2,1)S(1)}, bf16[8,6144]{1,0:T(8,128)(2,1)S(1)}, u32[]{:S(2)}, u32[]{:S(2)}) collective-permute-start(bf16[8,6144]{1,0:T(8,128)(2,1)S(1)} %shard_map.130._.own_ref), channel_id=1, source_target_pairs={{0,16},{1,17},{2,18},{3,19},{16,0},{17,1},{18,2},{19,3},{4,20},{5,... | collective-permute-start | bytes 294920 | tf_op jit(solution)/shard_map/ppermute | solution.py:344
  15.0 5.7 %collective-permute-start.4 = (bf16[8,6144]{1,0:T(8,128)(2,1)S(1)}, bf16[8,6144]{1,0:T(8,128)(2,1)S(1)}, u32[]{:S(2)}, u32[]{:S(2)}) collective-permute-start(bf16[8,6144]{1,0:T(8,128)(2,1)S(1)} %shard_map.130._.own_ref), channel_id=1, source_target_pairs={{0,2},{1,3},{2,0},{3,1},{16,18},{17,19},{18,16},{19,17},{4,6},{5,7... | collective-permute-start | bytes 294920 | tf_op jit(solution)/shard_map/ppermute | solution.py:344
  16.5 5.5 %collective-permute-start.3 = (bf16[8,6144]{1,0:T(8,128)(2,1)S(1)}, bf16[8,6144]{1,0:T(8,128)(2,1)S(1)}, u32[]{:S(2)}, u32[]{:S(2)}) collective-permute-start(bf16[8,6144]{1,0:T(8,128)(2,1)S(1)} %shard_map.130._.own_ref), channel_id=1, source_target_pairs={{0,18},{1,19},{2,16},{3,17},{16,2},{17,3},{18,0},{19,1},{4,22},{5,... | collective-permute-start | bytes 294920 | tf_op jit(solution)/shard_map/ppermute | solution.py:344
  20.7 23.5 %copy-start = (bf16[6144,4]{0,1:T(4,128)(2,1)S(1)}, bf16[6144,4]{0,1:T(4,128)(2,1)}, u32[]{:S(2)}) copy-start(bf16[6144,4]{0,1:T(4,128)(2,1)} %param.21) | copy-start | bytes 147460
  20.7 23.5 %copy-start.1 = (s32[4,2]{0,1:T(2,128)S(1)}, s32[4,2]{0,1:T(2,128)}, u32[]{:S(2)}) copy-start(s32[4,2]{0,1:T(2,128)} %param.22) | copy-start | bytes 100
  20.7 2.6 %collective-permute-start.8 = (bf16[16,6144]{1,0:T(8,128)(2,1)S(1)}, bf16[16,6144]{1,0:T(8,128)(2,1)S(1)}, u32[]{:S(2)}, u32[]{:S(2)}) collective-permute-start(bf16[16,6144]{1,0:T(8,128)(2,1)S(1)} %shard_map.132.sides_ref), channel_id=1, source_target_pairs={{0,1},{1,0},{2,3},{3,2},{16,17},{17,16},{18,19},{19,18},{4,5},{5,4... | collective-permute-start | bytes 589832 | tf_op jit(solution)/shard_map/ppermute | solution.py:344
  22.0 1.3 %collective-permute-start.7 = (bf16[8,6144]{1,0:T(8,128)(2,1)S(1)}, bf16[8,6144]{1,0:T(8,128)(2,1)S(1)}, u32[]{:S(2)}, u32[]{:S(2)}) collective-permute-start(bf16[8,6144]{1,0:T(8,128)(2,1)S(1)} %collective-permute-done.3.corner_ref), channel_id=1, source_target_pairs={{0,1},{1,0},{2,3},{3,2},{16,17},{17,16},{18,19},{19,18},{4,5},{5,4... | collective-permute-start | bytes 294920 | tf_op jit(solution)/shard_map/ppermute | solution.py:344
  30.3 1.4 %collective-permute-start.9 = (bf16[8,6144]{1,0:T(8,128)(2,1)S(1)}, bf16[8,6144]{1,0:T(8,128)(2,1)S(1)}, u32[]{:S(2)}, u32[]{:S(2)}) collective-permute-start(bf16[8,6144]{1,0:T(8,128)(2,1)S(1)} %get-tuple-element.36), channel_id=1, source_target_pairs={{0,1},{1,0},{2,3},{3,2},{16,17},{17,16},{18,19},{19,18},{4,5},{5,4... | collective-permute-start | bytes 294920 | tf_op jit(solution)/shard_map/ppermute | solution.py:344
  30.5 3.6 %collective-permute-start.11 = (bf16[8,6144]{1,0:T(8,128)(2,1)S(1)}, bf16[8,6144]{1,0:T(8,128)(2,1)S(1)}, u32[]{:S(2)}, u32[]{:S(2)}) collective-permute-start(bf16[8,6144]{1,0:T(8,128)(2,1)S(1)} %get-tuple-element.38), channel_id=1, source_target_pairs={{0,1},{1,0},{2,3},{3,2},{16,17},{17,16},{18,19},{19,18},{4,5},{5,4... | collective-permute-start | bytes 294920 | tf_op jit(solution)/shard_map/ppermute | solution.py:344
  30.9 3.9 %collective-permute-start.13 = (bf16[8,6144]{1,0:T(8,128)(2,1)S(1)}, bf16[8,6144]{1,0:T(8,128)(2,1)S(1)}, u32[]{:S(2)}, u32[]{:S(2)}) collective-permute-start(bf16[8,6144]{1,0:T(8,128)(2,1)S(1)} %get-tuple-element.40), channel_id=1, source_target_pairs={{0,1},{1,0},{2,3},{3,2},{16,17},{17,16},{18,19},{19,18},{4,5},{5,4... | collective-permute-start | bytes 294920 | tf_op jit(solution)/shard_map/ppermute | solution.py:344
  31.0 4.4 %collective-permute-start.15 = (bf16[8,6144]{1,0:T(8,128)(2,1)S(1)}, bf16[8,6144]{1,0:T(8,128)(2,1)S(1)}, u32[]{:S(2)}, u32[]{:S(2)}) collective-permute-start(bf16[8,6144]{1,0:T(8,128)(2,1)S(1)} %get-tuple-element.42), channel_id=1, source_target_pairs={{0,1},{1,0},{2,3},{3,2},{16,17},{17,16},{18,19},{19,18},{4,5},{5,4... | collective-permute-start | bytes 294920 | tf_op jit(solution)/shard_map/ppermute | solution.py:344
  31.7 5.9 %collective-permute-start.10 = (bf16[8,6144]{1,0:T(8,128)(2,1)S(1)}, bf16[8,6144]{1,0:T(8,128)(2,1)S(1)}, u32[]{:S(2)}, u32[]{:S(2)}) collective-permute-start(bf16[8,6144]{1,0:T(8,128)(2,1)S(1)} %shard_map.134), channel_id=1, source_target_pairs={{0,18},{1,19},{2,16},{3,17},{16,2},{17,3},{18,0},{19,1},{4,22},{5,... | collective-permute-start | bytes 294920 | tf_op jit(solution)/shard_map/ppermute | solution.py:344
  34.2 5.5 %collective-permute-start.12 = (bf16[8,6144]{1,0:T(8,128)(2,1)S(1)}, bf16[8,6144]{1,0:T(8,128)(2,1)S(1)}, u32[]{:S(2)}, u32[]{:S(2)}) collective-permute-start(bf16[8,6144]{1,0:T(8,128)(2,1)S(1)} %shard_map.135), channel_id=1, source_target_pairs={{0,16},{1,17},{2,18},{3,19},{16,0},{17,1},{18,2},{19,3},{4,20},{5,... | collective-permute-start | bytes 294920 | tf_op jit(solution)/shard_map/ppermute | solution.py:344
  34.8 4.9 %collective-permute-start.14 = (bf16[8,6144]{1,0:T(8,128)(2,1)S(1)}, bf16[8,6144]{1,0:T(8,128)(2,1)S(1)}, u32[]{:S(2)}, u32[]{:S(2)}) collective-permute-start(bf16[8,6144]{1,0:T(8,128)(2,1)S(1)} %shard_map.136), channel_id=1, source_target_pairs={{0,2},{1,3},{2,0},{3,1},{16,18},{17,19},{18,16},{19,17},{4,6},{5,7... | collective-permute-start | bytes 294920 | tf_op jit(solution)/shard_map/ppermute | solution.py:344
  39.7 5.7 %collective-permute-start.16 = (bf16[2,6144]{1,0:T(2,128)(2,1)S(1)}, bf16[2,6144]{1,0:T(2,128)(2,1)S(1)}, u32[]{:S(2)}, u32[]{:S(2)}) collective-permute-start(bf16[2,6144]{1,0:T(2,128)(2,1)S(1)} %get-tuple-element.43), channel_id=1, source_target_pairs={{0,12},{4,8},{8,4},{12,0},{1,13},{5,9},{9,5},{13,1},{2,14},{6,10},... | collective-permute-start | bytes 73736 | tf_op jit(solution)/shard_map/ppermute | solution.py:341
  41.4 4.8 %collective-permute-start.17 = (bf16[2,6144]{1,0:T(2,128)(2,1)S(1)}, bf16[2,6144]{1,0:T(2,128)(2,1)S(1)}, u32[]{:S(2)}, u32[]{:S(2)}) collective-permute-start(bf16[2,6144]{1,0:T(2,128)(2,1)S(1)} %get-tuple-element.44), channel_id=1, source_target_pairs={{0,8},{4,12},{8,0},{12,4},{1,9},{5,13},{9,1},{13,5},{2,10},{6,14},... | collective-permute-start | bytes 73736 | tf_op jit(solution)/shard_map/ppermute | solution.py:341
  41.9 4.4 %collective-permute-start.18 = (bf16[2,6144]{1,0:T(2,128)(2,1)S(1)}, bf16[2,6144]{1,0:T(2,128)(2,1)S(1)}, u32[]{:S(2)}, u32[]{:S(2)}) collective-permute-start(bf16[2,6144]{1,0:T(2,128)(2,1)S(1)} %get-tuple-element.45), channel_id=1, source_target_pairs={{0,4},{4,0},{8,12},{12,8},{1,5},{5,1},{9,13},{13,9},{2,6},{6,2},{1... | collective-permute-start | bytes 73736 | tf_op jit(solution)/shard_map/ppermute | solution.py:341

commit v6 on v5

--- a/solution.py
+++ b/solution.py
@@ -230,11 +230,14 @@
 ):
     *out_refs, x_ref, gate_sum, up_sum, down_ref, sems = refs
     chunks = sems.shape[0]
-    part = down_ref.shape[0] // chunks
+    part = down_ref.shape[1] // chunks
+
+    def columns(i, low, count):
+        return pl.ds(pl.multiple_of(i * part + low, 128), count)
 
     def load(i):
-        at = pl.ds(i * part, part)
-        return pltpu.make_async_copy(down_any.at[0, at], down_ref.at[at], sems.at[i])
+        at = columns(i, 0, part)
+        return pltpu.make_async_copy(down_any.at[0, :, at], down_ref.at[:, at], sems.at[i])
 
     pl.loop(0, chunks)(lambda i: load(i).start())
     width = x_ref.shape[1]
@@ -257,13 +260,16 @@
             first += tall
     gate = gate_sum[...]
     hidden = (gate / (1.0 + jnp.exp(-gate)) * up_sum[...]).astype(jnp.bfloat16)
-    pl.loop(0, chunks)(lambda i: load(i).wait())
     deep = 1024
-    for step in range(width // deep):
-        at = pl.ds(step * deep, deep)
-        piece = jnp.dot(hidden, down_ref[:, at], preferred_element_type=jnp.float32)
-        for i, ref in enumerate(out_refs):
-            ref[:, at] = piece[i * slots : (i + 1) * slots].astype(jnp.bfloat16)
+
+    @pl.loop(0, chunks)
+    def _(i):
+        load(i).wait()
+        for low in range(0, part, deep):
+            at = columns(i, low, deep)
+            piece = jnp.dot(hidden, down_ref[:, at], preferred_element_type=jnp.float32)
+            for j, ref in enumerate(out_refs):
+                ref[:, at] = piece[j * slots : (j + 1) * slots].astype(jnp.bfloat16)
 
 
 def add_kernel(a_ref, b_ref, out_ref):
@@ -449,7 +455,7 @@
             pltpu.VMEM((2 * half, hidden), jnp.float32),
             pltpu.VMEM((2 * half, hidden), jnp.float32),
             pltpu.VMEM((hidden, width), jnp.bfloat16),
-            pltpu.SemaphoreType.DMA((4,)),
+            pltpu.SemaphoreType.DMA((2,)),
         ],
         limit=28,
     )

time: 47.3 us -> 47.2 us (level)
  no operation moved by 1% of the time
where the time goes in v6:
time: 47.2 us; the launch traced here: 47.1 us
  starting transfers between devices  18.7 us (40%)
  Pallas kernels  17.8 us (38%)
  waiting for transfers between devices  10.4 us (22%)
    pallas_call x13, Pallas kernels, call(): pl.pallas_call(kernel, out_shape=outs, in_specs=in_specs, out_specs=jax.t...  17.8 us
    ppermute x6, starting transfers between devices, to_grp(): return lax.ppermute(x, 'grp', [(i, i ^ j) for i in range(experts)])  10.2 us
    ppermute x13, starting transfers between devices, to_plane(): return lax.ppermute(x, plane, [(i, i ^ k) for i in range(n_side * n_cuts)])  8.47 us
    ppermute x13, waiting for transfers between devices, to_plane(): return lax.ppermute(x, plane, [(i, i ^ k) for i in range(n_side * n_cuts)])  6.95 us
    ppermute x6, waiting for transfers between devices, to_grp(): return lax.ppermute(x, 'grp', [(i, i ^ j) for i in range(experts)])  3.41 us
  transfers between devices with their start and end apart: 19, of which 8 were waited for; matrix products, arithmetic and copies ran while one was open for 0% of the time, Pallas kernels for 14%

profile of v6, /device:TPU:0, one launch (start us, length us, event | category | flops | bytes accessed | tf_op | source)
XLA Modules:
  0.0 47.1 jit_solution(4067084333315601187)
XLA Ops:
  0.0 3.1 %shard_map.127 = (f32[4,6144]{1,0:T(4,128)S(1)}, f32[4,128]{1,0:T(4,128)S(1)}, f32[8,4]{1,0:T(8,128)S(1)}, bf16[6144]{0:T(1024)(128)(2,1)S(1)}) custom-call(s32[4]{0:T(128)} %refs_0_.1, s32[2,4]{1,0:T(2,128)} %bitcast.5, bf16[4,6144]{1,0:T(4,128)(2,1)} %refs_2_.1, bf16[4,1024]{1,0:T(4,128)(2,1)} %refs_3_.1, bf16[4,1024]{1,0:T(4,128)(2,1)} %refs_4_.1, ...), custom_call_target="tpu_custom_call" | custom-call | tf_op jit(solution)/shard_map/pallas_call | solution.py:304
  3.1 0.2 shard_map.128
  3.4 5.1 %collective-permute-start = (bf16[2,6144]{1,0:T(2,128)(2,1)S(1)}, bf16[2,6144]{1,0:T(2,128)(2,1)S(1)}, u32[]{:S(2)}, u32[]{:S(2)}) collective-permute-start(bf16[2,6144]{1,0:T(2,128)(2,1)S(1)} %get-tuple-element.30), channel_id=1, source_target_pairs={{0,12},{4,8},{8,4},{12,0},{1,13},{5,9},{9,5},{13,1},{2,14},{6,10},... | collective-permute-start | bytes 73736 | tf_op jit(solution)/shard_map/ppermute | solution.py:347
  8.5 0.0 collective-permute-start.1
  8.5 0.6 %collective-permute-start.2 = (bf16[2,6144]{1,0:T(2,128)(2,1)S(1)}, bf16[2,6144]{1,0:T(2,128)(2,1)S(1)}, u32[]{:S(2)}, u32[]{:S(2)}) collective-permute-start(bf16[2,6144]{1,0:T(2,128)(2,1)S(1)} %get-tuple-element.32), channel_id=1, source_target_pairs={{0,4},{4,0},{8,12},{12,8},{1,5},{5,1},{9,13},{13,9},{2,6},{6,2},{1... | collective-permute-start | bytes 73736 | tf_op jit(solution)/shard_map/ppermute | solution.py:347
  9.1 1.9 %shard_map.129.refs_4_.up_low_ref = bf16[1536,1024]{1,0:T(8,128)(2,1)S(1)} custom-call(bf16[1,6144,1024]{2,1,0:T(8,128)(2,1)} %w_any.3, bf16[4,6144]{1,0:T(4,128)(2,1)S(1)} %get-tuple-element.34._.normed_ref), custom_call_target="tpu_custom_call" | custom-call | tf_op jit(solution)/shard_map/pallas_call | solution.py:304
  11.0 0.0 collective-permute-done.refs_0_
  11.1 2.2 %collective-permute-done.1.refs_1_ = bf16[2,6144]{1,0:T(2,128)(2,1)S(1)} collective-permute-done((bf16[2,6144]{1,0:T(2,128)(2,1)S(1)}, bf16[2,6144]{1,0:T(2,128)(2,1)S(1)}, u32[]{:S(2)}, u32[]{:S(2)}) %collective-permute-start.1) | collective-permute-done | bytes 24608 | tf_op jit(solution)/shard_map/ppermute | solution.py:347
  13.2 0.0 collective-permute-done.2.refs_2_
  13.2 0.0 slice-start
  13.2 0.1 shard_map.130._.own_ref
  13.3 0.0 slice-start.1
  13.3 0.0 slice-start.2
  13.3 0.1 collective-permute-start.6
  13.4 1.6 %collective-permute-start.5 = (bf16[8,6144]{1,0:T(8,128)(2,1)S(1)}, bf16[8,6144]{1,0:T(8,128)(2,1)S(1)}, u32[]{:S(2)}, u32[]{:S(2)}) collective-permute-start(bf16[8,6144]{1,0:T(8,128)(2,1)S(1)} %shard_map.130._.own_ref), channel_id=1, source_target_pairs={{0,16},{1,17},{2,18},{3,19},{16,0},{17,1},{18,2},{19,3},{4,20},{5,... | collective-permute-start | bytes 294920 | tf_op jit(solution)/shard_map/ppermute | solution.py:350
  15.0 1.5 %collective-permute-start.4 = (bf16[8,6144]{1,0:T(8,128)(2,1)S(1)}, bf16[8,6144]{1,0:T(8,128)(2,1)S(1)}, u32[]{:S(2)}, u32[]{:S(2)}) collective-permute-start(bf16[8,6144]{1,0:T(8,128)(2,1)S(1)} %shard_map.130._.own_ref), channel_id=1, source_target_pairs={{0,2},{1,3},{2,0},{3,1},{16,18},{17,19},{18,16},{19,17},{4,6},{5,7... | collective-permute-start | bytes 294920 | tf_op jit(solution)/shard_map/ppermute | solution.py:350
  16.5 0.5 %collective-permute-start.3 = (bf16[8,6144]{1,0:T(8,128)(2,1)S(1)}, bf16[8,6144]{1,0:T(8,128)(2,1)S(1)}, u32[]{:S(2)}, u32[]{:S(2)}) collective-permute-start(bf16[8,6144]{1,0:T(8,128)(2,1)S(1)} %shard_map.130._.own_ref), channel_id=1, source_target_pairs={{0,18},{1,19},{2,16},{3,17},{16,2},{17,3},{18,0},{19,1},{4,22},{5,... | collective-permute-start | bytes 294920 | tf_op jit(solution)/shard_map/ppermute | solution.py:350
  17.0 3.7 %shard_map.131.refs_2_.up_high_ref = bf16[4608,1024]{1,0:T(8,128)(2,1)S(1)} custom-call(bf16[1,6144,1024]{2,1,0:T(8,128)(2,1)} %w_any.3, bf16[8,6144]{1,0:T(8,128)(2,1)S(1)} %shard_map.130._.own_ref), custom_call_target="tpu_custom_call" | custom-call | tf_op jit(solution)/shard_map/pallas_call | solution.py:304
  20.6 0.0 collective-permute-done.6.refs_3_.core_own_ref
  20.7 0.0 collective-permute-done.5.refs_1_
  20.7 0.0 collective-permute-done.4.refs_0_
  20.7 0.0 copy-start
  20.7 0.0 copy-start.1
  20.7 0.1 collective-permute-start.8
  20.8 1.2 %collective-permute-done.3.corner_ref = bf16[8,6144]{1,0:T(8,128)(2,1)S(1)} collective-permute-done((bf16[8,6144]{1,0:T(8,128)(2,1)S(1)}, bf16[8,6144]{1,0:T(8,128)(2,1)S(1)}, u32[]{:S(2)}, u32[]{:S(2)}) %collective-permute-start.3) | collective-permute-done | bytes 98336 | tf_op jit(solution)/shard_map/ppermute | solution.py:350
  22.0 0.0 collective-permute-start.7
  22.0 1.3 %collective-permute-done.7.core_corner_ref = bf16[8,6144]{1,0:T(8,128)(2,1)S(1)} collective-permute-done((bf16[8,6144]{1,0:T(8,128)(2,1)S(1)}, bf16[8,6144]{1,0:T(8,128)(2,1)S(1)}, u32[]{:S(2)}, u32[]{:S(2)}) %collective-permute-start.7) | collective-permute-done | bytes 98336 | tf_op jit(solution)/shard_map/ppermute | solution.py:350
  23.3 0.0 collective-permute-done.8.core_sides_ref
  23.3 0.0 slice-done
  23.3 0.0 slice-done.1
  23.3 0.0 slice-done.2
  23.3 6.9 %shard_map.133 = (bf16[8,6144]{1,0:T(8,128)(2,1)S(1)}, bf16[8,6144]{1,0:T(8,128)(2,1)S(1)}, bf16[8,6144]{1,0:T(8,128)(2,1)S(1)}, bf16[8,6144]{1,0:T(8,128)(2,1)S...) custom-call(bf16[8,6144]{1,0:T(8,128)(2,1)S(1)} %shard_map.130._.own, ...), custom_call_target="tpu_custom_call" | custom-call | tf_op jit(solution)/shard_map/pallas_call | solution.py:304
  30.2 0.2 collective-permute-start.9
  30.5 0.4 collective-permute-start.11
  30.8 0.1 collective-permute-start.13
  31.0 0.4 collective-permute-start.15
  31.3 0.3 collective-permute-done.9.b_ref
  31.6 2.4 %collective-permute-start.10 = (bf16[8,6144]{1,0:T(8,128)(2,1)S(1)}, bf16[8,6144]{1,0:T(8,128)(2,1)S(1)}, u32[]{:S(2)}, u32[]{:S(2)}) collective-permute-start(bf16[8,6144]{1,0:T(8,128)(2,1)S(1)} %shard_map.134), channel_id=1, source_target_pairs={{0,18},{1,19},{2,16},{3,17},{16,2},{17,3},{18,0},{19,1},{4,22},{5,... | collective-permute-start | bytes 294920 | tf_op jit(solution)/shard_map/ppermute | solution.py:350
  34.1 0.0 collective-permute-done.11.b_ref
  34.1 0.6 %collective-permute-start.12 = (bf16[8,6144]{1,0:T(8,128)(2,1)S(1)}, bf16[8,6144]{1,0:T(8,128)(2,1)S(1)}, u32[]{:S(2)}, u32[]{:S(2)}) collective-permute-start(bf16[8,6144]{1,0:T(8,128)(2,1)S(1)} %shard_map.135), channel_id=1, source_target_pairs={{0,16},{1,17},{2,18},{3,19},{16,0},{17,1},{18,2},{19,3},{4,20},{5,... | collective-permute-start | bytes 294920 | tf_op jit(solution)/shard_map/ppermute | solution.py:350
  34.7 0.0 collective-permute-done.13.b_ref
  34.7 0.7 %collective-permute-start.14 = (bf16[8,6144]{1,0:T(8,128)(2,1)S(1)}, bf16[8,6144]{1,0:T(8,128)(2,1)S(1)}, u32[]{:S(2)}, u32[]{:S(2)}) collective-permute-start(bf16[8,6144]{1,0:T(8,128)(2,1)S(1)} %shard_map.136), channel_id=1, source_target_pairs={{0,2},{1,3},{2,0},{3,1},{16,18},{17,19},{18,16},{19,17},{4,6},{5,7... | collective-permute-start | bytes 294920 | tf_op jit(solution)/shard_map/ppermute | solution.py:350
  35.4 0.0 collective-permute-done.15.refs_4_
  35.4 2.2 %collective-permute-done.10.refs_0_ = bf16[8,6144]{1,0:T(8,128)(2,1)S(1)} collective-permute-done((bf16[8,6144]{1,0:T(8,128)(2,1)S(1)}, bf16[8,6144]{1,0:T(8,128)(2,1)S(1)}, u32[]{:S(2)}, u32[]{:S(2)}) %collective-permute-start.10) | collective-permute-done | bytes 98336 | tf_op jit(solution)/shard_map/ppermute | solution.py:350
  37.5 2.0 %collective-permute-done.12.refs_1_ = bf16[8,6144]{1,0:T(8,128)(2,1)S(1)} collective-permute-done((bf16[8,6144]{1,0:T(8,128)(2,1)S(1)}, bf16[8,6144]{1,0:T(8,128)(2,1)S(1)}, u32[]{:S(2)}, u32[]{:S(2)}) %collective-permute-start.12) | collective-permute-done | bytes 98336 | tf_op jit(solution)/shard_map/ppermute | solution.py:350
  39.6 0.0 collective-permute-done.14.refs_2_
  39.6 0.1 shard_map.137
  39.7 1.7 %collective-permute-start.16 = (bf16[2,6144]{1,0:T(2,128)(2,1)S(1)}, bf16[2,6144]{1,0:T(2,128)(2,1)S(1)}, u32[]{:S(2)}, u32[]{:S(2)}) collective-permute-start(bf16[2,6144]{1,0:T(2,128)(2,1)S(1)} %get-tuple-element.43), channel_id=1, source_target_pairs={{0,12},{4,8},{8,4},{12,0},{1,13},{5,9},{9,5},{13,1},{2,14},{6,10},... | collective-permute-start | bytes 73736 | tf_op jit(solution)/shard_map/ppermute | solution.py:347
  41.3 0.5 %collective-permute-start.17 = (bf16[2,6144]{1,0:T(2,128)(2,1)S(1)}, bf16[2,6144]{1,0:T(2,128)(2,1)S(1)}, u32[]{:S(2)}, u32[]{:S(2)}) collective-permute-start(bf16[2,6144]{1,0:T(2,128)(2,1)S(1)} %get-tuple-element.44), channel_id=1, source_target_pairs={{0,8},{4,12},{8,0},{12,4},{1,9},{5,13},{9,1},{13,5},{2,10},{6,14},... | collective-permute-start | bytes 73736 | tf_op jit(solution)/shard_map/ppermute | solution.py:347
  41.8 2.3 %collective-permute-start.18 = (bf16[2,6144]{1,0:T(2,128)(2,1)S(1)}, bf16[2,6144]{1,0:T(2,128)(2,1)S(1)}, u32[]{:S(2)}, u32[]{:S(2)}) collective-permute-start(bf16[2,6144]{1,0:T(2,128)(2,1)S(1)} %get-tuple-element.45), channel_id=1, source_target_pairs={{0,4},{4,0},{8,12},{12,8},{1,5},{5,1},{9,13},{13,9},{2,6},{6,2},{1... | collective-permute-start | bytes 73736 | tf_op jit(solution)/shard_map/ppermute | solution.py:347
  44.1 0.0 copy-done
  44.1 0.0 copy-done.1
  44.1 0.8 %shard_map.138.refs_5_ = f32[4,8]{1,0:T(4,128)S(1)} custom-call(s32[2,4]{1,0:T(2,128)S(1)} %bitcast.6, bf16[4,6144]{1,0:T(4,128)(2,1)S(1)} %get-tuple-element.34._.normed_ref, bf16[4,6144]{1,0:T(4,128)(2,1)S(1)} %bitcast.4), custom_call_target="tpu_custom_call" | custom-call | tf_op jit(solution)/shard_map/pallas_call | solution.py:304
  44.9 0.4 collective-permute-done.16.refs_0_
  45.3 0.8 %collective-permute-done.17.refs_1_ = bf16[2,6144]{1,0:T(2,128)(2,1)S(1)} collective-permute-done((bf16[2,6144]{1,0:T(2,128)(2,1)S(1)}, bf16[2,6144]{1,0:T(2,128)(2,1)S(1)}, u32[]{:S(2)}, u32[]{:S(2)}) %collective-permute-start.17) | collective-permute-done | bytes 24608 | tf_op jit(solution)/shard_map/ppermute | solution.py:347
  46.2 0.0 collective-permute-done.18.refs_2_
  46.2 0.9 %shard_map.139 = bf16[4,6144]{1,0:T(4,128)(2,1)} custom-call(bf16[2,6144]{1,0:T(2,128)(2,1)S(1)} %collective-permute-done.16.refs_0_, bf16[2,6144]{1,0:T(2,128)(2,1)S(1)} %collective-permute-done.17.refs_1_, bf16[2,6144]{1,0:T(2,128)(2,1)S(1)} %collective-permute-done.18.refs_2_, bf16[2,6144]{1,0:T(2,128)(2,1)S(1)} %get-tuple-element.46.refs_3_, ...), custom_call_target="tpu_custom_call" | custom-call | tf_op jit(solution)/shard_map/pallas_call | solution.py:304
  (5 shorter events, 0.1 us)
Async XLA Ops:
  3.4 7.7 %collective-permute-start = (bf16[2,6144]{1,0:T(2,128)(2,1)S(1)}, bf16[2,6144]{1,0:T(2,128)(2,1)S(1)}, u32[]{:S(2)}, u32[]{:S(2)}) collective-permute-start(bf16[2,6144]{1,0:T(2,128)(2,1)S(1)} %get-tuple-element.30), channel_id=1, source_target_pairs={{0,12},{4,8},{8,4},{12,0},{1,13},{5,9},{9,5},{13,1},{2,14},{6,10},... | collective-permute-start | bytes 73736 | tf_op jit(solution)/shard_map/ppermute | solution.py:347
  8.5 4.7 %collective-permute-start.1 = (bf16[2,6144]{1,0:T(2,128)(2,1)S(1)}, bf16[2,6144]{1,0:T(2,128)(2,1)S(1)}, u32[]{:S(2)}, u32[]{:S(2)}) collective-permute-start(bf16[2,6144]{1,0:T(2,128)(2,1)S(1)} %get-tuple-element.31), channel_id=1, source_target_pairs={{0,8},{4,12},{8,0},{12,4},{1,9},{5,13},{9,1},{13,5},{2,10},{6,14},... | collective-permute-start | bytes 73736 | tf_op jit(solution)/shard_map/ppermute | solution.py:347
  8.5 4.7 %collective-permute-start.2 = (bf16[2,6144]{1,0:T(2,128)(2,1)S(1)}, bf16[2,6144]{1,0:T(2,128)(2,1)S(1)}, u32[]{:S(2)}, u32[]{:S(2)}) collective-permute-start(bf16[2,6144]{1,0:T(2,128)(2,1)S(1)} %get-tuple-element.32), channel_id=1, source_target_pairs={{0,4},{4,0},{8,12},{12,8},{1,5},{5,1},{9,13},{13,9},{2,6},{6,2},{1... | collective-permute-start | bytes 73736 | tf_op jit(solution)/shard_map/ppermute | solution.py:347
  13.2 10.1 %slice-start = ((s8[12582912]{0:T(1024)(128)(4,1)}), s8[4194304]{0:T(1024)(128)(4,1)S(1)}, s32[]{:S(2)}) async-start(s8[12582912]{0:T(1024)(128)(4,1)} %bitcast.2), calls=%async_computation | async-start | bytes 8388608
  13.3 10.0 %slice-start.1 = ((s8[12582912]{0:T(1024)(128)(4,1)}), s8[4194304]{0:T(1024)(128)(4,1)S(1)}, s32[]{:S(2)}) async-start(s8[12582912]{0:T(1024)(128)(4,1)} %bitcast.2), calls=%async_computation.1 | async-start | bytes 8388608
  13.3 10.0 %slice-start.2 = ((s8[12582912]{0:T(1024)(128)(4,1)}), s8[4194304]{0:T(1024)(128)(4,1)S(1)}, s32[]{:S(2)}) async-start(s8[12582912]{0:T(1024)(128)(4,1)} %bitcast.2), calls=%async_computation.2 | async-start | bytes 8388608
  13.3 7.3 %collective-permute-start.6 = (bf16[8,6144]{1,0:T(8,128)(2,1)S(1)}, bf16[8,6144]{1,0:T(8,128)(2,1)S(1)}, u32[]{:S(2)}, u32[]{:S(2)}) collective-permute-start(bf16[8,6144]{1,0:T(8,128)(2,1)S(1)} %shard_map.130._.own_ref), channel_id=1, source_target_pairs={{0,1},{1,0},{2,3},{3,2},{16,17},{17,16},{18,19},{19,18},{4,5},{5,4... | collective-permute-start | bytes 294920 | tf_op jit(solution)/shard_map/ppermute | solution.py:350
  13.4 7.3 %collective-permute-start.5 = (bf16[8,6144]{1,0:T(8,128)(2,1)S(1)}, bf16[8,6144]{1,0:T(8,128)(2,1)S(1)}, u32[]{:S(2)}, u32[]{:S(2)}) collective-permute-start(bf16[8,6144]{1,0:T(8,128)(2,1)S(1)} %shard_map.130._.own_ref), channel_id=1, source_target_pairs={{0,16},{1,17},{2,18},{3,19},{16,0},{17,1},{18,2},{19,3},{4,20},{5,... | collective-permute-start | bytes 294920 | tf_op jit(solution)/shard_map/ppermute | solution.py:350
  15.0 5.7 %collective-permute-start.4 = (bf16[8,6144]{1,0:T(8,128)(2,1)S(1)}, bf16[8,6144]{1,0:T(8,128)(2,1)S(1)}, u32[]{:S(2)}, u32[]{:S(2)}) collective-permute-start(bf16[8,6144]{1,0:T(8,128)(2,1)S(1)} %shard_map.130._.own_ref), channel_id=1, source_target_pairs={{0,2},{1,3},{2,0},{3,1},{16,18},{17,19},{18,16},{19,17},{4,6},{5,7... | collective-permute-start | bytes 294920 | tf_op jit(solution)/shard_map/ppermute | solution.py:350
  16.5 5.5 %collective-permute-start.3 = (bf16[8,6144]{1,0:T(8,128)(2,1)S(1)}, bf16[8,6144]{1,0:T(8,128)(2,1)S(1)}, u32[]{:S(2)}, u32[]{:S(2)}) collective-permute-start(bf16[8,6144]{1,0:T(8,128)(2,1)S(1)} %shard_map.130._.own_ref), channel_id=1, source_target_pairs={{0,18},{1,19},{2,16},{3,17},{16,2},{17,3},{18,0},{19,1},{4,22},{5,... | collective-permute-start | bytes 294920 | tf_op jit(solution)/shard_map/ppermute | solution.py:350
  20.7 23.4 %copy-start = (bf16[6144,4]{0,1:T(4,128)(2,1)S(1)}, bf16[6144,4]{0,1:T(4,128)(2,1)}, u32[]{:S(2)}) copy-start(bf16[6144,4]{0,1:T(4,128)(2,1)} %param.21) | copy-start | bytes 147460
  20.7 23.4 %copy-start.1 = (s32[4,2]{0,1:T(2,128)S(1)}, s32[4,2]{0,1:T(2,128)}, u32[]{:S(2)}) copy-start(s32[4,2]{0,1:T(2,128)} %param.22) | copy-start | bytes 100
  20.7 2.6 %collective-permute-start.8 = (bf16[16,6144]{1,0:T(8,128)(2,1)S(1)}, bf16[16,6144]{1,0:T(8,128)(2,1)S(1)}, u32[]{:S(2)}, u32[]{:S(2)}) collective-permute-start(bf16[16,6144]{1,0:T(8,128)(2,1)S(1)} %shard_map.132.sides_ref), channel_id=1, source_target_pairs={{0,1},{1,0},{2,3},{3,2},{16,17},{17,16},{18,19},{19,18},{4,5},{5,4... | collective-permute-start | bytes 589832 | tf_op jit(solution)/shard_map/ppermute | solution.py:350
  22.0 1.3 %collective-permute-start.7 = (bf16[8,6144]{1,0:T(8,128)(2,1)S(1)}, bf16[8,6144]{1,0:T(8,128)(2,1)S(1)}, u32[]{:S(2)}, u32[]{:S(2)}) collective-permute-start(bf16[8,6144]{1,0:T(8,128)(2,1)S(1)} %collective-permute-done.3.corner_ref), channel_id=1, source_target_pairs={{0,1},{1,0},{2,3},{3,2},{16,17},{17,16},{18,19},{19,18},{4,5},{5,4... | collective-permute-start | bytes 294920 | tf_op jit(solution)/shard_map/ppermute | solution.py:350
  30.2 1.4 %collective-permute-start.9 = (bf16[8,6144]{1,0:T(8,128)(2,1)S(1)}, bf16[8,6144]{1,0:T(8,128)(2,1)S(1)}, u32[]{:S(2)}, u32[]{:S(2)}) collective-permute-start(bf16[8,6144]{1,0:T(8,128)(2,1)S(1)} %get-tuple-element.36), channel_id=1, source_target_pairs={{0,1},{1,0},{2,3},{3,2},{16,17},{17,16},{18,19},{19,18},{4,5},{5,4... | collective-permute-start | bytes 294920 | tf_op jit(solution)/shard_map/ppermute | solution.py:350
  30.5 3.6 %collective-permute-start.11 = (bf16[8,6144]{1,0:T(8,128)(2,1)S(1)}, bf16[8,6144]{1,0:T(8,128)(2,1)S(1)}, u32[]{:S(2)}, u32[]{:S(2)}) collective-permute-start(bf16[8,6144]{1,0:T(8,128)(2,1)S(1)} %get-tuple-element.38), channel_id=1, source_target_pairs={{0,1},{1,0},{2,3},{3,2},{16,17},{17,16},{18,19},{19,18},{4,5},{5,4... | collective-permute-start | bytes 294920 | tf_op jit(solution)/shard_map/ppermute | solution.py:350
  30.8 3.8 %collective-permute-start.13 = (bf16[8,6144]{1,0:T(8,128)(2,1)S(1)}, bf16[8,6144]{1,0:T(8,128)(2,1)S(1)}, u32[]{:S(2)}, u32[]{:S(2)}) collective-permute-start(bf16[8,6144]{1,0:T(8,128)(2,1)S(1)} %get-tuple-element.40), channel_id=1, source_target_pairs={{0,1},{1,0},{2,3},{3,2},{16,17},{17,16},{18,19},{19,18},{4,5},{5,4... | collective-permute-start | bytes 294920 | tf_op jit(solution)/shard_map/ppermute | solution.py:350
  31.0 4.4 %collective-permute-start.15 = (bf16[8,6144]{1,0:T(8,128)(2,1)S(1)}, bf16[8,6144]{1,0:T(8,128)(2,1)S(1)}, u32[]{:S(2)}, u32[]{:S(2)}) collective-permute-start(bf16[8,6144]{1,0:T(8,128)(2,1)S(1)} %get-tuple-element.42), channel_id=1, source_target_pairs={{0,1},{1,0},{2,3},{3,2},{16,17},{17,16},{18,19},{19,18},{4,5},{5,4... | collective-permute-start | bytes 294920 | tf_op jit(solution)/shard_map/ppermute | solution.py:350
  31.6 5.9 %collective-permute-start.10 = (bf16[8,6144]{1,0:T(8,128)(2,1)S(1)}, bf16[8,6144]{1,0:T(8,128)(2,1)S(1)}, u32[]{:S(2)}, u32[]{:S(2)}) collective-permute-start(bf16[8,6144]{1,0:T(8,128)(2,1)S(1)} %shard_map.134), channel_id=1, source_target_pairs={{0,18},{1,19},{2,16},{3,17},{16,2},{17,3},{18,0},{19,1},{4,22},{5,... | collective-permute-start | bytes 294920 | tf_op jit(solution)/shard_map/ppermute | solution.py:350
  34.1 5.5 %collective-permute-start.12 = (bf16[8,6144]{1,0:T(8,128)(2,1)S(1)}, bf16[8,6144]{1,0:T(8,128)(2,1)S(1)}, u32[]{:S(2)}, u32[]{:S(2)}) collective-permute-start(bf16[8,6144]{1,0:T(8,128)(2,1)S(1)} %shard_map.135), channel_id=1, source_target_pairs={{0,16},{1,17},{2,18},{3,19},{16,0},{17,1},{18,2},{19,3},{4,20},{5,... | collective-permute-start | bytes 294920 | tf_op jit(solution)/shard_map/ppermute | solution.py:350
  34.7 4.9 %collective-permute-start.14 = (bf16[8,6144]{1,0:T(8,128)(2,1)S(1)}, bf16[8,6144]{1,0:T(8,128)(2,1)S(1)}, u32[]{:S(2)}, u32[]{:S(2)}) collective-permute-start(bf16[8,6144]{1,0:T(8,128)(2,1)S(1)} %shard_map.136), channel_id=1, source_target_pairs={{0,2},{1,3},{2,0},{3,1},{16,18},{17,19},{18,16},{19,17},{4,6},{5,7... | collective-permute-start | bytes 294920 | tf_op jit(solution)/shard_map/ppermute | solution.py:350
  39.7 5.7 %collective-permute-start.16 = (bf16[2,6144]{1,0:T(2,128)(2,1)S(1)}, bf16[2,6144]{1,0:T(2,128)(2,1)S(1)}, u32[]{:S(2)}, u32[]{:S(2)}) collective-permute-start(bf16[2,6144]{1,0:T(2,128)(2,1)S(1)} %get-tuple-element.43), channel_id=1, source_target_pairs={{0,12},{4,8},{8,4},{12,0},{1,13},{5,9},{9,5},{13,1},{2,14},{6,10},... | collective-permute-start | bytes 73736 | tf_op jit(solution)/shard_map/ppermute | solution.py:347
  41.3 4.8 %collective-permute-start.17 = (bf16[2,6144]{1,0:T(2,128)(2,1)S(1)}, bf16[2,6144]{1,0:T(2,128)(2,1)S(1)}, u32[]{:S(2)}, u32[]{:S(2)}) collective-permute-start(bf16[2,6144]{1,0:T(2,128)(2,1)S(1)} %get-tuple-element.44), channel_id=1, source_target_pairs={{0,8},{4,12},{8,0},{12,4},{1,9},{5,13},{9,1},{13,5},{2,10},{6,14},... | collective-permute-start | bytes 73736 | tf_op jit(solution)/shard_map/ppermute | solution.py:347
  41.8 4.4 %collective-permute-start.18 = (bf16[2,6144]{1,0:T(2,128)(2,1)S(1)}, bf16[2,6144]{1,0:T(2,128)(2,1)S(1)}, u32[]{:S(2)}, u32[]{:S(2)}) collective-permute-start(bf16[2,6144]{1,0:T(2,128)(2,1)S(1)} %get-tuple-element.45), channel_id=1, source_target_pairs={{0,4},{4,0},{8,12},{12,8},{1,5},{5,1},{9,13},{13,9},{2,6},{6,2},{1... | collective-permute-start | bytes 73736 | tf_op jit(solution)/shard_map/ppermute | solution.py:347
